TPU v7x, 512 devices: a whole 4x8x8 slice. The times are simulated.
512 devices in a mesh: gx: 16 (over z, core), yz: 32 (over x, y).
Axes of the slice: x: 4, y: 8, z: 8, core: 2. Of those that a mesh axis runs over, the one named last changes fastest.
Arguments:
- vorticity: bfloat16 [3, 512, 256, 512], P(None, 'gx', 'yz'), may hold values from -6 to 6
- velocity: bfloat16 [3, 512, 256, 512], P(None, 'gx', 'yz'), may hold values from -6 to 6
- blocks: int32 [512, 128], P(('gx', 'yz')), may hold values from 0 to 127, as said below
- counts: int32 [512], P(('gx', 'yz')), may hold values from 32 to 128, as said below
Outputs:
- lamb_vector: bfloat16 [3, 512, 256, 512], P(None, 'gx', 'yz')
Inputs may be any that keep to these rules, and one draw needn't show every extreme that they name: `blocks`: the first counts[x] entries of row x are different block numbers. `counts`: some x plane uses all 128 entries.
All inputs are finite; a program needn't handle non-finite values.
Results may differ from a plain program's by a relative error of at most 0.001.
Values sent between devices are 32-bit elements; how exact they have to be, the bound alone decides.
No kernel may reach another device: no remote copies, remote signals or barrier semaphores. Data moves between devices by JAX's collectives and lax.ppermute only.
A program may use at most 128 MiB of HBM per device.

v0:
```python
import jax
import jax.numpy as jnp
import numpy as np
from jax import lax
from jax.sharding import PartitionSpec as P

BY = 8
BZ = 128


root_half = 0.7071067811865476


def from_partner(value, axis, distance):
    mask = 2**distance
    pairs = [(source, source ^ mask) for source in range(lax.axis_size(axis))]
    return lax.ppermute(value, axis, pairs)


def haar_forward(values, dimension):
    length = values.shape[dimension]
    if length == 1:
        return values
    new_shape = values.shape[:dimension] + (length // 2, 2) + values.shape[dimension + 1 :]
    paired = values.reshape(new_shape)
    even_part = lax.index_in_dim(paired, 0, dimension + 1, keepdims=False)
    odd_part = lax.index_in_dim(paired, 1, dimension + 1, keepdims=False)
    coarse_part = haar_forward((even_part + odd_part) * root_half, dimension)
    detail_part = (even_part - odd_part) * root_half
    return jnp.stack([coarse_part, detail_part], axis=dimension + 1).reshape(values.shape)


def haar_inverse(values, dimension):
    length = values.shape[dimension]
    if length == 1:
        return values
    new_shape = values.shape[:dimension] + (length // 2, 2) + values.shape[dimension + 1 :]
    paired = values.reshape(new_shape)
    coarse_part = lax.index_in_dim(paired, 0, dimension + 1, keepdims=False)
    detail_part = lax.index_in_dim(paired, 1, dimension + 1, keepdims=False)
    coarse_part = haar_inverse(coarse_part, dimension)
    even_part = (coarse_part + detail_part) * root_half
    odd_part = (coarse_part - detail_part) * root_half
    return jnp.stack([even_part, odd_part], axis=dimension + 1).reshape(values.shape)


def haar_table(length):
    table = np.zeros((length, length), dtype=np.float32)
    table[0, :] = 1.0 / np.sqrt(length)
    for place in range(1, length):
        level = 0
        while place >> level & 1 == 0:
            level += 1
        half = 1 << level
        weight = 1.0 / np.sqrt(2.0 * half)
        table[place, place - half : place] = weight
        table[place, place : place + half] = -weight
    return jnp.asarray(table)


def last_forward(values):
    length = values.shape[-1]
    table = haar_table(length)
    flat = values.reshape(-1, length)
    result = lax.dot_general(
        flat,
        table,
        (((1,), (1,)), ((), ())),
        precision=lax.Precision.HIGHEST,
        preferred_element_type=jnp.float32,
    )
    return result.reshape(values.shape)


def last_inverse(values):
    length = values.shape[-1]
    table = haar_table(length)
    flat = values.reshape(-1, length)
    result = jnp.dot(
        flat, table, precision=lax.Precision.HIGHEST, preferred_element_type=jnp.float32
    )
    return result.reshape(values.shape)


def kept_blocks(block_rows, lengths, nblocks):
    in_use = jnp.arange(block_rows.shape[1], dtype=jnp.int32)[None, :] < lengths[:, None]
    matches = (
        block_rows[:, :, None] == jnp.arange(nblocks, dtype=jnp.int32)[None, None, :]
    ) & in_use[:, :, None]
    return jnp.any(matches, axis=1).astype(jnp.float32)


def spread_blocks(kept, tall, wide):
    rows_count, across, down = kept.shape
    grown = jnp.broadcast_to(kept[:, :, None, :, None], (rows_count, across, tall, down, wide))
    return grown.reshape(rows_count, across * tall, down * wide)


def cross_product(left, right):
    return jnp.stack(
        [
            left[1] * right[2] - left[2] * right[1],
            left[2] * right[0] - left[0] * right[2],
            left[0] * right[1] - left[1] * right[0],
        ]
    )


def pair_step(mine, partner, position, section_bit):
    active = position % (1 << section_bit) == 0
    higher = position >> section_bit & 1 == 1
    combined = jnp.where(higher, partner - mine, mine + partner) * root_half
    return jnp.where(active, combined, mine)


def body(vorticity, velocity, blocks, counts):
    slab = haar_forward(vorticity.astype(jnp.float32), 1)
    gx_bits = lax.axis_size("gx").bit_length() - 1
    gx_place = lax.axis_index("gx")
    leading = slab[:, 0:1]
    for section_bit in range(gx_bits):
        partner = from_partner(leading, "gx", section_bit)
        leading = pair_step(leading, partner, gx_place, section_bit)
    slab = jnp.concatenate([leading, slab[:, 1:]], axis=1)
    pieces = lax.all_to_all(slab, "yz", split_axis=1, concat_axis=2, tiled=True)
    across = pieces.shape[2] // BY
    down = pieces.shape[3] // BZ
    kept = kept_blocks(blocks, counts, across * down).reshape(blocks.shape[0], across, down)
    mask = spread_blocks(kept, BY, BZ)
    coeff = last_forward(haar_forward(pieces, 2)) * mask[None]
    coeff = haar_inverse(last_inverse(coeff), 2)
    slab = lax.all_to_all(coeff, "yz", split_axis=2, concat_axis=1, tiled=True)
    leading = slab[:, 0:1]
    for section_bit in reversed(range(gx_bits)):
        partner = from_partner(leading, "gx", section_bit)
        leading = pair_step(leading, partner, gx_place, section_bit)
    slab = jnp.concatenate([leading, slab[:, 1:]], axis=1)
    slab = haar_inverse(slab, 1)
    return cross_product(slab, velocity.astype(jnp.float32)).astype(jnp.bfloat16)


def solution(mesh):
    return jax.shard_map(
        body,
        mesh=mesh,
        in_specs=(
            P(None, "gx", "yz", None),
            P(None, "gx", "yz", None),
            P(("gx", "yz"), None),
            P(("gx", "yz")),
        ),
        out_specs=P(None, "gx", "yz", None),
        check_vma=False,
    )
```

profile of v0, /device:TPU:8, one launch (start us, length us, event | category | flops | bytes accessed | tf_op | source)
XLA Modules:
  0.0 177.4 jit_solution(15369540907437576602)
XLA Ops:
  0.0 1.3 convert.14
  1.3 0.2 add_multiply_fusion.3
  2.0 0.2 pad_maximum_fusion
  2.2 1.9 %collective-permute-start = (f32[3,1,8,512]{3,2,1,0:T(8,128)S(1)}, f32[3,1,8,512]{3,2,1,0:T(8,128)S(1)}, u32[]{:S(2)}, u32[]{:S(2)}) collective-permute-start(f32[3,1,8,512]{3,2,1,0:T(8,128)S(1)} %slice.267), channel_id=1, source_target_pairs={{0,32},{32,0},{64,96},{96,64},{128,160},{160,128},{192,224},{224,1... | collective-permute-start | bytes 147464 | tf_op jit(solution)/shard_map/ppermute | solution.py:17
  4.1 1.2 collective-permute-done
  5.3 4.3 %collective-permute-start.1 = (f32[3,1,8,512]{3,2,1,0:T(8,128)S(1)}, f32[3,1,8,512]{3,2,1,0:T(8,128)S(1)}, u32[]{:S(2)}, u32[]{:S(2)}) collective-permute-start(f32[3,1,8,512]{3,2,1,0:T(8,128)S(1)} %select_multiply_fusion.1), channel_id=1, source_target_pairs={{0,64},{32,96},{64,0},{96,32},{128,192},{160,224},{192,128},{224,1... | collective-permute-start | bytes 147464 | tf_op jit(solution)/shard_map/ppermute | solution.py:17
  9.6 2.0 %collective-permute-done.1 = f32[3,1,8,512]{3,2,1,0:T(8,128)S(1)} collective-permute-done((f32[3,1,8,512]{3,2,1,0:T(8,128)S(1)}, f32[3,1,8,512]{3,2,1,0:T(8,128)S(1)}, u32[]{:S(2)}, u32[]{:S(2)}) %collective-permute-start.1) | collective-permute-done | bytes 49184 | tf_op jit(solution)/shard_map/ppermute | solution.py:17
  11.7 6.1 %collective-permute-start.2 = (f32[3,1,8,512]{3,2,1,0:T(8,128)S(1)}, f32[3,1,8,512]{3,2,1,0:T(8,128)S(1)}, u32[]{:S(2)}, u32[]{:S(2)}) collective-permute-start(f32[3,1,8,512]{3,2,1,0:T(8,128)S(1)} %multiply_select_fusion.5), channel_id=1, source_target_pairs={{0,128},{32,160},{64,192},{96,224},{128,0},{160,32},{192,64},{224,... | collective-permute-start | bytes 147464 | tf_op jit(solution)/shard_map/ppermute | solution.py:17
  17.8 2.3 %collective-permute-done.2 = f32[3,1,8,512]{3,2,1,0:T(8,128)S(1)} collective-permute-done((f32[3,1,8,512]{3,2,1,0:T(8,128)S(1)}, f32[3,1,8,512]{3,2,1,0:T(8,128)S(1)}, u32[]{:S(2)}, u32[]{:S(2)}) %collective-permute-start.2) | collective-permute-done | bytes 49184 | tf_op jit(solution)/shard_map/ppermute | solution.py:17
  20.1 9.0 %collective-permute-start.3 = (f32[3,1,8,512]{3,2,1,0:T(8,128)S(1)}, f32[3,1,8,512]{3,2,1,0:T(8,128)S(1)}, u32[]{:S(2)}, u32[]{:S(2)}) collective-permute-start(f32[3,1,8,512]{3,2,1,0:T(8,128)S(1)} %multiply_select_fusion.4), channel_id=1, source_target_pairs={{0,256},{32,288},{64,320},{96,352},{128,384},{160,416},{192,448},{... | collective-permute-start | bytes 147464 | tf_op jit(solution)/shard_map/ppermute | solution.py:17
  29.1 0.1 slice.268
  29.3 1.9 %collective-permute-done.3 = f32[3,1,8,512]{3,2,1,0:T(8,128)S(1)} collective-permute-done((f32[3,1,8,512]{3,2,1,0:T(8,128)S(1)}, f32[3,1,8,512]{3,2,1,0:T(8,128)S(1)}, u32[]{:S(2)}, u32[]{:S(2)}) %collective-permute-start.3) | collective-permute-done | bytes 49184 | tf_op jit(solution)/shard_map/ppermute | solution.py:17
  31.2 0.1 pad_maximum_fusion.1
  31.4 1.3 copy.61
  32.7 10.3 %all-to-all-start = ((f32[3,32,8,512]{3,2,0,1:T(8,128)}), f32[3,32,8,512]{3,2,0,1:T(8,128)S(1)}, u32[]{:S(2)}, u32[]{:S(2)}) async-start(f32[3,32,8,512]{3,2,0,1:T(8,128)} %copy.61), calls=%async_computation | async-start | bytes 3145728 | tf_op jit(solution)/shard_map/all_to_all | solution.py:125
  43.9 1.0 broadcast_bitcast_fusion
  44.9 34.7 %all-to-all-done = f32[3,32,8,512]{3,2,0,1:T(8,128)S(1)} async-done(((f32[3,32,8,512]{3,2,0,1:T(8,128)}), f32[3,32,8,512]{3,2,0,1:T(8,128)S(1)}, u32[]{:S(2)}, u32[]{:S(2)}) %all-to-all-start) | async-done | bytes 1572896 | tf_op jit(solution)/shard_map/all_to_all | solution.py:125
  79.6 0.1 copy.62
  79.7 0.9 reshape.627
  80.7 1.2 fusion.10
  81.9 0.3 add_multiply_fusion.2
  82.2 0.5 mul.437
  82.7 0.8 add_multiply_fusion.6
  83.5 0.4 add_multiply_fusion.10
  83.9 0.2 add_multiply_fusion.14
  84.6 0.2 pad_maximum_fusion.16
  84.7 0.3 pad_maximum_fusion.12
  85.1 0.7 pad_maximum_fusion.6
  85.8 0.5 stack_reshape.43
  86.4 0.1 pad_maximum_fusion.2
  86.5 1.2 copy.65
  87.7 1.1 dot_general.10
  88.8 4.2 %convolution_multiply_fusion = f32[3,256,512]{2,1,0:T(8,128)S(1)} fusion(f32[3,256,512]{2,1,0:T(8,128)S(1)} %dot_general.10, f32[512,512,1]{1,0,2:T(8,128)} %constant.81, f32[256,512]{1,0:T(8,128)} %broadcast_bitcast_fusion), kind=kOutput, calls=%fused_computation.13 | convolution fusion | flops 2416312320 | bytes 4718592 | tf_op jit(solution)/shard_map/dot_general | solution.py:65
  93.0 0.9 reshape.628
  94.0 3.9 %fusion.2 = f32[3,1,128,2,512]{4,2,3,0,1:T(8,128)S(1)} fusion(f32[512,512,1,1]{1,0,3,2:T(8,128)} %constant.82, f32[3,128,2,512]{3,2,1,0:T(2,128)S(1)} %reshape.628), kind=kOutput, calls=%fused_computation.12 | convolution fusion | flops 2415919104 | bytes 4194304 | tf_op jit(solution)/shard_map/dot_general | solution.py:79
  98.0 0.5 reshape_squeeze.33
  98.4 0.3 slice.286
  99.3 0.2 add_multiply_fusion.13
  99.5 0.2 pad_maximum_fusion.17
  99.6 0.4 add_multiply_fusion.9
  100.1 0.3 pad_maximum_fusion.13
  100.4 1.0 add_multiply_fusion.5
  101.4 0.7 pad_maximum_fusion.7
  102.1 0.5 reshape.635
  102.7 0.2 add_multiply_fusion.1
  103.0 1.6 copy.67
  104.7 1.1 copy.68
  105.7 42.5 %all_to_all.21 = f32[3,1,256,512]{3,1,0,2:T(1,128)S(1)} all-to-all(f32[3,1,256,512]{3,1,0,2:T(1,128)S(1)} %copy.68), channel_id=1, replica_groups=mesh['gx'=16,'yz'=32] {'yz'}, dimensions={2} | all-to-all | bytes 3145728 | tf_op jit(solution)/shard_map/all_to_all | solution.py:132
  148.2 0.1 copy.86
  148.4 7.1 %collective-permute-start.4 = (f32[3,1,8,512]{3,2,1,0:T(8,128)S(1)}, f32[3,1,8,512]{3,2,1,0:T(8,128)S(1)}, u32[]{:S(2)}, u32[]{:S(2)}) collective-permute-start(f32[3,1,8,512]{3,2,1,0:T(8,128)S(1)} %slice.301), channel_id=1, source_target_pairs={{0,256},{32,288},{64,320},{96,352},{128,384},{160,416},{192,448},{... | collective-permute-start | bytes 147464 | tf_op jit(solution)/shard_map/ppermute | solution.py:17
  155.5 2.9 %collective-permute-done.4 = f32[3,1,8,512]{3,2,1,0:T(8,128)S(1)} collective-permute-done((f32[3,1,8,512]{3,2,1,0:T(8,128)S(1)}, f32[3,1,8,512]{3,2,1,0:T(8,128)S(1)}, u32[]{:S(2)}, u32[]{:S(2)}) %collective-permute-start.4) | collective-permute-done | bytes 49184 | tf_op jit(solution)/shard_map/ppermute | solution.py:17
  158.4 4.9 %collective-permute-start.5 = (f32[3,1,8,512]{3,2,1,0:T(8,128)S(1)}, f32[3,1,8,512]{3,2,1,0:T(8,128)S(1)}, u32[]{:S(2)}, u32[]{:S(2)}) collective-permute-start(f32[3,1,8,512]{3,2,1,0:T(8,128)S(1)} %multiply_select_fusion.2), channel_id=1, source_target_pairs={{0,128},{32,160},{64,192},{96,224},{128,0},{160,32},{192,64},{224,... | collective-permute-start | bytes 147464 | tf_op jit(solution)/shard_map/ppermute | solution.py:17
  163.3 2.1 %collective-permute-done.5 = f32[3,1,8,512]{3,2,1,0:T(8,128)S(1)} collective-permute-done((f32[3,1,8,512]{3,2,1,0:T(8,128)S(1)}, f32[3,1,8,512]{3,2,1,0:T(8,128)S(1)}, u32[]{:S(2)}, u32[]{:S(2)}) %collective-permute-start.5) | collective-permute-done | bytes 49184 | tf_op jit(solution)/shard_map/ppermute | solution.py:17
  165.3 4.5 %collective-permute-start.6 = (f32[3,1,8,512]{3,2,1,0:T(8,128)S(1)}, f32[3,1,8,512]{3,2,1,0:T(8,128)S(1)}, u32[]{:S(2)}, u32[]{:S(2)}) collective-permute-start(f32[3,1,8,512]{3,2,1,0:T(8,128)S(1)} %multiply_select_fusion.1), channel_id=1, source_target_pairs={{0,64},{32,96},{64,0},{96,32},{128,192},{160,224},{192,128},{224,1... | collective-permute-start | bytes 147464 | tf_op jit(solution)/shard_map/ppermute | solution.py:17
  169.8 2.1 %collective-permute-done.6 = f32[3,1,8,512]{3,2,1,0:T(8,128)S(1)} collective-permute-done((f32[3,1,8,512]{3,2,1,0:T(8,128)S(1)}, f32[3,1,8,512]{3,2,1,0:T(8,128)S(1)}, u32[]{:S(2)}, u32[]{:S(2)}) %collective-permute-start.6) | collective-permute-done | bytes 49184 | tf_op jit(solution)/shard_map/ppermute | solution.py:17
  171.9 1.9 %collective-permute-start.7 = (f32[3,1,8,512]{3,2,1,0:T(8,128)S(1)}, f32[3,1,8,512]{3,2,1,0:T(8,128)S(1)}, u32[]{:S(2)}, u32[]{:S(2)}) collective-permute-start(f32[3,1,8,512]{3,2,1,0:T(8,128)S(1)} %multiply_select_fusion), channel_id=1, source_target_pairs={{0,32},{32,0},{64,96},{96,64},{128,160},{160,128},{192,224},{224,1... | collective-permute-start | bytes 147464 | tf_op jit(solution)/shard_map/ppermute | solution.py:17
  173.8 0.2 convert_element_type.19
  174.0 0.1 slice.302
  174.2 0.8 collective-permute-done.7
  175.0 0.1 pad_maximum_fusion.4
  175.6 0.2 subtract_multiply_fusion
  175.8 0.1 fusion.5
  176.0 0.5 subtract_convert_fusion.2
  176.5 1.0 pad_maximum_fusion.9
  (60 shorter events, 2.0 us)
Async XLA Ops:
  2.2 3.1 %collective-permute-start = (f32[3,1,8,512]{3,2,1,0:T(8,128)S(1)}, f32[3,1,8,512]{3,2,1,0:T(8,128)S(1)}, u32[]{:S(2)}, u32[]{:S(2)}) collective-permute-start(f32[3,1,8,512]{3,2,1,0:T(8,128)S(1)} %slice.267), channel_id=1, source_target_pairs={{0,32},{32,0},{64,96},{96,64},{128,160},{160,128},{192,224},{224,1... | collective-permute-start | bytes 147464 | tf_op jit(solution)/shard_map/ppermute | solution.py:17
  5.3 6.3 %collective-permute-start.1 = (f32[3,1,8,512]{3,2,1,0:T(8,128)S(1)}, f32[3,1,8,512]{3,2,1,0:T(8,128)S(1)}, u32[]{:S(2)}, u32[]{:S(2)}) collective-permute-start(f32[3,1,8,512]{3,2,1,0:T(8,128)S(1)} %select_multiply_fusion.1), channel_id=1, source_target_pairs={{0,64},{32,96},{64,0},{96,32},{128,192},{160,224},{192,128},{224,1... | collective-permute-start | bytes 147464 | tf_op jit(solution)/shard_map/ppermute | solution.py:17
  11.7 8.4 %collective-permute-start.2 = (f32[3,1,8,512]{3,2,1,0:T(8,128)S(1)}, f32[3,1,8,512]{3,2,1,0:T(8,128)S(1)}, u32[]{:S(2)}, u32[]{:S(2)}) collective-permute-start(f32[3,1,8,512]{3,2,1,0:T(8,128)S(1)} %multiply_select_fusion.5), channel_id=1, source_target_pairs={{0,128},{32,160},{64,192},{96,224},{128,0},{160,32},{192,64},{224,... | collective-permute-start | bytes 147464 | tf_op jit(solution)/shard_map/ppermute | solution.py:17
  20.1 11.1 %collective-permute-start.3 = (f32[3,1,8,512]{3,2,1,0:T(8,128)S(1)}, f32[3,1,8,512]{3,2,1,0:T(8,128)S(1)}, u32[]{:S(2)}, u32[]{:S(2)}) collective-permute-start(f32[3,1,8,512]{3,2,1,0:T(8,128)S(1)} %multiply_select_fusion.4), channel_id=1, source_target_pairs={{0,256},{32,288},{64,320},{96,352},{128,384},{160,416},{192,448},{... | collective-permute-start | bytes 147464 | tf_op jit(solution)/shard_map/ppermute | solution.py:17
  32.7 11.0 %copy-start.1 = (s32[1,128]{1,0:T(1,128)S(1)}, s32[1,128]{1,0:T(1,128)}, u32[]{:S(2)}) copy-start(s32[1,128]{1,0:T(1,128)} %param.8) | copy-start | bytes 1540
  32.7 46.9 %all-to-all-start = ((f32[3,32,8,512]{3,2,0,1:T(8,128)}), f32[3,32,8,512]{3,2,0,1:T(8,128)S(1)}, u32[]{:S(2)}, u32[]{:S(2)}) async-start(f32[3,32,8,512]{3,2,0,1:T(8,128)} %copy.61), calls=%async_computation | async-start | bytes 3145728 | tf_op jit(solution)/shard_map/all_to_all | solution.py:125
  148.2 25.6 %copy-start = (bf16[3,32,8,512]{3,2,1,0:T(8,128)(2,1)S(1)}, bf16[3,32,8,512]{3,2,1,0:T(8,128)(2,1)}, u32[]{:S(2)}) copy-start(bf16[3,32,8,512]{3,2,1,0:T(8,128)(2,1)} %param.7) | copy-start | bytes 2359300
  148.4 10.0 %collective-permute-start.4 = (f32[3,1,8,512]{3,2,1,0:T(8,128)S(1)}, f32[3,1,8,512]{3,2,1,0:T(8,128)S(1)}, u32[]{:S(2)}, u32[]{:S(2)}) collective-permute-start(f32[3,1,8,512]{3,2,1,0:T(8,128)S(1)} %slice.301), channel_id=1, source_target_pairs={{0,256},{32,288},{64,320},{96,352},{128,384},{160,416},{192,448},{... | collective-permute-start | bytes 147464 | tf_op jit(solution)/shard_map/ppermute | solution.py:17
  158.4 6.9 %collective-permute-start.5 = (f32[3,1,8,512]{3,2,1,0:T(8,128)S(1)}, f32[3,1,8,512]{3,2,1,0:T(8,128)S(1)}, u32[]{:S(2)}, u32[]{:S(2)}) collective-permute-start(f32[3,1,8,512]{3,2,1,0:T(8,128)S(1)} %multiply_select_fusion.2), channel_id=1, source_target_pairs={{0,128},{32,160},{64,192},{96,224},{128,0},{160,32},{192,64},{224,... | collective-permute-start | bytes 147464 | tf_op jit(solution)/shard_map/ppermute | solution.py:17
  165.3 6.5 %collective-permute-start.6 = (f32[3,1,8,512]{3,2,1,0:T(8,128)S(1)}, f32[3,1,8,512]{3,2,1,0:T(8,128)S(1)}, u32[]{:S(2)}, u32[]{:S(2)}) collective-permute-start(f32[3,1,8,512]{3,2,1,0:T(8,128)S(1)} %multiply_select_fusion.1), channel_id=1, source_target_pairs={{0,64},{32,96},{64,0},{96,32},{128,192},{160,224},{192,128},{224,1... | collective-permute-start | bytes 147464 | tf_op jit(solution)/shard_map/ppermute | solution.py:17
  171.9 3.1 %collective-permute-start.7 = (f32[3,1,8,512]{3,2,1,0:T(8,128)S(1)}, f32[3,1,8,512]{3,2,1,0:T(8,128)S(1)}, u32[]{:S(2)}, u32[]{:S(2)}) collective-permute-start(f32[3,1,8,512]{3,2,1,0:T(8,128)S(1)} %multiply_select_fusion), channel_id=1, source_target_pairs={{0,32},{32,0},{64,96},{96,64},{128,160},{160,128},{192,224},{224,1... | collective-permute-start | bytes 147464 | tf_op jit(solution)/shard_map/ppermute | solution.py:17
where the time goes:
time: 178 us; the launch traced here: 177 us
  waiting for transfers between devices  50 us (28%)
  starting transfers between devices  49.9 us (28%)
  blocking collectives  42.5 us (24%)
  local copies, waits for them, and re-layouts  13.6 us (8%)
  other arithmetic  11.8 us (7%)
  matrix products  8.16 us (5%)
    all_to_all x1, blocking collectives, body(): slab = lax.all_to_all(coeff, 'yz', split_axis=2, concat_axis=1, tiled=True)  42.5 us
    ppermute x8, starting transfers between devices, from_partner(): return lax.ppermute(value, axis, pairs)  39.6 us
    all_to_all x1, waiting for transfers between devices, body(): pieces = lax.all_to_all(slab, 'yz', split_axis=1, concat_axis=2, tiled=True)  34.7 us
    ppermute x8, waiting for transfers between devices, from_partner(): return lax.ppermute(value, axis, pairs)  15.3 us
    all_to_all x1, starting transfers between devices, body(): pieces = lax.all_to_all(slab, 'yz', split_axis=1, concat_axis=2, tiled=True)  10.3 us
    dot_general x1, matrix products, last_forward(): lax.dot_general(flat, table, (((1,), (1,)), ((), ())), precision=lax.Prec...  4.21 us
    dot_general x1, matrix products, last_inverse(): jnp.dot(flat, table, precision=lax.Precision.HIGHEST, preferred_element_t...  3.94 us
  transfers between devices with their start and end apart: 9, of which 9 were waited for; matrix products, arithmetic and copies ran while one was open for 1% of the time, Pallas kernels for 0%

commit v1 on v0

v1 whole, which is shorter than its diff:
```python
import jax
import jax.numpy as jnp
from jax import lax
from jax.experimental import pallas as pl
from jax.experimental.pallas import tpu as pltpu
from jax.sharding import PartitionSpec as P


BY = 8
BZ = 128
ZB = 4
CHUNKS = 12
ROWS = 13
EXTRA = 12
CORNER = 48
SLICE = 16
HALF = 64
OWN_KEPT = 48
ALL_KEPT = 64
LINE_KEPT = 52
PACKED = 16
F32 = jnp.float32
BF16 = jnp.bfloat16


def iota(shape, dimension):
    return lax.broadcasted_iota(jnp.int32, shape, dimension)


def sign_of(place, cell, length):
    span = jnp.where(place == 0, length, 2 * (place & -place))
    sign = jnp.where((cell < place) | (place == 0), 1.0, -1.0)
    return jnp.where((cell ^ place) < span, sign, 0.0)


def weight_of(place, cell, length):
    span = jnp.where(place == 0, length, 2 * (place & -place))
    return sign_of(place, cell, length) / span.astype(F32)


def mix_table(wide):
    coarse, block = iota((wide, BZ), 1), iota((wide, BZ), 0) // BZ
    table = weight_of(jnp.minimum(coarse, ZB - 1), block, ZB)
    table = table - jnp.where(coarse == block, 1.0, 0.0)
    return (jnp.where(coarse < ZB, table, 0.0) / BZ).astype(BF16)


def unmix_table(wide):
    block, coarse = iota((wide, BZ), 1), iota((wide, BZ), 0) // BZ
    table = sign_of(coarse, jnp.minimum(block, ZB - 1), ZB)
    table = table - jnp.where(coarse == block, 1.0, 0.0)
    return (jnp.where(block < ZB, table, 0.0) / BZ).astype(BF16)


def halves(value):
    high = value.astype(BF16)
    low = (value - high.astype(F32)).astype(BF16)
    return high, low


def left_product(table, value):
    high, low = halves(value)
    return jnp.dot(table, high, preferred_element_type=F32) + jnp.dot(
        table, low, preferred_element_type=F32
    )


def right_product(value, table):
    high, low = halves(value)
    return jnp.dot(high, table, preferred_element_type=F32) + jnp.dot(
        low, table, preferred_element_type=F32
    )


def remix(value, table):
    shift = right_product(value, table)
    return jnp.concatenate(
        [value[:, zb * BZ : (zb + 1) * BZ] + shift[:, zb : zb + 1] for zb in range(ZB)], axis=1
    )


def forward_levels(values):
    count = len(values)
    result = [None] * count
    step = 1
    while step < count:
        for place in range(step, count, 2 * step):
            low, high = values[place - step], values[place]
            result[place] = (low - high) * 0.5
            values[place - step] = (low + high) * 0.5
        step *= 2
    result[0] = values[0]
    return result


def inverse_levels(values):
    count = len(values)
    values = list(values)
    step = count // 2
    while step >= 1:
        for place in range(step, count, 2 * step):
            mean, detail = values[place - step], values[place]
            values[place - step] = mean + detail
            values[place] = mean - detail
        step //= 2
    return values


def spread_table(part, wide):
    cell, lane = iota((wide, BZ), 0), iota((wide, BZ), 1)
    return jnp.where(lane == part * SLICE + cell % SLICE, 1.0, 0.0).astype(BF16)


def gather_table(part, wide):
    lane, cell = iota((BZ, wide), 0), iota((BZ, wide), 1)
    return jnp.where(lane == part * SLICE + cell % SLICE, 1.0, 0.0).astype(BF16)


def pick_table(first, wide):
    lane, cell = iota((BZ, wide), 0), iota((BZ, wide), 1)
    return jnp.where(lane == first + cell // BZ, 1.0, 0.0).astype(BF16)


def head_kernel(counts_hbm, blocks_hbm, vort_hbm, send, line, own, counts, blocks, vort, sems):
    parts, cells, wide = vort.shape
    planes = cells // BY
    copies = [
        pltpu.make_async_copy(vort_hbm.at[c], vort.at[c], sems.at[c]) for c in range(parts)
    ]
    copies.append(pltpu.make_async_copy(blocks_hbm, blocks, sems.at[parts]))
    copies.append(pltpu.make_async_copy(counts_hbm, counts, sems.at[parts + 1]))
    for copy in copies:
        copy.start()
    row, column = iota((planes + BY, cells), 0), iota((planes + BY, cells), 1)
    fine = jnp.where(row - planes == column % BY, 1.0, 0.0) - 1.0 / BY
    table = jnp.where(
        row < planes,
        weight_of(jnp.minimum(row, planes - 1), column // BY, planes) / BY,
        fine / planes,
    ).astype(BF16)
    mix = mix_table(wide)
    target, cell = iota((planes, wide), 0), iota((planes, wide), 1)
    extra = jnp.zeros((planes, BZ), F32)
    for c in range(parts):
        copies[c].wait()
        rows = remix(jnp.dot(table, vort[c], preferred_element_type=F32), mix)
        for zb in range(ZB):
            chunk = c * ZB + zb
            part = rows[:, zb * BZ : (zb + 1) * BZ]
            send[pl.ds(chunk, planes, stride=ROWS), :] = part[0:planes]
            line[chunk * BY : (chunk + 1) * BY, :] = part[planes : planes + BY]
        corner = jnp.where(cell // SLICE == target, rows[0:1], 0.0)
        extra = extra + right_product(corner, spread_table(c, wide))
    copies[parts].wait()
    copies[parts + 1].wait()
    nblocks = blocks.shape[1]
    square = (nblocks, nblocks)
    listed = (blocks[...] == iota(square, 0)) & (iota(square, 1) < counts[0])
    kept = lax.dot_general(
        jnp.ones((planes, nblocks), BF16),
        jnp.where(listed, 1.0, 0.0).astype(BF16),
        (((1,), (1,)), ((), ())),
        preferred_element_type=F32,
    )
    kept = jnp.minimum(kept, 1.0)
    own[...] = kept[0:8]
    target, block = iota((planes, nblocks), 0), iota((planes, nblocks), 1)
    block_row, lane = iota(square, 0), iota(square, 1)
    mine = jnp.where(block // ZB == target, kept, 0.0).astype(BF16)
    slot = jnp.where(lane == OWN_KEPT + block_row % ZB, 1.0, 0.0).astype(BF16)
    extra = extra + jnp.dot(mine, slot, preferred_element_type=F32)
    every = jnp.where(block % ZB == target * SLICE // BZ, kept, 0.0).astype(BF16)
    slot = jnp.where(lane == ALL_KEPT + block_row // ZB, 1.0, 0.0).astype(BF16)
    extra = extra + jnp.dot(every, slot, preferred_element_type=F32)
    send[pl.ds(EXTRA, planes, stride=ROWS), :] = extra


def level_tables(length):
    square = (length, length)
    forward = weight_of(iota(square, 0), iota(square, 1), length).astype(BF16)
    inverse = sign_of(iota(square, 1), iota(square, 0), length).astype(BF16)
    return forward, inverse


def plane_kernel(own, recv, after, back, corner):
    del after
    planes = recv.shape[0] // ROWS
    forward, inverse = level_tables(planes)
    spread = jnp.where(iota((planes, BZ), 1) // ZB == iota((planes, BZ), 0), own[0:1], 0.0)
    pick = jnp.where(iota((BZ, ZB * BZ), 0) % ZB == iota((BZ, ZB * BZ), 1) // BZ, 1.0, 0.0)
    mask = jnp.dot(spread.astype(BF16), pick.astype(BF16), preferred_element_type=F32)
    extra = recv[pl.ds(EXTRA, planes, stride=ROWS), :]
    lane = iota((PACKED, BZ), 1)
    row = iota((PACKED, BZ), 0)
    heads = extra[0:1]
    low = jnp.sum(jnp.where(lane == ALL_KEPT + row, heads, 0.0), axis=1, keepdims=True)
    high = jnp.sum(jnp.where(lane == ALL_KEPT + PACKED + row, heads, 0.0), axis=1, keepdims=True)
    levels = left_product(forward, jnp.where(iota((planes, BZ), 1) < CORNER, extra, 0.0))
    packed = levels[0:PACKED] + pltpu.roll(levels[PACKED:planes], HALF, 1)
    packed = jnp.where(lane == CORNER, low, packed)
    packed = jnp.where(lane == HALF + CORNER, high, packed)
    shifted = pltpu.roll(jnp.broadcast_to(heads, (PACKED, BZ)), LINE_KEPT - OWN_KEPT, 1)
    packed = jnp.where((lane >= LINE_KEPT) & (lane < LINE_KEPT + ZB), shifted, packed)
    for g in range(corner.shape[0]):
        corner[g] = packed
    for c in range(3):
        data = jnp.concatenate(
            [recv[pl.ds(c * ZB + zb, planes, stride=ROWS), :] for zb in range(ZB)], axis=1
        )
        data = left_product(inverse, left_product(forward, data) * mask)
        for zb in range(ZB):
            back[pl.ds(c * ZB + zb, planes, stride=ROWS), :] = data[:, zb * BZ : (zb + 1) * BZ]


def corner_kernel(place, gathered, back_in, after, back):
    del after
    slabs = gathered.shape[0]
    planes = back.shape[0] // ROWS
    lane = iota((PACKED, BZ), 1)
    back[...] = back_in[...]
    values = forward_levels([gathered[g] for g in range(slabs)])
    total = jnp.zeros((PACKED, BZ), F32)
    for p in range(slabs):
        low = gathered[p, :, CORNER : CORNER + 1]
        high = gathered[p, :, HALF + CORNER : HALF + CORNER + 1]
        sign = sign_of(jnp.int32(p), place[0], slabs)
        total = total + values[p] * jnp.where(lane < HALF, low, high) * sign
    total = jnp.concatenate([total, pltpu.roll(total, HALF, 1)], axis=0)
    total = jnp.where(iota((planes, BZ), 1) < CORNER, total, 0.0)
    back[pl.ds(EXTRA, planes, stride=ROWS), :] = left_product(level_tables(planes)[1], total)


def details_kernel(recv, vort_hbm, velocity_hbm, after, detail, velocity, vort, sems):
    del after
    parts, cells, wide = vort.shape
    planes = cells // BY
    copies = [
        pltpu.make_async_copy(vort_hbm.at[c], vort.at[c], sems.at[c]) for c in range(parts)
    ]
    copies.append(pltpu.make_async_copy(velocity_hbm, velocity, sems.at[parts]))
    for copy in copies:
        copy.start()
    tall = jnp.where(
        (iota((cells, planes), 0) // BY == iota((cells, planes), 1))
        & (iota((cells, planes), 1) > 0),
        1.0,
        0.0,
    ).astype(BF16)
    kept = recv[pl.ds(EXTRA, planes, stride=ROWS), :].astype(BF16)
    kept = jnp.dot(tall, kept, preferred_element_type=F32).astype(BF16)
    mask = jnp.dot(kept, pick_table(OWN_KEPT, wide), preferred_element_type=F32)
    row, column = iota((cells, cells), 0), iota((cells, cells), 1)
    same = jnp.where(row % BY == column % BY, 1.0, 0.0)
    forward = (weight_of(row // BY, column // BY, planes) * (same - 1.0 / BY)).astype(BF16)
    inverse = (sign_of(column // BY, row // BY, planes) * same).astype(BF16)
    mix, unmix = mix_table(wide), unmix_table(wide)
    for c in range(parts):
        copies[c].wait()
        rows = jnp.dot(forward, vort[c], preferred_element_type=F32)
        rows = remix(rows, mix) * mask
        detail[c] = remix(left_product(inverse, rows), unmix)
    copies[parts].wait()


def finish_kernel(place, got, gathered, detail, velocity, *refs):
    pairs, (out, rows) = refs[:-2], refs[-2:]
    planes = got.shape[0] // ROWS
    parts, cells, wide = velocity.shape
    wanted = [gathered[0, 0:1, :]]
    for level in range(len(pairs) // 2):
        half = 1 << level
        slab = place[0] // (2 * half) * (2 * half) + half
        wanted.append(gathered[slab, 0:1, :])
    wanted += [jnp.zeros((1, BZ), F32)] * (8 - len(wanted))
    wanted = jnp.concatenate(wanted, axis=0).astype(BF16)
    mask = jnp.dot(wanted, pick_table(LINE_KEPT, wide), preferred_element_type=F32)
    inverse = level_tables(planes)[1]
    extra = got[pl.ds(EXTRA, planes, stride=ROWS), :]
    target, cell = iota((planes, wide), 0), iota((planes, wide), 1)
    for c in range(parts):
        for zb in range(ZB):
            span = slice((c * ZB + zb) * BY, (c * ZB + zb + 1) * BY)
            lanes = slice(zb * BZ, (zb + 1) * BZ)
            total = (pairs[-2][span, :] + pairs[-1][span, :]) * 0.5 * mask[0:1, lanes]
            for level in range(len(pairs) // 2):
                mine, other = pairs[2 * level][span, :], pairs[2 * level + 1][span, :]
                total = total + (mine - other) * 0.5 * mask[level + 1 : level + 2, lanes]
            rows[parts * planes + c * BY : parts * planes + (c + 1) * BY, lanes] = total
        corner = right_product(extra, gather_table(c, wide))
        corner = jnp.sum(jnp.where(cell // SLICE == target, corner, 0.0), axis=0, keepdims=True)
        data = jnp.concatenate(
            [got[pl.ds(c * ZB + zb, planes, stride=ROWS), :] for zb in range(ZB)], axis=1
        )
        data = jnp.where(target == 0, corner, data)
        rows[c * planes : (c + 1) * planes, :] = left_product(inverse, data)
    rows[...] = remix(rows[...], unmix_table(wide))
    for x in range(planes):
        span = slice(x * BY, (x + 1) * BY)
        smooth = [
            detail[c, span, :]
            + rows[c * planes + x : c * planes + x + 1, :]
            + rows[parts * planes + c * BY : parts * planes + (c + 1) * BY, :]
            for c in range(parts)
        ]
        speed = [velocity[c, span, :].astype(F32) for c in range(parts)]
        for c in range(parts):
            a, b = (c + 1) % parts, (c + 2) % parts
            out[c, span, :] = (smooth[a] * speed[b] - smooth[b] * speed[a]).astype(BF16)


def exchange(value, axis):
    return lax.all_to_all(value, axis, split_axis=0, concat_axis=0, tiled=True)


def over_yz(rows, planes):
    moved = exchange(rows.reshape(planes, ROWS, 1, BZ), "yz")
    return moved.reshape(planes * ROWS, BZ)


def from_partner(value, distance):
    pairs = [(source, source ^ distance) for source in range(lax.axis_size("gx"))]
    return lax.ppermute(value, "gx", pairs)


def body(vorticity, velocity, blocks, counts):
    parts, planes, tall, wide = vorticity.shape
    cells = planes * tall
    slabs = lax.axis_size("gx")
    smem = pl.BlockSpec(memory_space=pltpu.SMEM)
    vmem = pl.BlockSpec(memory_space=pltpu.VMEM)
    hbm = pl.BlockSpec(memory_space=pl.ANY)
    params = pltpu.CompilerParams(vmem_limit_bytes=32 * 1024 * 1024)
    large = pltpu.CompilerParams(vmem_limit_bytes=60 * 1024 * 1024)
    place = jnp.stack([lax.axis_index("gx"), lax.axis_index("yz")]).astype(jnp.int32)
    vort = vorticity.reshape(parts, cells, wide)
    speed = velocity.reshape(parts, cells, wide)

    def array(*shape):
        return jax.ShapeDtypeStruct(shape, F32)

    send, line, own = pl.pallas_call(
        head_kernel,
        out_shape=(array(planes * ROWS, BZ), array(CHUNKS * BY, BZ), array(8, BZ)),
        in_specs=[hbm, hbm, hbm],
        out_specs=(vmem, vmem, vmem),
        scratch_shapes=[
            pltpu.SMEM(counts.shape, jnp.int32),
            pltpu.VMEM(blocks.shape, jnp.int32),
            pltpu.VMEM((parts, cells, wide), BF16),
            pltpu.SemaphoreType.DMA((parts + 2,)),
        ],
        compiler_params=large,
        name="head",
    )(counts, blocks, vort)
    pairs = []
    distance = 1
    while distance < slabs:
        other = from_partner(line, distance)
        pairs += [line, other]
        line = (line + other) * 0.5
        distance *= 2
    recv = over_yz(send, planes)
    back, corner = pl.pallas_call(
        plane_kernel,
        out_shape=(array(planes * ROWS, BZ), array(slabs, PACKED, BZ)),
        in_specs=[vmem, vmem, hbm],
        out_specs=(vmem, vmem),
        compiler_params=params,
        name="plane",
    )(own, recv, pairs[min(4, len(pairs) - 2)])
    gathered = exchange(corner, "gx")
    back = pl.pallas_call(
        corner_kernel,
        out_shape=array(planes * ROWS, BZ),
        in_specs=[smem, vmem, vmem, hbm],
        out_specs=vmem,
        compiler_params=params,
        name="corner",
    )(place, gathered, back, pairs[min(6, len(pairs) - 2)])
    got = over_yz(back, planes)
    detail, speed = pl.pallas_call(
        details_kernel,
        out_shape=(array(parts, cells, wide), jax.ShapeDtypeStruct((parts, cells, wide), BF16)),
        in_specs=[vmem, hbm, hbm, hbm],
        out_specs=(vmem, vmem),
        scratch_shapes=[
            pltpu.VMEM((parts, cells, wide), BF16),
            pltpu.SemaphoreType.DMA((parts + 1,)),
        ],
        compiler_params=params,
        cost_estimate=pl.CostEstimate(
            flops=24 * parts * cells * cells * wide,
            bytes_accessed=6 * parts * cells * wide,
            transcendentals=0,
        ),
        name="details",
    )(recv, vort, speed, back)
    out = pl.pallas_call(
        finish_kernel,
        out_shape=jax.ShapeDtypeStruct((parts, cells, wide), BF16),
        in_specs=[smem] + [vmem] * (4 + len(pairs)),
        out_specs=vmem,
        scratch_shapes=[pltpu.VMEM((parts * (planes + tall), wide), F32)],
        compiler_params=params,
        name="finish",
    )(place, got, gathered, detail, speed, *pairs)
    return out.reshape(parts, planes, tall, wide)


def solution(mesh):
    return jax.shard_map(
        body,
        mesh=mesh,
        in_specs=(
            P(None, "gx", "yz", None),
            P(None, "gx", "yz", None),
            P(("gx", "yz"), None),
            P(("gx", "yz")),
        ),
        out_specs=P(None, "gx", "yz", None),
        check_vma=False,
    )
```

time: 178 us -> 76.7 us (0.43)
  blocking collectives: 42.5 us -> 0 us
  waiting for transfers between devices: 50 us -> 12.7 us
  Pallas kernels: 0 us -> 13.9 us
  other arithmetic: 11.8 us -> 0.91 us
  local copies, waits for them, and re-layouts: 13.6 us -> 3.82 us
  matrix products: 8.16 us -> 0 us
  starting transfers between devices: 49.9 us -> 44 us
    all_to_all x1 -> x0, blocking collectives: 42.5 us -> none  [body(): slab = lax.all_to_all(coeff, 'yz', split_axis=2, concat_axis=1, tiled=True)]
    all_to_all x1 -> x3, waiting for transfers between devices: 34.7 us -> 10.2 us  [exchange(): return lax.all_to_all(value, axis, split_axis=0, concat_axis=0, tiled=True)]
    ppermute x8 -> x4, starting transfers between devices: 39.6 us -> 15.8 us  [from_partner(): return lax.ppermute(value, 'gx', pairs)]
    all_to_all x1 -> x3, starting transfers between devices: 10.3 us -> 28.2 us  [exchange(): return lax.all_to_all(value, axis, split_axis=0, concat_axis=0, tiled=True)]
    pallas_call x0 -> x5, Pallas kernels: none -> 13.9 us  [the longest x1 4.72 us: body(): pl.pallas_call(details_kernel, out_shape=(array(parts, cells, wide), jax....]
    ppermute x8 -> x4, waiting for transfers between devices: 15.3 us -> 2.49 us  [from_partner(): return lax.ppermute(value, 'gx', pairs)]
    dot_general x2 -> x0, matrix products: 8.16 us -> none  [the longest x1 4.21 us: last_forward(): lax.dot_general(flat, table, (((1,), (1,)), ((), ())), precision=lax.Prec...]
    another operation x26 -> x1, other arithmetic: 5 us -> 0.08 us  [body(): jnp.stack([lax.axis_index('gx'), lax.axis_index('yz')]).astype(jnp.int32)]
  transfers between devices with their start and end apart: 9 -> 7, of which waited for: 9 -> 4; matrix products, arithmetic and copies ran while one was open for 1% -> 1% of each run, Pallas kernels for 0% -> 7%
where the time goes in v1:
time: 76.7 us; the launch traced here: 76.1 us
  starting transfers between devices  44 us (57%)
  Pallas kernels  13.9 us (18%)
  waiting for transfers between devices  12.7 us (17%)
  local copies, waits for them, and re-layouts  3.82 us (5%)
  other arithmetic  0.91 us (1%)
  between operations  0.8 us (1%)
    all_to_all x3, starting transfers between devices, exchange(): return lax.all_to_all(value, axis, split_axis=0, concat_axis=0, tiled=True)  28.2 us
    ppermute x4, starting transfers between devices, from_partner(): return lax.ppermute(value, 'gx', pairs)  15.8 us
    all_to_all x3, waiting for transfers between devices, exchange(): return lax.all_to_all(value, axis, split_axis=0, concat_axis=0, tiled=True)  10.2 us
    pallas_call x1, Pallas kernels, body(): pl.pallas_call(details_kernel, out_shape=(array(parts, cells, wide), jax....  4.72 us
    unnamed x12, local copies, waits for them, and re-layouts  3.82 us
    pallas_call x1, Pallas kernels, body(): pl.pallas_call(head_kernel, out_shape=(array(planes * ROWS, BZ), array(CH...  3.64 us
    pallas_call x1, Pallas kernels, body(): pl.pallas_call(finish_kernel, out_shape=jax.ShapeDtypeStruct((parts, cell...  3.04 us
    ppermute x4, waiting for transfers between devices, from_partner(): return lax.ppermute(value, 'gx', pairs)  2.49 us
  transfers between devices with their start and end apart: 7, of which 4 were waited for; matrix products, arithmetic and copies ran while one was open for 1% of the time, Pallas kernels for 7%

profile of v1, /device:TPU:8, one launch (start us, length us, event | category | flops | bytes accessed | tf_op | source)
XLA Modules:
  0.0 76.1 jit_solution(7554296525451246724)
XLA Ops:
  0.7 0.0 copy-start
  0.7 3.6 %head.1 = (f32[416,128]{1,0:T(8,128)}, f32[96,128]{1,0:T(8,128)}, f32[8,128]{1,0:T(8,128)}) custom-call(s32[1]{0:T(128)S(6)} %copy.7.counts_hbm, s32[1,128]{1,0:T(1,128)} %blocks_hbm.1, bf16[3,256,512]{2,1,0:T(8,128)(2,1)} %bitcast.12), custom_call_target="tpu_custom_call" | custom-call | tf_op jit(solution)/shard_map/head/pallas_call | solution.py:341
  4.3 1.9 %collective-permute-start = (f32[96,128]{1,0:T(8,128)}, f32[96,128]{1,0:T(8,128)S(1)}, u32[]{:S(2)}, u32[]{:S(2)}) collective-permute-start(f32[96,128]{1,0:T(8,128)} %get-tuple-element.14.refs_0_), channel_id=1, source_target_pairs={{0,32},{32,0},{64,96},{96,64},{128,160},{160,128},{192,224},{224,1... | collective-permute-start | bytes 147464 | tf_op jit(solution)/shard_map/ppermute | solution.py:322
  6.2 10.2 %all-to-all-start = ((f32[32,13,1,128]{3,2,1,0:T(1,128)}), f32[32,13,1,128]{3,2,1,0:T(1,128)S(1)}, u32[]{:S(2)}, u32[]{:S(2)}) async-start(f32[32,13,1,128]{3,2,1,0:T(1,128)} %bitcast.15), calls=%async_computation | async-start | bytes 425984 | tf_op jit(solution)/shard_map/all_to_all | solution.py:312
  16.4 0.0 collective-permute-done.refs_1_
  16.4 0.8 %add_multiply_fusion.2.refs_2_ = f32[96,128]{1,0:T(8,128)S(1)} fusion(f32[96,128]{1,0:T(8,128)} %get-tuple-element.14.refs_0_, f32[96,128]{1,0:T(8,128)S(1)} %collective-permute-done.refs_1_), kind=kLoop, calls=%fused_computation.2 | loop fusion | flops 24576 | bytes 147456 | tf_op jit(solution)/shard_map/mul | solution.py:360
  17.2 4.3 %collective-permute-start.1 = (f32[96,128]{1,0:T(8,128)S(1)}, f32[96,128]{1,0:T(8,128)S(1)}, u32[]{:S(2)}, u32[]{:S(2)}) collective-permute-start(f32[96,128]{1,0:T(8,128)S(1)} %add_multiply_fusion.2.refs_2_), channel_id=1, source_target_pairs={{0,64},{32,96},{64,0},{96,32},{128,192},{160,224},{192,128},{224,1... | collective-permute-start | bytes 147464 | tf_op jit(solution)/shard_map/ppermute | solution.py:322
  21.5 2.0 %collective-permute-done.1.refs_3_ = f32[96,128]{1,0:T(8,128)S(1)} collective-permute-done((f32[96,128]{1,0:T(8,128)S(1)}, f32[96,128]{1,0:T(8,128)S(1)}, u32[]{:S(2)}, u32[]{:S(2)}) %collective-permute-start.1) | collective-permute-done | bytes 49184 | tf_op jit(solution)/shard_map/ppermute | solution.py:322
  23.6 6.1 %collective-permute-start.2 = (f32[96,128]{1,0:T(8,128)S(1)}, f32[96,128]{1,0:T(8,128)S(1)}, u32[]{:S(2)}, u32[]{:S(2)}) collective-permute-start(f32[96,128]{1,0:T(8,128)S(1)} %add_multiply_fusion.1.after.refs_4_), channel_id=1, source_target_pairs={{0,128},{32,160},{64,192},{96,224},{128,0},{160,32},{192,64},{224,... | collective-permute-start | bytes 147464 | tf_op jit(solution)/shard_map/ppermute | solution.py:322
  29.7 0.0 all-to-all-done
  29.7 0.0 copy-start.4
  29.7 0.7 copy-done.4
  30.4 0.9 %plane.1 = (f32[416,128]{1,0:T(8,128)S(1)}, f32[16,16,128]{2,1,0:T(8,128)}) custom-call(f32[8,128]{1,0:T(8,128)S(1)} %copy-done.4, f32[416,128]{1,0:T(8,128)S(1)} %bitcast.9, f32[96,128]{1,0:T(8,128)S(1)} %add_multiply_fusion.1.after.refs_4_), custom_call_target="tpu_custom_call" | custom-call | tf_op jit(solution)/shard_map/plane/pallas_call | solution.py:363
  31.3 9.1 %all-to-all-start.1 = ((f32[16,16,128]{2,1,0:T(8,128)}), f32[16,16,128]{2,1,0:T(8,128)S(1)}, u32[]{:S(2)}, u32[]{:S(2)}) async-start(f32[16,16,128]{2,1,0:T(8,128)} %get-tuple-element.15), calls=%async_computation.1 | async-start | bytes 262144 | tf_op jit(solution)/shard_map/all_to_all | solution.py:312
  40.4 0.1 pad_add_fusion.place
  40.5 0.0 collective-permute-done.2.refs_5_
  40.5 8.6 %all-to-all-done.1.gathered = f32[16,16,128]{2,1,0:T(8,128)S(1)} async-done(((f32[16,16,128]{2,1,0:T(8,128)}), f32[16,16,128]{2,1,0:T(8,128)S(1)}, u32[]{:S(2)}, u32[]{:S(2)}) %all-to-all-start.1) | async-done | bytes 131104 | tf_op jit(solution)/shard_map/all_to_all | solution.py:312
  49.2 1.6 %corner.1.after = f32[416,128]{1,0:T(8,128)} custom-call(s32[2]{0:T(128)S(1)} %pad_add_fusion.place, f32[16,16,128]{2,1,0:T(8,128)S(1)} %all-to-all-done.1.gathered, f32[416,128]{1,0:T(8,128)S(1)} %get-tuple-element.16.back_in, f32[96,128]{1,0:T(8,128)S(1)} %add_multiply_fusion.after.refs_6_), custom_call_target="tpu_custom_call" | custom-call | tf_op jit(solution)/shard_map/corner/pallas_call | solution.py:372
  50.8 8.9 %all-to-all-start.2 = ((f32[32,13,1,128]{3,2,1,0:T(1,128)}), f32[32,13,1,128]{3,2,1,0:T(1,128)S(1)}, u32[]{:S(2)}, u32[]{:S(2)}) async-start(f32[32,13,1,128]{3,2,1,0:T(1,128)} %bitcast.5), calls=%async_computation.2 | async-start | bytes 425984 | tf_op jit(solution)/shard_map/all_to_all | solution.py:312
  59.6 3.6 %collective-permute-start.3 = (f32[96,128]{1,0:T(8,128)S(1)}, f32[96,128]{1,0:T(8,128)S(1)}, u32[]{:S(2)}, u32[]{:S(2)}) collective-permute-start(f32[96,128]{1,0:T(8,128)S(1)} %add_multiply_fusion.after.refs_6_), channel_id=1, source_target_pairs={{0,256},{32,288},{64,320},{96,352},{128,384},{160,416},{192,448},{... | collective-permute-start | bytes 147464 | tf_op jit(solution)/shard_map/ppermute | solution.py:322
  63.2 0.0 copy-done
  63.2 0.0 copy-start.5
  63.2 1.1 %copy-done.5 = bf16[3,32,8,512]{3,2,1,0:T(8,128)(2,1)S(1)} copy-done((bf16[3,32,8,512]{3,2,1,0:T(8,128)(2,1)S(1)}, bf16[3,32,8,512]{3,2,1,0:T(8,128)(2,1)}, u32[]{:S(2)}) %copy-start.5) | copy-done | bytes 786456
  64.4 0.0 copy-start.3
  64.4 4.7 %details.1 = (f32[3,256,512]{2,1,0:T(8,128)S(1)}, bf16[3,256,512]{2,1,0:T(8,128)(2,1)S(1)}) custom-call(f32[416,128]{1,0:T(8,128)S(1)} %bitcast.10, bf16[3,256,512]{2,1,0:T(8,128)(2,1)S(1)} %bitcast.13, bf16[3,256,512]{2,1,0:T(8,128)(2,1)S(1)} %bitcast.14, f32[416,128]{1,0:T(8,128)} %corner.1.after), custom_call_target="tpu_custom_call" | custom-call | flops 2415919104 | bytes 2359296 | tf_op jit(solution)/shard_map/details/pallas_call | solution.py:381
  69.1 0.0 copy-start.1
  69.1 0.9 %copy-done.1 = bf16[3,256,512]{2,1,0:T(8,128)(2,1)} copy-done((bf16[3,256,512]{2,1,0:T(8,128)(2,1)}, bf16[3,256,512]{2,1,0:T(8,128)(2,1)S(1)}, u32[]{:S(2)}) %copy-start.1) | copy-done | bytes 786456
  70.0 0.4 collective-permute-done.3.refs_7_
  70.4 1.5 %all-to-all-done.2 = f32[32,13,1,128]{3,2,1,0:T(1,128)S(1)} async-done(((f32[32,13,1,128]{3,2,1,0:T(1,128)}), f32[32,13,1,128]{3,2,1,0:T(1,128)S(1)}, u32[]{:S(2)}, u32[]{:S(2)}) %all-to-all-start.2) | async-done | bytes 213024 | tf_op jit(solution)/shard_map/all_to_all | solution.py:312
  71.9 0.0 copy-done.3
  71.9 0.0 copy-start.2
  71.9 1.1 %copy-done.2 = bf16[3,256,512]{2,1,0:T(8,128)(2,1)S(1)} copy-done((bf16[3,256,512]{2,1,0:T(8,128)(2,1)S(1)}, bf16[3,256,512]{2,1,0:T(8,128)(2,1)}, u32[]{:S(2)}) %copy-start.2) | copy-done | bytes 786456
  73.1 3.0 %finish.1 = bf16[3,256,512]{2,1,0:T(8,128)(2,1)} custom-call(s32[2]{0:T(128)S(1)} %pad_add_fusion.place, f32[416,128]{1,0:T(8,128)S(1)} %bitcast.11, f32[16,16,128]{2,1,0:T(8,128)S(1)} %all-to-all-done.1.gathered, f32[3,256,512]{2,1,0:T(8,128)S(1)} %get-tuple-element.17.detail, bf16[3,256,512]{2,1,0:T(8,128)(2,1)S(1)} %copy-done.2, f32[96,128]{1,0:T(8,128)S(1)} %copy-done.3, ...), custom_call_target="tpu_custom_call" | custom-call | tf_op jit(solution)/shard_map/finish/pallas_call | solution.py:398
  (2 shorter events, 0.0 us)
Async XLA Ops:
  0.7 62.6 %copy-start = (bf16[3,32,8,512]{3,2,1,0:T(8,128)(2,1)S(1)}, bf16[3,32,8,512]{3,2,1,0:T(8,128)(2,1)}, u32[]{:S(2)}) copy-start(bf16[3,32,8,512]{3,2,1,0:T(8,128)(2,1)} %param.4) | copy-start | bytes 2359300
  4.3 12.1 %collective-permute-start = (f32[96,128]{1,0:T(8,128)}, f32[96,128]{1,0:T(8,128)S(1)}, u32[]{:S(2)}, u32[]{:S(2)}) collective-permute-start(f32[96,128]{1,0:T(8,128)} %get-tuple-element.14.refs_0_), channel_id=1, source_target_pairs={{0,32},{32,0},{64,96},{96,64},{128,160},{160,128},{192,224},{224,1... | collective-permute-start | bytes 147464 | tf_op jit(solution)/shard_map/ppermute | solution.py:322
  6.2 23.4 %all-to-all-start = ((f32[32,13,1,128]{3,2,1,0:T(1,128)}), f32[32,13,1,128]{3,2,1,0:T(1,128)S(1)}, u32[]{:S(2)}, u32[]{:S(2)}) async-start(f32[32,13,1,128]{3,2,1,0:T(1,128)} %bitcast.15), calls=%async_computation | async-start | bytes 425984 | tf_op jit(solution)/shard_map/all_to_all | solution.py:312
  17.2 6.3 %collective-permute-start.1 = (f32[96,128]{1,0:T(8,128)S(1)}, f32[96,128]{1,0:T(8,128)S(1)}, u32[]{:S(2)}, u32[]{:S(2)}) collective-permute-start(f32[96,128]{1,0:T(8,128)S(1)} %add_multiply_fusion.2.refs_2_), channel_id=1, source_target_pairs={{0,64},{32,96},{64,0},{96,32},{128,192},{160,224},{192,128},{224,1... | collective-permute-start | bytes 147464 | tf_op jit(solution)/shard_map/ppermute | solution.py:322
  23.6 16.9 %collective-permute-start.2 = (f32[96,128]{1,0:T(8,128)S(1)}, f32[96,128]{1,0:T(8,128)S(1)}, u32[]{:S(2)}, u32[]{:S(2)}) collective-permute-start(f32[96,128]{1,0:T(8,128)S(1)} %add_multiply_fusion.1.after.refs_4_), channel_id=1, source_target_pairs={{0,128},{32,160},{64,192},{96,224},{128,0},{160,32},{192,64},{224,... | collective-permute-start | bytes 147464 | tf_op jit(solution)/shard_map/ppermute | solution.py:322
  29.7 0.7 copy-start.4
  31.3 17.9 %all-to-all-start.1 = ((f32[16,16,128]{2,1,0:T(8,128)}), f32[16,16,128]{2,1,0:T(8,128)S(1)}, u32[]{:S(2)}, u32[]{:S(2)}) async-start(f32[16,16,128]{2,1,0:T(8,128)} %get-tuple-element.15), calls=%async_computation.1 | async-start | bytes 262144 | tf_op jit(solution)/shard_map/all_to_all | solution.py:312
  50.8 21.2 %all-to-all-start.2 = ((f32[32,13,1,128]{3,2,1,0:T(1,128)}), f32[32,13,1,128]{3,2,1,0:T(1,128)S(1)}, u32[]{:S(2)}, u32[]{:S(2)}) async-start(f32[32,13,1,128]{3,2,1,0:T(1,128)} %bitcast.5), calls=%async_computation.2 | async-start | bytes 425984 | tf_op jit(solution)/shard_map/all_to_all | solution.py:312
  59.6 10.8 %collective-permute-start.3 = (f32[96,128]{1,0:T(8,128)S(1)}, f32[96,128]{1,0:T(8,128)S(1)}, u32[]{:S(2)}, u32[]{:S(2)}) collective-permute-start(f32[96,128]{1,0:T(8,128)S(1)} %add_multiply_fusion.after.refs_6_), channel_id=1, source_target_pairs={{0,256},{32,288},{64,320},{96,352},{128,384},{160,416},{192,448},{... | collective-permute-start | bytes 147464 | tf_op jit(solution)/shard_map/ppermute | solution.py:322
  63.2 1.1 %copy-start.5 = (bf16[3,32,8,512]{3,2,1,0:T(8,128)(2,1)S(1)}, bf16[3,32,8,512]{3,2,1,0:T(8,128)(2,1)}, u32[]{:S(2)}) copy-start(bf16[3,32,8,512]{3,2,1,0:T(8,128)(2,1)} %param.5) | copy-start | bytes 2359300
  64.4 7.6 %copy-start.3 = (f32[96,128]{1,0:T(8,128)S(1)}, f32[96,128]{1,0:T(8,128)}, u32[]{:S(2)}) copy-start(f32[96,128]{1,0:T(8,128)} %get-tuple-element.14.refs_0_) | copy-start | bytes 147460
  69.1 0.9 %copy-start.1 = (bf16[3,256,512]{2,1,0:T(8,128)(2,1)}, bf16[3,256,512]{2,1,0:T(8,128)(2,1)S(1)}, u32[]{:S(2)}) copy-start(bf16[3,256,512]{2,1,0:T(8,128)(2,1)S(1)} %get-tuple-element.18.velocity) | copy-start | bytes 2359300
  71.9 1.1 %copy-start.2 = (bf16[3,256,512]{2,1,0:T(8,128)(2,1)S(1)}, bf16[3,256,512]{2,1,0:T(8,128)(2,1)}, u32[]{:S(2)}) copy-start(bf16[3,256,512]{2,1,0:T(8,128)(2,1)} %copy-done.1) | copy-start | bytes 2359300

commit v2 on v1

v2 whole, which is shorter than its diff:
```python
import jax
import jax.numpy as jnp
from jax import lax
from jax.experimental import pallas as pl
from jax.experimental.pallas import tpu as pltpu
from jax.sharding import PartitionSpec as P


BY = 8
BZ = 128
ZB = 4
CHUNKS = 12
ROWS = 13
EXTRA = 12
CORNER = 48
SLICE = 16
HALF = 64
OWN_KEPT = 48
ALL_KEPT = 64
LINE_KEPT = 52
PACKED = 16
F32 = jnp.float32
BF16 = jnp.bfloat16


def iota(shape, dimension):
    return lax.broadcasted_iota(jnp.int32, shape, dimension)


def sign_of(place, cell, length):
    span = jnp.where(place == 0, length, 2 * (place & -place))
    sign = jnp.where((cell < place) | (place == 0), 1.0, -1.0)
    return jnp.where((cell ^ place) < span, sign, 0.0)


def weight_of(place, cell, length):
    span = jnp.where(place == 0, length, 2 * (place & -place))
    return sign_of(place, cell, length) / span.astype(F32)


def mix_table(wide):
    coarse = iota((8, BZ), 1)
    parts = []
    for block in range(wide // BZ):
        row = weight_of(jnp.minimum(coarse, ZB - 1), jnp.int32(block), ZB)
        row = jnp.where(coarse < ZB, row - jnp.where(coarse == block, 1.0, 0.0), 0.0) / BZ
        parts.append(jnp.broadcast_to(row[0:1], (BZ, BZ)))
    return jnp.concatenate(parts, axis=0).astype(BF16)


def unmix_table(wide):
    block = iota((8, BZ), 1)
    parts = []
    for coarse in range(wide // BZ):
        row = sign_of(jnp.int32(coarse), jnp.minimum(block, ZB - 1), ZB)
        row = jnp.where(block < ZB, row - jnp.where(block == coarse, 1.0, 0.0), 0.0) / BZ
        parts.append(jnp.broadcast_to(row[0:1], (BZ, BZ)))
    return jnp.concatenate(parts, axis=0).astype(BF16)


def halves(value):
    high = value.astype(BF16)
    low = (value - high.astype(F32)).astype(BF16)
    return high, low


def left_product(table, value):
    high, low = halves(value)
    return jnp.dot(table, high, preferred_element_type=F32) + jnp.dot(
        table, low, preferred_element_type=F32
    )


def right_product(value, table):
    high, low = halves(value)
    return jnp.dot(high, table, preferred_element_type=F32) + jnp.dot(
        low, table, preferred_element_type=F32
    )


def remix(value, table):
    shift = right_product(value, table)
    return jnp.concatenate(
        [value[:, zb * BZ : (zb + 1) * BZ] + shift[:, zb : zb + 1] for zb in range(ZB)], axis=1
    )


def forward_levels(values):
    count = len(values)
    result = [None] * count
    step = 1
    while step < count:
        for place in range(step, count, 2 * step):
            low, high = values[place - step], values[place]
            result[place] = (low - high) * 0.5
            values[place - step] = (low + high) * 0.5
        step *= 2
    result[0] = values[0]
    return result


def inverse_levels(values):
    count = len(values)
    values = list(values)
    step = count // 2
    while step >= 1:
        for place in range(step, count, 2 * step):
            mean, detail = values[place - step], values[place]
            values[place - step] = mean + detail
            values[place] = mean - detail
        step //= 2
    return values


def pick_table(first, wide):
    lane, cell = iota((BZ, wide), 0), iota((BZ, wide), 1)
    return jnp.where(lane == (first + (cell >> 7)) & (BZ - 1), 1.0, 0.0).astype(BF16)


def head_kernel(counts_hbm, blocks_hbm, vort_hbm, send, line, own, counts, blocks, vort, sems):
    parts, cells, wide = vort.shape
    planes = cells // BY
    copies = [
        pltpu.make_async_copy(vort_hbm.at[c], vort.at[c], sems.at[c]) for c in range(parts)
    ]
    copies.append(pltpu.make_async_copy(blocks_hbm, blocks, sems.at[parts]))
    copies.append(pltpu.make_async_copy(counts_hbm, counts, sems.at[parts + 1]))
    for copy in reversed(copies):
        copy.start()
    row, column = iota((planes + BY, cells), 0), iota((planes + BY, cells), 1)
    fine = jnp.where(row - planes == column & (BY - 1), 1.0, 0.0) - 1.0 / BY
    table = jnp.where(
        row < planes,
        weight_of(jnp.minimum(row, planes - 1), column >> 3, planes) * (1.0 / BY),
        fine * (1.0 / planes),
    ).astype(BF16)
    mix = mix_table(wide)
    copies[parts].wait()
    copies[parts + 1].wait()
    nblocks = blocks.shape[1]
    square = (nblocks, nblocks)
    listed = (blocks[...] == iota(square, 0)) & (iota(square, 1) < counts[0])
    kept = lax.dot_general(
        jnp.ones((planes, nblocks), BF16),
        jnp.where(listed, 1.0, 0.0).astype(BF16),
        (((1,), (1,)), ((), ())),
        preferred_element_type=F32,
    )
    kept = jnp.minimum(kept, 1.0)
    own[...] = kept[0:8]
    target, block = iota((planes, nblocks), 0), iota((planes, nblocks), 1)
    block_row, lane = iota(square, 0), iota(square, 1)
    mine = jnp.where(block >> 2 == target, kept, 0.0).astype(BF16)
    slot = jnp.where(lane == OWN_KEPT + (block_row & 3), 1.0, 0.0).astype(BF16)
    extra = jnp.dot(mine, slot, preferred_element_type=F32)
    every = jnp.where(block & 3 == target >> 3, kept, 0.0).astype(BF16)
    slot = jnp.where(lane == ALL_KEPT + (block_row >> 2), 1.0, 0.0).astype(BF16)
    extra = extra + jnp.dot(every, slot, preferred_element_type=F32)
    lane, turn = iota((8, BZ), 1), iota((8, BZ), 0)
    extra = [
        pltpu.roll(extra[zb * 8 : (zb + 1) * 8], 0, 1, stride=SLICE, stride_axis=0)
        for zb in range(ZB)
    ]
    for c in range(parts):
        copies[c].wait()
        rows = remix(jnp.dot(table, vort[c], preferred_element_type=F32), mix)
        for zb in range(ZB):
            chunk = c * ZB + zb
            part = rows[:, zb * BZ : (zb + 1) * BZ]
            send[pl.ds(chunk, planes, stride=ROWS), :] = part[0:planes]
            line[chunk * BY : (chunk + 1) * BY, :] = part[planes : planes + BY]
            turned = jnp.broadcast_to(part[0:1], (8, BZ))
            turned = pltpu.roll(turned, c * SLICE, 1) if c else turned
            extra[zb] = jnp.where(lane >> 4 == (turn + c) & 7, turned, extra[zb])
    send[pl.ds(EXTRA, planes, stride=ROWS), :] = jnp.concatenate(extra, axis=0)


def level_tables(length):
    square = (length, length)
    forward = weight_of(iota(square, 0), iota(square, 1), length).astype(BF16)
    inverse = sign_of(iota(square, 1), iota(square, 0), length).astype(BF16)
    return forward, inverse


def plane_kernel(place, own_hbm, recv, after, back, corner, own, sems):
    del after
    planes = recv.shape[0] // ROWS
    copy = pltpu.make_async_copy(own_hbm, own, sems.at[0])
    copy.start()
    forward, inverse = level_tables(planes)
    extra = recv[pl.ds(EXTRA, planes, stride=ROWS), :]
    extra = pltpu.roll(extra, (BZ - SLICE * (place[1] & 7)) & (BZ - 1), 1)
    lane = iota((PACKED, BZ), 1)
    row = iota((PACKED, BZ), 0)
    heads = extra[0:1]
    low = jnp.sum(jnp.where(lane == ALL_KEPT + row, heads, 0.0), axis=1, keepdims=True)
    high = jnp.sum(jnp.where(lane == ALL_KEPT + PACKED + row, heads, 0.0), axis=1, keepdims=True)
    levels = left_product(forward, jnp.where(iota((planes, BZ), 1) < CORNER, extra, 0.0))
    packed = levels[0:PACKED] + pltpu.roll(levels[PACKED:planes], HALF, 1)
    packed = jnp.where(lane == CORNER, low, packed)
    packed = jnp.where(lane == HALF + CORNER, high, packed)
    shifted = pltpu.roll(jnp.broadcast_to(heads, (PACKED, BZ)), LINE_KEPT - OWN_KEPT, 1)
    packed = jnp.where((lane >= LINE_KEPT) & (lane < LINE_KEPT + ZB), shifted, packed)
    for g in range(corner.shape[0]):
        corner[g] = packed
    pick = jnp.where(iota((BZ, ZB * BZ), 0) & 3 == iota((BZ, ZB * BZ), 1) >> 7, 1.0, 0.0)
    copy.wait()
    spread = jnp.where(iota((planes, BZ), 1) >> 2 == iota((planes, BZ), 0), own[0:1], 0.0)
    mask = jnp.dot(spread.astype(BF16), pick.astype(BF16), preferred_element_type=F32)
    for c in range(3):
        data = jnp.concatenate(
            [recv[pl.ds(c * ZB + zb, planes, stride=ROWS), :] for zb in range(ZB)], axis=1
        )
        data = left_product(inverse, left_product(forward, data) * mask)
        for zb in range(ZB):
            back[pl.ds(c * ZB + zb, planes, stride=ROWS), :] = data[:, zb * BZ : (zb + 1) * BZ]


def levels_kernel(vort_hbm, mine, other, after, rows, means, vort, sems):
    del after
    parts, cells, wide = vort.shape
    planes = cells // BY
    copies = [
        pltpu.make_async_copy(vort_hbm.at[c], vort.at[c], sems.at[c]) for c in range(parts)
    ]
    for copy in copies:
        copy.start()
    means[...] = (mine[...] + other[...]) * 0.5
    row, column = iota((cells, cells), 0), iota((cells, cells), 1)
    same = jnp.where(row & (BY - 1) == column & (BY - 1), 1.0 - 1.0 / BY, -1.0 / BY)
    forward = (sign_of(row >> 3, column >> 3, planes) * same).astype(BF16)
    mix = mix_table(wide)
    for c in range(parts):
        copies[c].wait()
        rows[c] = remix(jnp.dot(forward, vort[c], preferred_element_type=F32), mix)


def corner_kernel(place, gathered, back_in, after, back):
    del after
    slabs = gathered.shape[0]
    planes = back.shape[0] // ROWS
    lane = iota((PACKED, BZ), 1)
    back[...] = back_in[...]
    values = forward_levels([gathered[g] for g in range(slabs)])
    total = jnp.zeros((PACKED, BZ), F32)
    for p in range(slabs):
        low = gathered[p, :, CORNER : CORNER + 1]
        high = gathered[p, :, HALF + CORNER : HALF + CORNER + 1]
        sign = sign_of(jnp.int32(p), place[0], slabs)
        total = total + values[p] * jnp.where(lane < HALF, low, high) * sign
    total = jnp.concatenate([total, pltpu.roll(total, HALF, 1)], axis=0)
    total = jnp.where(iota((planes, BZ), 1) < CORNER, total, 0.0)
    total = pltpu.roll(left_product(level_tables(planes)[1], total), SLICE * (place[1] & 7), 1)
    back[pl.ds(EXTRA, planes, stride=ROWS), :] = total


def line_kernel(place, gathered, after, *refs):
    del after
    pairs, (total, means, mask) = refs[:-3], refs[-3:]
    levels = len(pairs) // 2
    wanted = [gathered[0, 0:1, :]]
    for level in range(levels + 1):
        half = 1 << level
        slab = ((place[0] >> (level + 1)) << (level + 1)) + half
        wanted.append(gathered[jnp.minimum(slab, gathered.shape[0] - 1), 0:1, :])
    wanted += [jnp.zeros((1, BZ), F32)] * (8 - len(wanted))
    wanted = jnp.concatenate(wanted, axis=0).astype(BF16)
    mask[...] = jnp.dot(wanted, pick_table(LINE_KEPT, mask.shape[1]), preferred_element_type=F32)
    means[...] = (pairs[-2][...] + pairs[-1][...]) * 0.5
    for chunk in range(CHUNKS):
        span = slice(chunk * BY, (chunk + 1) * BY)
        lanes = slice(chunk % ZB * BZ, (chunk % ZB + 1) * BZ)
        result = jnp.zeros((BY, BZ), F32)
        for level in range(levels):
            mine, other = pairs[2 * level][span, :], pairs[2 * level + 1][span, :]
            result = result + (mine - other) * 0.5 * mask[level + 1 : level + 2, lanes]
        total[span, :] = result


def details_kernel(place, recv, rows, velocity_hbm, after, detail, velocity, sems):
    del after
    parts, cells, wide = rows.shape
    planes = cells // BY
    copy = pltpu.make_async_copy(velocity_hbm, velocity, sems.at[0])
    copy.start()
    row, column = iota((cells, planes), 0), iota((cells, planes), 1)
    span = jnp.maximum(2 * (column & -column), 1).astype(F32)
    tall = jnp.where((row >> 3 == column) & (column > 0), 1.0 / span, 0.0).astype(BF16)
    kept = recv[pl.ds(EXTRA, planes, stride=ROWS), :].astype(BF16)
    kept = jnp.dot(tall, kept, preferred_element_type=F32).astype(BF16)
    mask = jnp.dot(kept, pick_table(OWN_KEPT + SLICE * (place[1] & 7), wide), preferred_element_type=F32)
    row, column = iota((cells, cells), 0), iota((cells, cells), 1)
    same = row & (BY - 1) == column & (BY - 1)
    inverse = jnp.where(same, sign_of(column >> 3, row >> 3, planes), 0.0).astype(BF16)
    unmix = unmix_table(wide)
    for c in range(parts):
        detail[c] = remix(left_product(inverse, rows[c] * mask), unmix)
    copy.wait()


def finish_kernel(got, mine, other, partial, mask, detail, velocity, out, rows):
    planes = got.shape[0] // ROWS
    parts, cells, wide = velocity.shape
    inverse = level_tables(planes)[1]
    extra = got[pl.ds(EXTRA, planes, stride=ROWS), :]
    slot, lane = iota((8, BZ), 0), iota((8, BZ), 1)
    for c in range(parts):
        columns = []
        for zb in range(ZB):
            span = slice((c * ZB + zb) * BY, (c * ZB + zb + 1) * BY)
            lanes = slice(zb * BZ, (zb + 1) * BZ)
            last = (mine[span, :] - other[span, :]) * 0.5
            mean = (mine[span, :] + other[span, :]) * 0.5
            total = partial[span, :] + last * mask[4:5, lanes] + mean * mask[0:1, lanes]
            rows[parts * planes + c * BY : parts * planes + (c + 1) * BY, lanes] = total
            corner = extra[zb * 8 : (zb + 1) * 8]
            corner = jnp.where(lane >> 4 == (slot + c) & 7, corner, 0.0)
            corner = jnp.sum(corner, axis=0, keepdims=True)
            corner = pltpu.roll(corner, BZ - c * SLICE, 1) if c else corner
            data = got[pl.ds(c * ZB + zb, planes, stride=ROWS), :]
            columns.append(jnp.where(iota((planes, BZ), 0) == 0, corner, data))
        rows[c * planes : (c + 1) * planes, :] = left_product(
            inverse, jnp.concatenate(columns, axis=1)
        )
    rows[...] = remix(rows[...], unmix_table(wide))
    for x in range(planes):
        span = slice(x * BY, (x + 1) * BY)
        smooth = [
            detail[c, span, :]
            + rows[c * planes + x : c * planes + x + 1, :]
            + rows[parts * planes + c * BY : parts * planes + (c + 1) * BY, :]
            for c in range(parts)
        ]
        speed = [velocity[c, span, :].astype(F32) for c in range(parts)]
        for c in range(parts):
            a, b = (c + 1) % parts, (c + 2) % parts
            out[c, span, :] = (smooth[a] * speed[b] - smooth[b] * speed[a]).astype(BF16)


def exchange(value, axis):
    return lax.all_to_all(value, axis, split_axis=0, concat_axis=0, tiled=True)


def over_yz(rows, planes):
    moved = exchange(rows.reshape(planes, ROWS, 1, BZ), "yz")
    return moved.reshape(planes * ROWS, BZ)


def from_partner(value, distance):
    if distance >= lax.axis_size("gx"):
        return value
    pairs = [(source, source ^ distance) for source in range(lax.axis_size("gx"))]
    return lax.ppermute(value, "gx", pairs)


def body(vorticity, velocity, blocks, counts):
    parts, planes, tall, wide = vorticity.shape
    cells = planes * tall
    slabs = lax.axis_size("gx")
    smem = pl.BlockSpec(memory_space=pltpu.SMEM)
    vmem = pl.BlockSpec(memory_space=pltpu.VMEM)
    loose = pl.BlockSpec(memory_space=pl.ANY)
    params = pltpu.CompilerParams(vmem_limit_bytes=32 * 1024 * 1024)
    place = jnp.stack([lax.axis_index("gx"), lax.axis_index("yz")]).astype(jnp.int32)
    vort = vorticity.reshape(parts, cells, wide)
    line_shape = (CHUNKS * BY, BZ)

    def array(*shape):
        return jax.ShapeDtypeStruct(shape, F32)

    def call(kernel, name, out_shape, in_specs, scratch=(), cost=None, params=params):
        many = isinstance(out_shape, tuple)
        return pl.pallas_call(
            kernel,
            out_shape=out_shape,
            in_specs=in_specs,
            out_specs=tuple(vmem for _ in out_shape) if many else vmem,
            scratch_shapes=list(scratch),
            compiler_params=params,
            cost_estimate=cost,
            name=name,
        )

    def cost(products):
        return pl.CostEstimate(
            flops=products * 2 * parts * cells * cells * wide,
            bytes_accessed=10 * parts * cells * wide,
            transcendentals=0,
        )

    vort_scratch = pltpu.VMEM((parts, cells, wide), BF16)
    send, line, own = call(
        head_kernel,
        "head",
        (array(planes * ROWS, BZ), array(*line_shape), array(8, BZ)),
        [loose] * 3,
        [
            pltpu.SMEM(counts.shape, jnp.int32),
            pltpu.VMEM(blocks.shape, jnp.int32),
            vort_scratch,
            pltpu.SemaphoreType.DMA((parts + 2,)),
        ],
        params=pltpu.CompilerParams(vmem_limit_bytes=60 * 1024 * 1024),
    )(counts, blocks, vort)
    recv = over_yz(send, planes)
    pairs = [line, from_partner(line, 1)]
    line = (pairs[0] + pairs[1]) * 0.5
    pairs += [line, from_partner(line, 2)]
    back, corner = call(
        plane_kernel,
        "plane",
        (array(planes * ROWS, BZ), array(slabs, PACKED, BZ)),
        [smem, loose, vmem, loose],
        [pltpu.VMEM((8, BZ), F32), pltpu.SemaphoreType.DMA((1,))],
    )(place, own, recv, pairs[3])
    gathered = exchange(corner, "gx")
    rows, line = call(
        levels_kernel,
        "levels",
        (array(parts, cells, wide), array(*line_shape)),
        [loose, vmem, vmem, loose],
        [vort_scratch, pltpu.SemaphoreType.DMA((parts,))],
        cost(3),
    )(vort, pairs[2], pairs[3], corner)
    pairs += [line, from_partner(line, 4)]
    back = call(
        corner_kernel, "corner", array(planes * ROWS, BZ), [smem, vmem, vmem, loose]
    )(place, gathered, back, line)
    got = over_yz(back, planes)
    partial, line, mask = call(
        line_kernel,
        "line",
        (array(*line_shape), array(*line_shape), array(8, wide)),
        [smem, vmem, loose] + [vmem] * 6,
    )(place, gathered, back, *pairs)
    other = from_partner(line, 8)
    detail, speed = call(
        details_kernel,
        "details",
        (array(parts, cells, wide), jax.ShapeDtypeStruct((parts, cells, wide), BF16)),
        [smem, vmem, vmem, loose, loose],
        [pltpu.SemaphoreType.DMA((1,))],
        cost(4),
    )(place, recv, rows, velocity.reshape(parts, cells, wide), line)
    out = call(
        finish_kernel,
        "finish",
        jax.ShapeDtypeStruct((parts, cells, wide), BF16),
        [vmem] * 7,
        [pltpu.VMEM((parts * (planes + tall), wide), F32)],
    )(got, line, other, partial, mask, detail, speed)
    return out.reshape(parts, planes, tall, wide)


def solution(mesh):
    return jax.shard_map(
        body,
        mesh=mesh,
        in_specs=(
            P(None, "gx", "yz", None),
            P(None, "gx", "yz", None),
            P(("gx", "yz"), None),
            P(("gx", "yz")),
        ),
        out_specs=P(None, "gx", "yz", None),
        check_vma=False,
    )
```

time: 76.7 us -> 78.4 us (1.022)
  the two profiles are of different devices: /device:TPU:8 before, /device:TPU:2 now
where the time goes in v2:
time: 78.4 us; the launch traced here: 77.8 us
  starting transfers between devices  41.9 us (53%)
  waiting for transfers between devices  16.3 us (21%)
  Pallas kernels  13.5 us (17%)
  local copies, waits for them, and re-layouts  4.39 us (6%)
  other arithmetic  0.88 us (1%)
  between operations  0.86 us (1%)
    all_to_all x3, starting transfers between devices, exchange(): return lax.all_to_all(value, axis, split_axis=0, concat_axis=0, tiled=True)  30.1 us
    ppermute x4, starting transfers between devices, from_partner(): return lax.ppermute(value, 'gx', pairs)  11.8 us
    ppermute x4, waiting for transfers between devices, from_partner(): return lax.ppermute(value, 'gx', pairs)  10.9 us
    all_to_all x3, waiting for transfers between devices, exchange(): return lax.all_to_all(value, axis, split_axis=0, concat_axis=0, tiled=True)  5.42 us
    unnamed x12, local copies, waits for them, and re-layouts  4.39 us
    pallas_call x1, Pallas kernels, body(): call(head_kernel, 'head', (array(planes * ROWS, BZ), array(*line_shape),...  3.13 us
    pallas_call x1, Pallas kernels, body(): call(details_kernel, 'details', (array(parts, cells, wide), jax.ShapeDtyp...  2.32 us
    pallas_call x1, Pallas kernels, body(): call(levels_kernel, 'levels', (array(parts, cells, wide), array(*line_sha...  2.13 us
  transfers between devices with their start and end apart: 7, of which 5 were waited for; matrix products, arithmetic and copies ran while one was open for 1% of the time, Pallas kernels for 7%

profile of v2, /device:TPU:2, one launch (start us, length us, event | category | flops | bytes accessed | tf_op | source)
XLA Modules:
  0.0 77.8 jit_solution(2446180632169566789)
XLA Ops:
  0.0 0.0 copy-start
  0.7 3.1 %head.1 = (f32[416,128]{1,0:T(8,128)}, f32[96,128]{1,0:T(8,128)}, f32[8,128]{1,0:T(8,128)}) custom-call(s32[1]{0:T(128)S(6)} %copy.7.counts_hbm, s32[1,128]{1,0:T(1,128)} %blocks_hbm.1, bf16[3,256,512]{2,1,0:T(8,128)(2,1)} %bitcast.12), custom_call_target="tpu_custom_call" | custom-call | tf_op jit(solution)/shard_map/head/pallas_call | solution.py:392
  3.9 10.3 %all-to-all-start = ((f32[32,13,1,128]{3,2,1,0:T(1,128)}), f32[32,13,1,128]{3,2,1,0:T(1,128)S(1)}, u32[]{:S(2)}, u32[]{:S(2)}) async-start(f32[32,13,1,128]{3,2,1,0:T(1,128)} %bitcast.15), calls=%async_computation | async-start | bytes 425984 | tf_op jit(solution)/shard_map/all_to_all | solution.py:341
  14.1 1.9 %collective-permute-start = (f32[96,128]{1,0:T(8,128)}, f32[96,128]{1,0:T(8,128)S(1)}, u32[]{:S(2)}, u32[]{:S(2)}) collective-permute-start(f32[96,128]{1,0:T(8,128)} %get-tuple-element.19.refs_0_), channel_id=1, source_target_pairs={{0,32},{32,0},{64,96},{96,64},{128,160},{160,128},{192,224},{224,1... | collective-permute-start | bytes 147464 | tf_op jit(solution)/shard_map/ppermute | solution.py:353
  16.1 1.4 %collective-permute-done.refs_1_ = f32[96,128]{1,0:T(8,128)S(1)} collective-permute-done((f32[96,128]{1,0:T(8,128)}, f32[96,128]{1,0:T(8,128)S(1)}, u32[]{:S(2)}, u32[]{:S(2)}) %collective-permute-start) | collective-permute-done | bytes 49184 | tf_op jit(solution)/shard_map/ppermute | solution.py:353
  17.5 0.8 %add_multiply_fusion.mine.refs_2_ = f32[96,128]{1,0:T(8,128)S(1)} fusion(f32[96,128]{1,0:T(8,128)} %get-tuple-element.19.refs_0_, f32[96,128]{1,0:T(8,128)S(1)} %collective-permute-done.refs_1_), kind=kLoop, calls=%fused_computation | loop fusion | flops 24576 | bytes 147456 | tf_op jit(solution)/shard_map/mul | solution.py:407
  18.3 4.3 %collective-permute-start.1 = (f32[96,128]{1,0:T(8,128)S(1)}, f32[96,128]{1,0:T(8,128)S(1)}, u32[]{:S(2)}, u32[]{:S(2)}) collective-permute-start(f32[96,128]{1,0:T(8,128)S(1)} %add_multiply_fusion.mine.refs_2_), channel_id=1, source_target_pairs={{0,64},{32,96},{64,0},{96,32},{128,192},{160,224},{192,128},{224,1... | collective-permute-start | bytes 147464 | tf_op jit(solution)/shard_map/ppermute | solution.py:353
  22.6 0.1 pad_add_fusion.place
  22.6 2.0 %collective-permute-done.1.after.other.refs_3_ = f32[96,128]{1,0:T(8,128)S(1)} collective-permute-done((f32[96,128]{1,0:T(8,128)S(1)}, f32[96,128]{1,0:T(8,128)S(1)}, u32[]{:S(2)}, u32[]{:S(2)}) %collective-permute-start.1) | collective-permute-done | bytes 49184 | tf_op jit(solution)/shard_map/ppermute | solution.py:353
  24.6 0.0 all-to-all-done
  24.6 0.0 copy-start.2
  24.6 0.7 copy-done.2
  25.3 1.5 %plane.1 = (f32[416,128]{1,0:T(8,128)S(1)}, f32[16,16,128]{2,1,0:T(8,128)}) custom-call(s32[2]{0:T(128)S(1)} %pad_add_fusion.place, f32[8,128]{1,0:T(8,128)S(1)} %copy-done.2, f32[416,128]{1,0:T(8,128)S(1)} %bitcast.10, f32[96,128]{1,0:T(8,128)S(1)} %collective-permute-done.1.after.other.refs_3_), custom_call_target="tpu_custom_call" | custom-call | tf_op jit(solution)/shard_map/plane/pallas_call | solution.py:409
  26.8 10.3 %all-to-all-start.1 = ((f32[16,16,128]{2,1,0:T(8,128)}), f32[16,16,128]{2,1,0:T(8,128)S(1)}, u32[]{:S(2)}, u32[]{:S(2)}) async-start(f32[16,16,128]{2,1,0:T(8,128)} %get-tuple-element.20.after), calls=%async_computation.1 | async-start | bytes 262144 | tf_op jit(solution)/shard_map/all_to_all | solution.py:341
  37.1 0.0 copy-done
  37.1 0.0 copy-start.1
  37.2 2.1 %levels.1 = (f32[3,256,512]{2,1,0:T(8,128)S(1)}, f32[96,128]{1,0:T(8,128)S(1)}) custom-call(bf16[3,256,512]{2,1,0:T(8,128)(2,1)S(1)} %bitcast.13, f32[96,128]{1,0:T(8,128)S(1)} %add_multiply_fusion.mine.refs_2_, f32[96,128]{1,0:T(8,128)S(1)} %collective-permute-done.1.after.other.refs_3_, f32[16,16,128]{2,1,0:T(8,128)} %get-tuple-element.20.after), custom_call_target="tpu_custom_call" | custom-call | flops 603979776 | bytes 3932160 | tf_op jit(solution)/shard_map/levels/pallas_call | solution.py:417
  39.3 0.0 copy-start.4
  39.3 1.2 %copy-done.4 = f32[3,256,512]{2,1,0:T(8,128)} copy-done((f32[3,256,512]{2,1,0:T(8,128)}, f32[3,256,512]{2,1,0:T(8,128)S(1)}, u32[]{:S(2)}) %copy-start.4) | copy-done | bytes 1572888
  40.5 5.4 %all-to-all-done.1.gathered = f32[16,16,128]{2,1,0:T(8,128)S(1)} async-done(((f32[16,16,128]{2,1,0:T(8,128)}), f32[16,16,128]{2,1,0:T(8,128)S(1)}, u32[]{:S(2)}, u32[]{:S(2)}) %all-to-all-start.1) | async-done | bytes 131104 | tf_op jit(solution)/shard_map/all_to_all | solution.py:341
  45.9 1.6 %corner.1.after = f32[416,128]{1,0:T(8,128)} custom-call(s32[2]{0:T(128)S(1)} %pad_add_fusion.place, f32[16,16,128]{2,1,0:T(8,128)S(1)} %all-to-all-done.1.gathered, f32[416,128]{1,0:T(8,128)S(1)} %get-tuple-element.21.back_in, f32[96,128]{1,0:T(8,128)S(1)} %get-tuple-element.22.after.refs_4_), custom_call_target="tpu_custom_call" | custom-call | tf_op jit(solution)/shard_map/corner/pallas_call | solution.py:426
  47.5 9.5 %all-to-all-start.2 = ((f32[32,13,1,128]{3,2,1,0:T(1,128)}), f32[32,13,1,128]{3,2,1,0:T(1,128)S(1)}, u32[]{:S(2)}, u32[]{:S(2)}) async-start(f32[32,13,1,128]{3,2,1,0:T(1,128)} %bitcast.5), calls=%async_computation.2 | async-start | bytes 425984 | tf_op jit(solution)/shard_map/all_to_all | solution.py:341
  57.1 2.7 %collective-permute-start.2 = (f32[96,128]{1,0:T(8,128)S(1)}, f32[96,128]{1,0:T(8,128)S(1)}, u32[]{:S(2)}, u32[]{:S(2)}) collective-permute-start(f32[96,128]{1,0:T(8,128)S(1)} %get-tuple-element.22.after.refs_4_), channel_id=1, source_target_pairs={{0,128},{32,160},{64,192},{96,224},{128,0},{160,32},{192,64},{224,... | collective-permute-start | bytes 147464 | tf_op jit(solution)/shard_map/ppermute | solution.py:353
  59.8 4.9 %collective-permute-done.2.refs_5_ = f32[96,128]{1,0:T(8,128)S(1)} collective-permute-done((f32[96,128]{1,0:T(8,128)S(1)}, f32[96,128]{1,0:T(8,128)S(1)}, u32[]{:S(2)}, u32[]{:S(2)}) %collective-permute-start.2) | collective-permute-done | bytes 49184 | tf_op jit(solution)/shard_map/ppermute | solution.py:353
  64.6 0.0 copy-done.1
  64.6 0.7 line.1
  65.3 2.9 %collective-permute-start.3 = (f32[96,128]{1,0:T(8,128)S(1)}, f32[96,128]{1,0:T(8,128)S(1)}, u32[]{:S(2)}, u32[]{:S(2)}) collective-permute-start(f32[96,128]{1,0:T(8,128)S(1)} %get-tuple-element.23.after.mine), channel_id=1, source_target_pairs={{0,256},{32,288},{64,320},{96,352},{128,384},{160,416},{192,448},{... | collective-permute-start | bytes 147464 | tf_op jit(solution)/shard_map/ppermute | solution.py:353
  68.2 0.0 copy-start.3
  68.2 1.1 %copy-done.3 = bf16[3,32,8,512]{3,2,1,0:T(8,128)(2,1)S(1)} copy-done((bf16[3,32,8,512]{3,2,1,0:T(8,128)(2,1)S(1)}, bf16[3,32,8,512]{3,2,1,0:T(8,128)(2,1)}, u32[]{:S(2)}) %copy-start.3) | copy-done | bytes 786456
  69.4 0.0 copy-start.5
  69.4 1.4 %copy-done.5 = f32[3,256,512]{2,1,0:T(8,128)S(1)} copy-done((f32[3,256,512]{2,1,0:T(8,128)S(1)}, f32[3,256,512]{2,1,0:T(8,128)}, u32[]{:S(2)}) %copy-start.5) | copy-done | bytes 1572888
  70.8 2.3 %details.1 = (f32[3,256,512]{2,1,0:T(8,128)S(1)}, bf16[3,256,512]{2,1,0:T(8,128)(2,1)S(1)}) custom-call(s32[2]{0:T(128)S(1)} %pad_add_fusion.place, f32[416,128]{1,0:T(8,128)S(1)} %bitcast.11, f32[3,256,512]{2,1,0:T(8,128)S(1)} %copy-done.5, bf16[3,256,512]{2,1,0:T(8,128)(2,1)S(1)} %bitcast.14, f32[96,128]{1,0:T(8,128)S(1)} %get-tuple-element.23.after.mine), custom_call_target="tpu_custom_call" | custom-call | flops 805306368 | bytes 3932160 | tf_op jit(solution)/shard_map/details/pallas_call | solution.py:437
  73.1 2.6 %collective-permute-done.3.other = f32[96,128]{1,0:T(8,128)S(1)} collective-permute-done((f32[96,128]{1,0:T(8,128)S(1)}, f32[96,128]{1,0:T(8,128)S(1)}, u32[]{:S(2)}, u32[]{:S(2)}) %collective-permute-start.3) | collective-permute-done | bytes 49184 | tf_op jit(solution)/shard_map/ppermute | solution.py:353
  75.7 0.0 all-to-all-done.2
  75.7 2.1 %finish.1 = bf16[3,256,512]{2,1,0:T(8,128)(2,1)} custom-call(f32[416,128]{1,0:T(8,128)S(1)} %bitcast.9, f32[96,128]{1,0:T(8,128)S(1)} %get-tuple-element.23.after.mine, f32[96,128]{1,0:T(8,128)S(1)} %collective-permute-done.3.other, f32[96,128]{1,0:T(8,128)S(1)} %get-tuple-element.24.partial, f32[8,512]{1,0:T(8,128)S(1)} %get-tuple-element.25.mask, ...), custom_call_target="tpu_custom_call" | custom-call | tf_op jit(solution)/shard_map/finish/pallas_call | solution.py:445
Async XLA Ops:
  0.0 37.1 %copy-start = (bf16[3,32,8,512]{3,2,1,0:T(8,128)(2,1)S(1)}, bf16[3,32,8,512]{3,2,1,0:T(8,128)(2,1)}, u32[]{:S(2)}) copy-start(bf16[3,32,8,512]{3,2,1,0:T(8,128)(2,1)} %param.4) | copy-start | bytes 2359300
  3.9 20.7 %all-to-all-start = ((f32[32,13,1,128]{3,2,1,0:T(1,128)}), f32[32,13,1,128]{3,2,1,0:T(1,128)S(1)}, u32[]{:S(2)}, u32[]{:S(2)}) async-start(f32[32,13,1,128]{3,2,1,0:T(1,128)} %bitcast.15), calls=%async_computation | async-start | bytes 425984 | tf_op jit(solution)/shard_map/all_to_all | solution.py:341
  14.1 3.3 %collective-permute-start = (f32[96,128]{1,0:T(8,128)}, f32[96,128]{1,0:T(8,128)S(1)}, u32[]{:S(2)}, u32[]{:S(2)}) collective-permute-start(f32[96,128]{1,0:T(8,128)} %get-tuple-element.19.refs_0_), channel_id=1, source_target_pairs={{0,32},{32,0},{64,96},{96,64},{128,160},{160,128},{192,224},{224,1... | collective-permute-start | bytes 147464 | tf_op jit(solution)/shard_map/ppermute | solution.py:353
  18.3 6.3 %collective-permute-start.1 = (f32[96,128]{1,0:T(8,128)S(1)}, f32[96,128]{1,0:T(8,128)S(1)}, u32[]{:S(2)}, u32[]{:S(2)}) collective-permute-start(f32[96,128]{1,0:T(8,128)S(1)} %add_multiply_fusion.mine.refs_2_), channel_id=1, source_target_pairs={{0,64},{32,96},{64,0},{96,32},{128,192},{160,224},{192,128},{224,1... | collective-permute-start | bytes 147464 | tf_op jit(solution)/shard_map/ppermute | solution.py:353
  24.6 0.7 copy-start.2
  26.8 19.1 %all-to-all-start.1 = ((f32[16,16,128]{2,1,0:T(8,128)}), f32[16,16,128]{2,1,0:T(8,128)S(1)}, u32[]{:S(2)}, u32[]{:S(2)}) async-start(f32[16,16,128]{2,1,0:T(8,128)} %get-tuple-element.20.after), calls=%async_computation.1 | async-start | bytes 262144 | tf_op jit(solution)/shard_map/all_to_all | solution.py:341
  37.1 27.5 %copy-start.1 = (f32[96,128]{1,0:T(8,128)S(1)}, f32[96,128]{1,0:T(8,128)}, u32[]{:S(2)}) copy-start(f32[96,128]{1,0:T(8,128)} %get-tuple-element.19.refs_0_) | copy-start | bytes 147460
  39.3 1.2 %copy-start.4 = (f32[3,256,512]{2,1,0:T(8,128)}, f32[3,256,512]{2,1,0:T(8,128)S(1)}, u32[]{:S(2)}) copy-start(f32[3,256,512]{2,1,0:T(8,128)S(1)} %get-tuple-element.26.rows) | copy-start | bytes 4718596
  47.5 28.2 %all-to-all-start.2 = ((f32[32,13,1,128]{3,2,1,0:T(1,128)}), f32[32,13,1,128]{3,2,1,0:T(1,128)S(1)}, u32[]{:S(2)}, u32[]{:S(2)}) async-start(f32[32,13,1,128]{3,2,1,0:T(1,128)} %bitcast.5), calls=%async_computation.2 | async-start | bytes 425984 | tf_op jit(solution)/shard_map/all_to_all | solution.py:341
  57.1 7.6 %collective-permute-start.2 = (f32[96,128]{1,0:T(8,128)S(1)}, f32[96,128]{1,0:T(8,128)S(1)}, u32[]{:S(2)}, u32[]{:S(2)}) collective-permute-start(f32[96,128]{1,0:T(8,128)S(1)} %get-tuple-element.22.after.refs_4_), channel_id=1, source_target_pairs={{0,128},{32,160},{64,192},{96,224},{128,0},{160,32},{192,64},{224,... | collective-permute-start | bytes 147464 | tf_op jit(solution)/shard_map/ppermute | solution.py:353
  65.3 10.4 %collective-permute-start.3 = (f32[96,128]{1,0:T(8,128)S(1)}, f32[96,128]{1,0:T(8,128)S(1)}, u32[]{:S(2)}, u32[]{:S(2)}) collective-permute-start(f32[96,128]{1,0:T(8,128)S(1)} %get-tuple-element.23.after.mine), channel_id=1, source_target_pairs={{0,256},{32,288},{64,320},{96,352},{128,384},{160,416},{192,448},{... | collective-permute-start | bytes 147464 | tf_op jit(solution)/shard_map/ppermute | solution.py:353
  68.2 1.1 %copy-start.3 = (bf16[3,32,8,512]{3,2,1,0:T(8,128)(2,1)S(1)}, bf16[3,32,8,512]{3,2,1,0:T(8,128)(2,1)}, u32[]{:S(2)}) copy-start(bf16[3,32,8,512]{3,2,1,0:T(8,128)(2,1)} %param.5) | copy-start | bytes 2359300
  69.4 1.4 %copy-start.5 = (f32[3,256,512]{2,1,0:T(8,128)S(1)}, f32[3,256,512]{2,1,0:T(8,128)}, u32[]{:S(2)}) copy-start(f32[3,256,512]{2,1,0:T(8,128)} %copy-done.4) | copy-start | bytes 4718596

commit v3 on v2

--- a/solution.py
+++ b/solution.py
@@ -10,13 +10,12 @@
 BZ = 128
 ZB = 4
 CHUNKS = 12
-ROWS = 13
+ROWS = 14
 EXTRA = 12
+KEPT = 13
 CORNER = 48
 SLICE = 16
 HALF = 64
-OWN_KEPT = 48
-ALL_KEPT = 64
 LINE_KEPT = 52
 PACKED = 16
 F32 = jnp.float32
@@ -117,7 +116,7 @@
     return jnp.where(lane == (first + (cell >> 7)) & (BZ - 1), 1.0, 0.0).astype(BF16)
 
 
-def head_kernel(counts_hbm, blocks_hbm, vort_hbm, send, line, own, counts, blocks, vort, sems):
+def head_kernel(counts_hbm, blocks_hbm, vort_hbm, send, line, counts, blocks, vort, sems):
     parts, cells, wide = vort.shape
     planes = cells // BY
     copies = [
@@ -146,21 +145,9 @@
         (((1,), (1,)), ((), ())),
         preferred_element_type=F32,
     )
-    kept = jnp.minimum(kept, 1.0)
-    own[...] = kept[0:8]
-    target, block = iota((planes, nblocks), 0), iota((planes, nblocks), 1)
-    block_row, lane = iota(square, 0), iota(square, 1)
-    mine = jnp.where(block >> 2 == target, kept, 0.0).astype(BF16)
-    slot = jnp.where(lane == OWN_KEPT + (block_row & 3), 1.0, 0.0).astype(BF16)
-    extra = jnp.dot(mine, slot, preferred_element_type=F32)
-    every = jnp.where(block & 3 == target >> 3, kept, 0.0).astype(BF16)
-    slot = jnp.where(lane == ALL_KEPT + (block_row >> 2), 1.0, 0.0).astype(BF16)
-    extra = extra + jnp.dot(every, slot, preferred_element_type=F32)
+    send[pl.ds(KEPT, planes, stride=ROWS), :] = jnp.minimum(kept, 1.0)
     lane, turn = iota((8, BZ), 1), iota((8, BZ), 0)
-    extra = [
-        pltpu.roll(extra[zb * 8 : (zb + 1) * 8], 0, 1, stride=SLICE, stride_axis=0)
-        for zb in range(ZB)
-    ]
+    extra = [jnp.zeros((8, BZ), F32) for zb in range(ZB)]
     for c in range(parts):
         copies[c].wait()
         rows = remix(jnp.dot(table, vort[c], preferred_element_type=F32), mix)
@@ -182,30 +169,29 @@
     return forward, inverse
 
 
-def plane_kernel(place, own_hbm, recv, after, back, corner, own, sems):
+def plane_kernel(place, recv, after, back, corner):
     del after
     planes = recv.shape[0] // ROWS
-    copy = pltpu.make_async_copy(own_hbm, own, sems.at[0])
-    copy.start()
     forward, inverse = level_tables(planes)
     extra = recv[pl.ds(EXTRA, planes, stride=ROWS), :]
     extra = pltpu.roll(extra, (BZ - SLICE * (place[1] & 7)) & (BZ - 1), 1)
     lane = iota((PACKED, BZ), 1)
     row = iota((PACKED, BZ), 0)
-    heads = extra[0:1]
-    low = jnp.sum(jnp.where(lane == ALL_KEPT + row, heads, 0.0), axis=1, keepdims=True)
-    high = jnp.sum(jnp.where(lane == ALL_KEPT + PACKED + row, heads, 0.0), axis=1, keepdims=True)
+    heads = recv[KEPT : KEPT + 1, :]
+    first = 4 * row + (place[1] >> 3)
+    low = jnp.sum(jnp.where(lane == first, heads, 0.0), axis=1, keepdims=True)
+    high = jnp.sum(jnp.where(lane == first + HALF, heads, 0.0), axis=1, keepdims=True)
     levels = left_product(forward, jnp.where(iota((planes, BZ), 1) < CORNER, extra, 0.0))
     packed = levels[0:PACKED] + pltpu.roll(levels[PACKED:planes], HALF, 1)
     packed = jnp.where(lane == CORNER, low, packed)
     packed = jnp.where(lane == HALF + CORNER, high, packed)
-    shifted = pltpu.roll(jnp.broadcast_to(heads, (PACKED, BZ)), LINE_KEPT - OWN_KEPT, 1)
+    shifted = pltpu.roll(jnp.broadcast_to(heads, (PACKED, BZ)), (LINE_KEPT - ZB * place[1]) & (BZ - 1), 1)
     packed = jnp.where((lane >= LINE_KEPT) & (lane < LINE_KEPT + ZB), shifted, packed)
     for g in range(corner.shape[0]):
         corner[g] = packed
     pick = jnp.where(iota((BZ, ZB * BZ), 0) & 3 == iota((BZ, ZB * BZ), 1) >> 7, 1.0, 0.0)
-    copy.wait()
-    spread = jnp.where(iota((planes, BZ), 1) >> 2 == iota((planes, BZ), 0), own[0:1], 0.0)
+    own = recv[pl.ds(place[1] * ROWS + KEPT, 1), :]
+    spread = jnp.where(iota((planes, BZ), 1) >> 2 == iota((planes, BZ), 0), own, 0.0)
     mask = jnp.dot(spread.astype(BF16), pick.astype(BF16), preferred_element_type=F32)
     for c in range(3):
         data = jnp.concatenate(
@@ -216,27 +202,38 @@
             back[pl.ds(c * ZB + zb, planes, stride=ROWS), :] = data[:, zb * BZ : (zb + 1) * BZ]
 
 
-def levels_kernel(vort_hbm, mine, other, after, rows, means, vort, sems):
+def details_kernel(place, recv, vort_hbm, velocity_hbm, after, detail, velocity, vort, sems):
     del after
     parts, cells, wide = vort.shape
     planes = cells // BY
     copies = [
         pltpu.make_async_copy(vort_hbm.at[c], vort.at[c], sems.at[c]) for c in range(parts)
     ]
+    copies.append(pltpu.make_async_copy(velocity_hbm, velocity, sems.at[parts]))
     for copy in copies:
         copy.start()
-    means[...] = (mine[...] + other[...]) * 0.5
+    row, column = iota((cells, planes), 0), iota((cells, planes), 1)
+    span = jnp.maximum(2 * (column & -column), 1).astype(F32)
+    tall = jnp.where((row >> 3 == column) & (column > 0), 1.0 / span, 0.0).astype(BF16)
+    kept = recv[pl.ds(KEPT, planes, stride=ROWS), :].astype(BF16)
+    kept = jnp.dot(tall, kept, preferred_element_type=F32).astype(BF16)
+    mask = jnp.dot(kept, pick_table(ZB * place[1], wide), preferred_element_type=F32)
     row, column = iota((cells, cells), 0), iota((cells, cells), 1)
-    same = jnp.where(row & (BY - 1) == column & (BY - 1), 1.0 - 1.0 / BY, -1.0 / BY)
-    forward = (sign_of(row >> 3, column >> 3, planes) * same).astype(BF16)
-    mix = mix_table(wide)
+    same = row & (BY - 1) == column & (BY - 1)
+    sign = sign_of(row >> 3, column >> 3, planes)
+    forward = (sign * jnp.where(same, 1.0 - 1.0 / BY, -1.0 / BY)).astype(BF16)
+    sign = sign_of(column >> 3, row >> 3, planes)
+    inverse = jnp.where(same, sign, 0.0).astype(BF16)
+    mix, unmix = mix_table(wide), unmix_table(wide)
     for c in range(parts):
         copies[c].wait()
-        rows[c] = remix(jnp.dot(forward, vort[c], preferred_element_type=F32), mix)
-
-
-def corner_kernel(place, gathered, back_in, after, back):
-    del after
+        rows = remix(jnp.dot(forward, vort[c], preferred_element_type=F32), mix)
+        detail[c] = remix(left_product(inverse, rows * mask), unmix)
+    copies[parts].wait()
+
+
+def corner_kernel(place, gathered, back_in, mine, other, back, means):
+    means[...] = (mine[...] + other[...]) * 0.5
     slabs = gathered.shape[0]
     planes = back.shape[0] // ROWS
     lane = iota((PACKED, BZ), 1)
@@ -254,48 +251,23 @@
     back[pl.ds(EXTRA, planes, stride=ROWS), :] = total
 
 
-def line_kernel(place, gathered, after, *refs):
+def line_kernel(place, gathered, after, mine, one, two, three, half, other, total, mask):
     del after
-    pairs, (total, means, mask) = refs[:-3], refs[-3:]
-    levels = len(pairs) // 2
     wanted = [gathered[0, 0:1, :]]
-    for level in range(levels + 1):
-        half = 1 << level
-        slab = ((place[0] >> (level + 1)) << (level + 1)) + half
+    for level in range(4):
+        slab = ((place[0] >> (level + 1)) << (level + 1)) + (1 << level)
         wanted.append(gathered[jnp.minimum(slab, gathered.shape[0] - 1), 0:1, :])
     wanted += [jnp.zeros((1, BZ), F32)] * (8 - len(wanted))
     wanted = jnp.concatenate(wanted, axis=0).astype(BF16)
     mask[...] = jnp.dot(wanted, pick_table(LINE_KEPT, mask.shape[1]), preferred_element_type=F32)
-    means[...] = (pairs[-2][...] + pairs[-1][...]) * 0.5
     for chunk in range(CHUNKS):
         span = slice(chunk * BY, (chunk + 1) * BY)
         lanes = slice(chunk % ZB * BZ, (chunk % ZB + 1) * BZ)
-        result = jnp.zeros((BY, BZ), F32)
-        for level in range(levels):
-            mine, other = pairs[2 * level][span, :], pairs[2 * level + 1][span, :]
-            result = result + (mine - other) * 0.5 * mask[level + 1 : level + 2, lanes]
+        near, far = mine[span, :] + one[span, :], two[span, :] + three[span, :]
+        result = (mine[span, :] - one[span, :]) * 0.5 * mask[1:2, lanes]
+        result = result + (near - far) * 0.25 * mask[2:3, lanes]
+        result = result + (half[span, :] - other[span, :]) * 0.5 * mask[3:4, lanes]
         total[span, :] = result
-
-
-def details_kernel(place, recv, rows, velocity_hbm, after, detail, velocity, sems):
-    del after
-    parts, cells, wide = rows.shape
-    planes = cells // BY
-    copy = pltpu.make_async_copy(velocity_hbm, velocity, sems.at[0])
-    copy.start()
-    row, column = iota((cells, planes), 0), iota((cells, planes), 1)
-    span = jnp.maximum(2 * (column & -column), 1).astype(F32)
-    tall = jnp.where((row >> 3 == column) & (column > 0), 1.0 / span, 0.0).astype(BF16)
-    kept = recv[pl.ds(EXTRA, planes, stride=ROWS), :].astype(BF16)
-    kept = jnp.dot(tall, kept, preferred_element_type=F32).astype(BF16)
-    mask = jnp.dot(kept, pick_table(OWN_KEPT + SLICE * (place[1] & 7), wide), preferred_element_type=F32)
-    row, column = iota((cells, cells), 0), iota((cells, cells), 1)
-    same = row & (BY - 1) == column & (BY - 1)
-    inverse = jnp.where(same, sign_of(column >> 3, row >> 3, planes), 0.0).astype(BF16)
-    unmix = unmix_table(wide)
-    for c in range(parts):
-        detail[c] = remix(left_product(inverse, rows[c] * mask), unmix)
-    copy.wait()
 
 
 def finish_kernel(got, mine, other, partial, mask, detail, velocity, out, rows):
@@ -389,10 +361,10 @@
         )
 
     vort_scratch = pltpu.VMEM((parts, cells, wide), BF16)
-    send, line, own = call(
+    send, line = call(
         head_kernel,
         "head",
-        (array(planes * ROWS, BZ), array(*line_shape), array(8, BZ)),
+        (array(planes * ROWS, BZ), array(*line_shape)),
         [loose] * 3,
         [
             pltpu.SMEM(counts.shape, jnp.int32),
@@ -403,52 +375,45 @@
         params=pltpu.CompilerParams(vmem_limit_bytes=60 * 1024 * 1024),
     )(counts, blocks, vort)
     recv = over_yz(send, planes)
-    pairs = [line, from_partner(line, 1)]
-    line = (pairs[0] + pairs[1]) * 0.5
-    pairs += [line, from_partner(line, 2)]
+    near = [from_partner(line, distance) for distance in (1, 2, 3)]
+    half = (line + near[0] + (near[1] + near[2])) * 0.25
     back, corner = call(
         plane_kernel,
         "plane",
         (array(planes * ROWS, BZ), array(slabs, PACKED, BZ)),
-        [smem, loose, vmem, loose],
-        [pltpu.VMEM((8, BZ), F32), pltpu.SemaphoreType.DMA((1,))],
-    )(place, own, recv, pairs[3])
+        [smem, vmem, loose],
+    )(place, recv, half)
     gathered = exchange(corner, "gx")
-    rows, line = call(
-        levels_kernel,
-        "levels",
-        (array(parts, cells, wide), array(*line_shape)),
-        [loose, vmem, vmem, loose],
-        [vort_scratch, pltpu.SemaphoreType.DMA((parts,))],
-        cost(3),
-    )(vort, pairs[2], pairs[3], corner)
-    pairs += [line, from_partner(line, 4)]
-    back = call(
-        corner_kernel, "corner", array(planes * ROWS, BZ), [smem, vmem, vmem, loose]
-    )(place, gathered, back, line)
-    got = over_yz(back, planes)
-    partial, line, mask = call(
-        line_kernel,
-        "line",
-        (array(*line_shape), array(*line_shape), array(8, wide)),
-        [smem, vmem, loose] + [vmem] * 6,
-    )(place, gathered, back, *pairs)
-    other = from_partner(line, 8)
+    opposite = from_partner(half, 4)
     detail, speed = call(
         details_kernel,
         "details",
         (array(parts, cells, wide), jax.ShapeDtypeStruct((parts, cells, wide), BF16)),
-        [smem, vmem, vmem, loose, loose],
-        [pltpu.SemaphoreType.DMA((1,))],
-        cost(4),
-    )(place, recv, rows, velocity.reshape(parts, cells, wide), line)
+        [smem, vmem, loose, loose, loose],
+        [vort_scratch, pltpu.SemaphoreType.DMA((parts + 1,))],
+        cost(7),
+    )(place, recv, vort, velocity.reshape(parts, cells, wide), corner)
+    back, means = call(
+        corner_kernel,
+        "corner",
+        (array(planes * ROWS, BZ), array(*line_shape)),
+        [smem] + [vmem] * 4,
+    )(place, gathered, back, half, opposite)
+    got = over_yz(back, planes)
+    other = from_partner(means, 8)
+    partial, mask = call(
+        line_kernel,
+        "line",
+        (array(*line_shape), array(8, wide)),
+        [smem, vmem, loose] + [vmem] * 6,
+    )(place, gathered, means, line, *near, half, opposite)
     out = call(
         finish_kernel,
         "finish",
         jax.ShapeDtypeStruct((parts, cells, wide), BF16),
         [vmem] * 7,
         [pltpu.VMEM((parts * (planes + tall), wide), F32)],
-    )(got, line, other, partial, mask, detail, speed)
+    )(got, means, other, partial, mask, detail, speed)
     return out.reshape(parts, planes, tall, wide)
 
 

time: 78.4 us -> 73.2 us (0.934)
  waiting for transfers between devices: 16.3 us -> 5.53 us
  starting transfers between devices: 41.9 us -> 48.9 us
  local copies, waits for them, and re-layouts: 4.39 us -> 2.26 us
    ppermute x4 -> x5, starting transfers between devices: 11.8 us -> 19.6 us  [from_partner(): return lax.ppermute(value, 'gx', pairs)]
    ppermute x4 -> x5, waiting for transfers between devices: 10.9 us -> 5.13 us  [from_partner(): return lax.ppermute(value, 'gx', pairs)]
    all_to_all x3, waiting for transfers between devices: 5.42 us -> 0.41 us  [exchange(): return lax.all_to_all(value, axis, split_axis=0, concat_axis=0, tiled=True)]
    pallas_call x1, Pallas kernels: 2.32 us -> 5.09 us  [body(): call(details_kernel, 'details', (array(parts, cells, wide), jax.ShapeDtyp...]
    unnamed x12 -> x6, local copies, waits for them, and re-layouts: 4.39 us -> 2.26 us
    pallas_call x4 -> x3, Pallas kernels: 7.61 us -> 5.51 us  [the longest x1 3.16 us: body(): call(head_kernel, 'head', (array(planes * ROWS, BZ), array(*line_shape)),...]
  transfers between devices with their start and end apart: 7 -> 8, of which waited for: 5 -> 4; matrix products, arithmetic and copies ran while one was open for 1% -> 1% of each run, Pallas kernels for 7% -> 8%
where the time goes in v3:
time: 73.2 us; the launch traced here: 72.6 us
  starting transfers between devices  48.9 us (67%)
  Pallas kernels  14.2 us (19%)
  waiting for transfers between devices  5.53 us (8%)
  local copies, waits for them, and re-layouts  2.26 us (3%)
  other arithmetic  0.89 us (1%)
  between operations  0.78 us (1%)
    all_to_all x3, starting transfers between devices, exchange(): return lax.all_to_all(value, axis, split_axis=0, concat_axis=0, tiled=True)  29.4 us
    ppermute x5, starting transfers between devices, from_partner(): return lax.ppermute(value, 'gx', pairs)  19.6 us
    ppermute x5, waiting for transfers between devices, from_partner(): return lax.ppermute(value, 'gx', pairs)  5.13 us
    pallas_call x1, Pallas kernels, body(): call(details_kernel, 'details', (array(parts, cells, wide), jax.ShapeDtyp...  5.09 us
    pallas_call x1, Pallas kernels, body(): call(head_kernel, 'head', (array(planes * ROWS, BZ), array(*line_shape)),...  3.16 us
    unnamed x6, local copies, waits for them, and re-layouts  2.26 us
    pallas_call x1, Pallas kernels, body(): call(finish_kernel, 'finish', jax.ShapeDtypeStruct((parts, cells, wide),...  2.08 us
    pallas_call x1, Pallas kernels, body(): call(corner_kernel, 'corner', (array(planes * ROWS, BZ), array(*line_shap...  1.66 us
  transfers between devices with their start and end apart: 8, of which 4 were waited for; matrix products, arithmetic and copies ran while one was open for 1% of the time, Pallas kernels for 8%

profile of v3, /device:TPU:2, one launch (start us, length us, event | category | flops | bytes accessed | tf_op | source)
XLA Modules:
  0.0 72.6 jit_solution(15164448373727983601)
XLA Ops:
  0.7 3.2 %head.1 = (f32[448,128]{1,0:T(8,128)}, f32[96,128]{1,0:T(8,128)}) custom-call(s32[1]{0:T(128)S(6)} %copy.7.counts_hbm, s32[1,128]{1,0:T(1,128)} %blocks_hbm.1, bf16[3,256,512]{2,1,0:T(8,128)(2,1)} %bitcast.12), custom_call_target="tpu_custom_call" | custom-call | tf_op jit(solution)/shard_map/head/pallas_call | solution.py:364
  3.8 10.3 %all-to-all-start = ((f32[32,14,1,128]{3,2,1,0:T(1,128)}), f32[32,14,1,128]{3,2,1,0:T(1,128)S(1)}, u32[]{:S(2)}, u32[]{:S(2)}) async-start(f32[32,14,1,128]{3,2,1,0:T(1,128)} %bitcast.15), calls=%async_computation | async-start | bytes 458752 | tf_op jit(solution)/shard_map/all_to_all | solution.py:313
  14.1 3.2 %collective-permute-start.2 = (f32[96,128]{1,0:T(8,128)}, f32[96,128]{1,0:T(8,128)S(1)}, u32[]{:S(2)}, u32[]{:S(2)}) collective-permute-start(f32[96,128]{1,0:T(8,128)} %get-tuple-element.16.mine), channel_id=1, source_target_pairs={{0,96},{32,64},{64,32},{96,0},{128,224},{160,192},{192,160},{224,1... | collective-permute-start | bytes 147464 | tf_op jit(solution)/shard_map/ppermute | solution.py:325
  17.3 3.0 %collective-permute-start.1 = (f32[96,128]{1,0:T(8,128)}, f32[96,128]{1,0:T(8,128)S(1)}, u32[]{:S(2)}, u32[]{:S(2)}) collective-permute-start(f32[96,128]{1,0:T(8,128)} %get-tuple-element.16.mine), channel_id=1, source_target_pairs={{0,64},{32,96},{64,0},{96,32},{128,192},{160,224},{192,128},{224,1... | collective-permute-start | bytes 147464 | tf_op jit(solution)/shard_map/ppermute | solution.py:325
  20.3 2.0 %collective-permute-start = (f32[96,128]{1,0:T(8,128)}, f32[96,128]{1,0:T(8,128)S(1)}, u32[]{:S(2)}, u32[]{:S(2)}) collective-permute-start(f32[96,128]{1,0:T(8,128)} %get-tuple-element.16.mine), channel_id=1, source_target_pairs={{0,32},{32,0},{64,96},{96,64},{128,160},{160,128},{192,224},{224,1... | collective-permute-start | bytes 147464 | tf_op jit(solution)/shard_map/ppermute | solution.py:325
  22.3 0.1 pad_add_fusion.place
  22.4 0.0 collective-permute-done.2.three
  22.4 1.3 %collective-permute-done.1.two = f32[96,128]{1,0:T(8,128)S(1)} collective-permute-done((f32[96,128]{1,0:T(8,128)}, f32[96,128]{1,0:T(8,128)S(1)}, u32[]{:S(2)}, u32[]{:S(2)}) %collective-permute-start.1) | collective-permute-done | bytes 49184 | tf_op jit(solution)/shard_map/ppermute | solution.py:325
  23.7 0.0 collective-permute-done.one
  23.7 0.8 %add_multiply_fusion.after.mine.half = f32[96,128]{1,0:T(8,128)S(1)} fusion(f32[96,128]{1,0:T(8,128)S(1)} %collective-permute-done.1.two, f32[96,128]{1,0:T(8,128)S(1)} %collective-permute-done.2.three, f32[96,128]{1,0:T(8,128)} %get-tuple-element.16.mine, f32[96,128]{1,0:T(8,128)S(1)} %collective-permute-done.one), kind=kLoop, calls=%fused_computation | loop fusion | flops 49152 | bytes 245760 | tf_op jit(solution)/shard_map/mul | solution.py:379
  24.5 0.2 all-to-all-done
  24.7 1.5 %plane.1 = (f32[448,128]{1,0:T(8,128)S(1)}, f32[16,16,128]{2,1,0:T(8,128)}) custom-call(s32[2]{0:T(128)S(1)} %pad_add_fusion.place, f32[448,128]{1,0:T(8,128)S(1)} %bitcast.10, f32[96,128]{1,0:T(8,128)S(1)} %add_multiply_fusion.after.mine.half), custom_call_target="tpu_custom_call" | custom-call | tf_op jit(solution)/shard_map/plane/pallas_call | solution.py:380
  26.3 10.4 %all-to-all-start.1 = ((f32[16,16,128]{2,1,0:T(8,128)}), f32[16,16,128]{2,1,0:T(8,128)S(1)}, u32[]{:S(2)}, u32[]{:S(2)}) async-start(f32[16,16,128]{2,1,0:T(8,128)} %get-tuple-element.17.after), calls=%async_computation.1 | async-start | bytes 262144 | tf_op jit(solution)/shard_map/all_to_all | solution.py:313
  36.7 4.7 %collective-permute-start.3 = (f32[96,128]{1,0:T(8,128)S(1)}, f32[96,128]{1,0:T(8,128)S(1)}, u32[]{:S(2)}, u32[]{:S(2)}) collective-permute-start(f32[96,128]{1,0:T(8,128)S(1)} %add_multiply_fusion.after.mine.half), channel_id=1, source_target_pairs={{0,128},{32,160},{64,192},{96,224},{128,0},{160,32},{192,64},{224,... | collective-permute-start | bytes 147464 | tf_op jit(solution)/shard_map/ppermute | solution.py:325
  41.4 3.8 %collective-permute-done.3.other = f32[96,128]{1,0:T(8,128)S(1)} collective-permute-done((f32[96,128]{1,0:T(8,128)S(1)}, f32[96,128]{1,0:T(8,128)S(1)}, u32[]{:S(2)}, u32[]{:S(2)}) %collective-permute-start.3) | collective-permute-done | bytes 49184 | tf_op jit(solution)/shard_map/ppermute | solution.py:325
  45.2 0.2 all-to-all-done.1.gathered
  45.4 1.7 %corner.1 = (f32[448,128]{1,0:T(8,128)}, f32[96,128]{1,0:T(8,128)S(1)}) custom-call(s32[2]{0:T(128)S(1)} %pad_add_fusion.place, f32[16,16,128]{2,1,0:T(8,128)S(1)} %all-to-all-done.1.gathered, f32[448,128]{1,0:T(8,128)S(1)} %get-tuple-element.18.back_in, f32[96,128]{1,0:T(8,128)S(1)} %add_multiply_fusion.after.mine.half, ...), custom_call_target="tpu_custom_call" | custom-call | tf_op jit(solution)/shard_map/corner/pallas_call | solution.py:396
  47.1 8.7 %all-to-all-start.2 = ((f32[32,14,1,128]{3,2,1,0:T(1,128)}), f32[32,14,1,128]{3,2,1,0:T(1,128)S(1)}, u32[]{:S(2)}, u32[]{:S(2)}) async-start(f32[32,14,1,128]{3,2,1,0:T(1,128)} %bitcast.5), calls=%async_computation.2 | async-start | bytes 458752 | tf_op jit(solution)/shard_map/all_to_all | solution.py:313
  55.8 6.6 %collective-permute-start.4 = (f32[96,128]{1,0:T(8,128)S(1)}, f32[96,128]{1,0:T(8,128)S(1)}, u32[]{:S(2)}, u32[]{:S(2)}) collective-permute-start(f32[96,128]{1,0:T(8,128)S(1)} %get-tuple-element.20.after.mine), channel_id=1, source_target_pairs={{0,256},{32,288},{64,320},{96,352},{128,384},{160,416},{192,448},{... | collective-permute-start | bytes 147464 | tf_op jit(solution)/shard_map/ppermute | solution.py:325
  62.4 0.0 copy-start
  62.4 1.1 %copy-done = bf16[3,32,8,512]{3,2,1,0:T(8,128)(2,1)S(1)} copy-done((bf16[3,32,8,512]{3,2,1,0:T(8,128)(2,1)S(1)}, bf16[3,32,8,512]{3,2,1,0:T(8,128)(2,1)}, u32[]{:S(2)}) %copy-start) | copy-done | bytes 786456
  63.5 0.0 copy-start.2
  63.5 1.1 %copy-done.2 = bf16[3,32,8,512]{3,2,1,0:T(8,128)(2,1)S(1)} copy-done((bf16[3,32,8,512]{3,2,1,0:T(8,128)(2,1)S(1)}, bf16[3,32,8,512]{3,2,1,0:T(8,128)(2,1)}, u32[]{:S(2)}) %copy-start.2) | copy-done | bytes 786456
  64.7 0.0 copy-start.1
  64.7 5.1 %details.1 = (f32[3,256,512]{2,1,0:T(8,128)S(1)}, bf16[3,256,512]{2,1,0:T(8,128)(2,1)S(1)}) custom-call(s32[2]{0:T(128)S(1)} %pad_add_fusion.place, f32[448,128]{1,0:T(8,128)S(1)} %bitcast.11, bf16[3,256,512]{2,1,0:T(8,128)(2,1)S(1)} %bitcast.13, bf16[3,256,512]{2,1,0:T(8,128)(2,1)S(1)} %bitcast.14, f32[16,16,128]{2,1,0:T(8,128)} %get-tuple-element.17.after), custom_call_target="tpu_custom_call" | custom-call | flops 1409286144 | bytes 3932160 | tf_op jit(solution)/shard_map/details/pallas_call | solution.py:388
  69.8 0.0 copy-done.1
  69.8 0.7 line.1
  70.5 0.0 collective-permute-done.4.other
  70.5 0.0 all-to-all-done.2
  70.5 2.1 %finish.1 = bf16[3,256,512]{2,1,0:T(8,128)(2,1)} custom-call(f32[448,128]{1,0:T(8,128)S(1)} %bitcast.9, f32[96,128]{1,0:T(8,128)S(1)} %get-tuple-element.20.after.mine, f32[96,128]{1,0:T(8,128)S(1)} %collective-permute-done.4.other, f32[96,128]{1,0:T(8,128)S(1)} %get-tuple-element.21.partial, f32[8,512]{1,0:T(8,128)S(1)} %get-tuple-element.22.mask, ...), custom_call_target="tpu_custom_call" | custom-call | tf_op jit(solution)/shard_map/finish/pallas_call | solution.py:410
Async XLA Ops:
  3.8 20.9 %all-to-all-start = ((f32[32,14,1,128]{3,2,1,0:T(1,128)}), f32[32,14,1,128]{3,2,1,0:T(1,128)S(1)}, u32[]{:S(2)}, u32[]{:S(2)}) async-start(f32[32,14,1,128]{3,2,1,0:T(1,128)} %bitcast.15), calls=%async_computation | async-start | bytes 458752 | tf_op jit(solution)/shard_map/all_to_all | solution.py:313
  14.1 8.3 %collective-permute-start.2 = (f32[96,128]{1,0:T(8,128)}, f32[96,128]{1,0:T(8,128)S(1)}, u32[]{:S(2)}, u32[]{:S(2)}) collective-permute-start(f32[96,128]{1,0:T(8,128)} %get-tuple-element.16.mine), channel_id=1, source_target_pairs={{0,96},{32,64},{64,32},{96,0},{128,224},{160,192},{192,160},{224,1... | collective-permute-start | bytes 147464 | tf_op jit(solution)/shard_map/ppermute | solution.py:325
  17.3 6.5 %collective-permute-start.1 = (f32[96,128]{1,0:T(8,128)}, f32[96,128]{1,0:T(8,128)S(1)}, u32[]{:S(2)}, u32[]{:S(2)}) collective-permute-start(f32[96,128]{1,0:T(8,128)} %get-tuple-element.16.mine), channel_id=1, source_target_pairs={{0,64},{32,96},{64,0},{96,32},{128,192},{160,224},{192,128},{224,1... | collective-permute-start | bytes 147464 | tf_op jit(solution)/shard_map/ppermute | solution.py:325
  20.3 3.4 %collective-permute-start = (f32[96,128]{1,0:T(8,128)}, f32[96,128]{1,0:T(8,128)S(1)}, u32[]{:S(2)}, u32[]{:S(2)}) collective-permute-start(f32[96,128]{1,0:T(8,128)} %get-tuple-element.16.mine), channel_id=1, source_target_pairs={{0,32},{32,0},{64,96},{96,64},{128,160},{160,128},{192,224},{224,1... | collective-permute-start | bytes 147464 | tf_op jit(solution)/shard_map/ppermute | solution.py:325
  26.3 19.2 %all-to-all-start.1 = ((f32[16,16,128]{2,1,0:T(8,128)}), f32[16,16,128]{2,1,0:T(8,128)S(1)}, u32[]{:S(2)}, u32[]{:S(2)}) async-start(f32[16,16,128]{2,1,0:T(8,128)} %get-tuple-element.17.after), calls=%async_computation.1 | async-start | bytes 262144 | tf_op jit(solution)/shard_map/all_to_all | solution.py:313
  36.7 8.6 %collective-permute-start.3 = (f32[96,128]{1,0:T(8,128)S(1)}, f32[96,128]{1,0:T(8,128)S(1)}, u32[]{:S(2)}, u32[]{:S(2)}) collective-permute-start(f32[96,128]{1,0:T(8,128)S(1)} %add_multiply_fusion.after.mine.half), channel_id=1, source_target_pairs={{0,128},{32,160},{64,192},{96,224},{128,0},{160,32},{192,64},{224,... | collective-permute-start | bytes 147464 | tf_op jit(solution)/shard_map/ppermute | solution.py:325
  47.1 23.4 %all-to-all-start.2 = ((f32[32,14,1,128]{3,2,1,0:T(1,128)}), f32[32,14,1,128]{3,2,1,0:T(1,128)S(1)}, u32[]{:S(2)}, u32[]{:S(2)}) async-start(f32[32,14,1,128]{3,2,1,0:T(1,128)} %bitcast.5), calls=%async_computation.2 | async-start | bytes 458752 | tf_op jit(solution)/shard_map/all_to_all | solution.py:313
  55.8 14.7 %collective-permute-start.4 = (f32[96,128]{1,0:T(8,128)S(1)}, f32[96,128]{1,0:T(8,128)S(1)}, u32[]{:S(2)}, u32[]{:S(2)}) collective-permute-start(f32[96,128]{1,0:T(8,128)S(1)} %get-tuple-element.20.after.mine), channel_id=1, source_target_pairs={{0,256},{32,288},{64,320},{96,352},{128,384},{160,416},{192,448},{... | collective-permute-start | bytes 147464 | tf_op jit(solution)/shard_map/ppermute | solution.py:325
  62.4 1.1 %copy-start = (bf16[3,32,8,512]{3,2,1,0:T(8,128)(2,1)S(1)}, bf16[3,32,8,512]{3,2,1,0:T(8,128)(2,1)}, u32[]{:S(2)}) copy-start(bf16[3,32,8,512]{3,2,1,0:T(8,128)(2,1)} %param.4) | copy-start | bytes 2359300
  63.5 1.1 %copy-start.2 = (bf16[3,32,8,512]{3,2,1,0:T(8,128)(2,1)S(1)}, bf16[3,32,8,512]{3,2,1,0:T(8,128)(2,1)}, u32[]{:S(2)}) copy-start(bf16[3,32,8,512]{3,2,1,0:T(8,128)(2,1)} %param.5) | copy-start | bytes 2359300
  64.7 5.1 %copy-start.1 = (f32[96,128]{1,0:T(8,128)S(1)}, f32[96,128]{1,0:T(8,128)}, u32[]{:S(2)}) copy-start(f32[96,128]{1,0:T(8,128)} %get-tuple-element.16.mine) | copy-start | bytes 147460

commit v4 on v3

--- a/solution.py
+++ b/solution.py
@@ -202,16 +202,10 @@
             back[pl.ds(c * ZB + zb, planes, stride=ROWS), :] = data[:, zb * BZ : (zb + 1) * BZ]
 
 
-def details_kernel(place, recv, vort_hbm, velocity_hbm, after, detail, velocity, vort, sems):
+def details_kernel(place, recv, vort, after, detail):
     del after
     parts, cells, wide = vort.shape
     planes = cells // BY
-    copies = [
-        pltpu.make_async_copy(vort_hbm.at[c], vort.at[c], sems.at[c]) for c in range(parts)
-    ]
-    copies.append(pltpu.make_async_copy(velocity_hbm, velocity, sems.at[parts]))
-    for copy in copies:
-        copy.start()
     row, column = iota((cells, planes), 0), iota((cells, planes), 1)
     span = jnp.maximum(2 * (column & -column), 1).astype(F32)
     tall = jnp.where((row >> 3 == column) & (column > 0), 1.0 / span, 0.0).astype(BF16)
@@ -226,13 +220,12 @@
     inverse = jnp.where(same, sign, 0.0).astype(BF16)
     mix, unmix = mix_table(wide), unmix_table(wide)
     for c in range(parts):
-        copies[c].wait()
         rows = remix(jnp.dot(forward, vort[c], preferred_element_type=F32), mix)
         detail[c] = remix(left_product(inverse, rows * mask), unmix)
-    copies[parts].wait()
-
-
-def corner_kernel(place, gathered, back_in, mine, other, back, means):
+
+
+def corner_kernel(place, gathered, back_in, mine, other, after, back, means):
+    del after
     means[...] = (mine[...] + other[...]) * 0.5
     slabs = gathered.shape[0]
     planes = back.shape[0] // ROWS
@@ -385,20 +378,19 @@
     )(place, recv, half)
     gathered = exchange(corner, "gx")
     opposite = from_partner(half, 4)
-    detail, speed = call(
+    detail = call(
         details_kernel,
         "details",
-        (array(parts, cells, wide), jax.ShapeDtypeStruct((parts, cells, wide), BF16)),
-        [smem, vmem, loose, loose, loose],
-        [vort_scratch, pltpu.SemaphoreType.DMA((parts + 1,))],
-        cost(7),
-    )(place, recv, vort, velocity.reshape(parts, cells, wide), corner)
+        array(parts, cells, wide),
+        [smem, vmem, vmem, loose],
+        cost=cost(7),
+    )(place, recv, vort, corner)
     back, means = call(
         corner_kernel,
         "corner",
         (array(planes * ROWS, BZ), array(*line_shape)),
-        [smem] + [vmem] * 4,
-    )(place, gathered, back, half, opposite)
+        [smem] + [vmem] * 4 + [loose],
+    )(place, gathered, back, half, opposite, detail)
     got = over_yz(back, planes)
     other = from_partner(means, 8)
     partial, mask = call(
@@ -413,7 +405,7 @@
         jax.ShapeDtypeStruct((parts, cells, wide), BF16),
         [vmem] * 7,
         [pltpu.VMEM((parts * (planes + tall), wide), F32)],
-    )(got, means, other, partial, mask, detail, speed)
+    )(got, means, other, partial, mask, detail, velocity.reshape(parts, cells, wide))
     return out.reshape(parts, planes, tall, wide)
 
 

time: 73.2 us -> 71.1 us (0.971)
  the two profiles are of different devices: /device:TPU:2 before, /device:TPU:8 now
where the time goes in v4:
time: 71.1 us; the launch traced here: 70.5 us
  starting transfers between devices  47.7 us (67%)
  Pallas kernels  13.2 us (19%)
  waiting for transfers between devices  7.86 us (11%)
  other arithmetic  0.89 us (1%)
  between operations  0.86 us (1%)
    all_to_all x3, starting transfers between devices, exchange(): return lax.all_to_all(value, axis, split_axis=0, concat_axis=0, tiled=True)  28.3 us
    ppermute x5, starting transfers between devices, from_partner(): return lax.ppermute(value, 'gx', pairs)  19.5 us
    pallas_call x1, Pallas kernels, body(): call(details_kernel, 'details', array(parts, cells, wide), [smem, vmem, v...  4.08 us
    ppermute x5, waiting for transfers between devices, from_partner(): return lax.ppermute(value, 'gx', pairs)  3.95 us
    all_to_all x3, waiting for transfers between devices, exchange(): return lax.all_to_all(value, axis, split_axis=0, concat_axis=0, tiled=True)  3.91 us
    pallas_call x1, Pallas kernels, body(): call(head_kernel, 'head', (array(planes * ROWS, BZ), array(*line_shape)),...  3.16 us
    pallas_call x1, Pallas kernels, body(): call(finish_kernel, 'finish', jax.ShapeDtypeStruct((parts, cells, wide),...  2.09 us
    pallas_call x1, Pallas kernels, body(): call(corner_kernel, 'corner', (array(planes * ROWS, BZ), array(*line_shap...  1.66 us
  transfers between devices with their start and end apart: 8, of which 4 were waited for; matrix products, arithmetic and copies ran while one was open for 1% of the time, Pallas kernels for 7%

profile of v4, /device:TPU:8, one launch (start us, length us, event | category | flops | bytes accessed | tf_op | source)
XLA Modules:
  0.0 70.5 jit_solution(16918736876260632566)
XLA Ops:
  0.0 0.0 copy-start.1
  0.7 3.2 %head.1 = (f32[448,128]{1,0:T(8,128)}, f32[96,128]{1,0:T(8,128)}) custom-call(s32[1]{0:T(128)S(6)} %copy.7.counts_hbm, s32[1,128]{1,0:T(1,128)} %blocks_hbm.1, bf16[3,256,512]{2,1,0:T(8,128)(2,1)} %bitcast.13), custom_call_target="tpu_custom_call" | custom-call | tf_op jit(solution)/shard_map/head/pallas_call | solution.py:357
  3.9 10.2 %all-to-all-start = ((f32[32,14,1,128]{3,2,1,0:T(1,128)}), f32[32,14,1,128]{3,2,1,0:T(1,128)S(1)}, u32[]{:S(2)}, u32[]{:S(2)}) async-start(f32[32,14,1,128]{3,2,1,0:T(1,128)} %bitcast.15), calls=%async_computation | async-start | bytes 458752 | tf_op jit(solution)/shard_map/all_to_all | solution.py:306
  14.1 3.2 %collective-permute-start.2 = (f32[96,128]{1,0:T(8,128)}, f32[96,128]{1,0:T(8,128)S(1)}, u32[]{:S(2)}, u32[]{:S(2)}) collective-permute-start(f32[96,128]{1,0:T(8,128)} %get-tuple-element.14.mine), channel_id=1, source_target_pairs={{0,96},{32,64},{64,32},{96,0},{128,224},{160,192},{192,160},{224,1... | collective-permute-start | bytes 147464 | tf_op jit(solution)/shard_map/ppermute | solution.py:318
  17.2 3.0 %collective-permute-start.1 = (f32[96,128]{1,0:T(8,128)}, f32[96,128]{1,0:T(8,128)S(1)}, u32[]{:S(2)}, u32[]{:S(2)}) collective-permute-start(f32[96,128]{1,0:T(8,128)} %get-tuple-element.14.mine), channel_id=1, source_target_pairs={{0,64},{32,96},{64,0},{96,32},{128,192},{160,224},{192,128},{224,1... | collective-permute-start | bytes 147464 | tf_op jit(solution)/shard_map/ppermute | solution.py:318
  20.3 2.0 %collective-permute-start = (f32[96,128]{1,0:T(8,128)}, f32[96,128]{1,0:T(8,128)S(1)}, u32[]{:S(2)}, u32[]{:S(2)}) collective-permute-start(f32[96,128]{1,0:T(8,128)} %get-tuple-element.14.mine), channel_id=1, source_target_pairs={{0,32},{32,0},{64,96},{96,64},{128,160},{160,128},{192,224},{224,1... | collective-permute-start | bytes 147464 | tf_op jit(solution)/shard_map/ppermute | solution.py:318
  22.3 0.1 pad_add_fusion.place
  22.4 0.0 collective-permute-done.2.three
  22.4 1.3 %collective-permute-done.1.two = f32[96,128]{1,0:T(8,128)S(1)} collective-permute-done((f32[96,128]{1,0:T(8,128)}, f32[96,128]{1,0:T(8,128)S(1)}, u32[]{:S(2)}, u32[]{:S(2)}) %collective-permute-start.1) | collective-permute-done | bytes 49184 | tf_op jit(solution)/shard_map/ppermute | solution.py:318
  23.7 0.0 collective-permute-done.one
  23.7 0.8 %add_multiply_fusion.after.mine.half = f32[96,128]{1,0:T(8,128)S(1)} fusion(f32[96,128]{1,0:T(8,128)S(1)} %collective-permute-done.1.two, f32[96,128]{1,0:T(8,128)S(1)} %collective-permute-done.2.three, f32[96,128]{1,0:T(8,128)} %get-tuple-element.14.mine, f32[96,128]{1,0:T(8,128)S(1)} %collective-permute-done.one), kind=kLoop, calls=%fused_computation | loop fusion | flops 49152 | bytes 245760 | tf_op jit(solution)/shard_map/mul | solution.py:372
  24.5 1.2 %all-to-all-done = f32[32,14,1,128]{3,2,1,0:T(1,128)S(1)} async-done(((f32[32,14,1,128]{3,2,1,0:T(1,128)}), f32[32,14,1,128]{3,2,1,0:T(1,128)S(1)}, u32[]{:S(2)}, u32[]{:S(2)}) %all-to-all-start) | async-done | bytes 229408 | tf_op jit(solution)/shard_map/all_to_all | solution.py:306
  25.7 1.5 %plane.1 = (f32[448,128]{1,0:T(8,128)S(1)}, f32[16,16,128]{2,1,0:T(8,128)}) custom-call(s32[2]{0:T(128)S(1)} %pad_add_fusion.place, f32[448,128]{1,0:T(8,128)S(1)} %bitcast.10, f32[96,128]{1,0:T(8,128)S(1)} %add_multiply_fusion.after.mine.half), custom_call_target="tpu_custom_call" | custom-call | tf_op jit(solution)/shard_map/plane/pallas_call | solution.py:373
  27.2 10.4 %all-to-all-start.1 = ((f32[16,16,128]{2,1,0:T(8,128)}), f32[16,16,128]{2,1,0:T(8,128)S(1)}, u32[]{:S(2)}, u32[]{:S(2)}) async-start(f32[16,16,128]{2,1,0:T(8,128)} %get-tuple-element.15.after), calls=%async_computation.1 | async-start | bytes 262144 | tf_op jit(solution)/shard_map/all_to_all | solution.py:306
  37.6 4.7 %collective-permute-start.3 = (f32[96,128]{1,0:T(8,128)S(1)}, f32[96,128]{1,0:T(8,128)S(1)}, u32[]{:S(2)}, u32[]{:S(2)}) collective-permute-start(f32[96,128]{1,0:T(8,128)S(1)} %add_multiply_fusion.after.mine.half), channel_id=1, source_target_pairs={{0,128},{32,160},{64,192},{96,224},{128,0},{160,32},{192,64},{224,... | collective-permute-start | bytes 147464 | tf_op jit(solution)/shard_map/ppermute | solution.py:318
  42.4 0.0 copy-done.1
  42.4 4.1 %details.1.after.detail = f32[3,256,512]{2,1,0:T(8,128)S(1)} custom-call(s32[2]{0:T(128)S(1)} %pad_add_fusion.place, f32[448,128]{1,0:T(8,128)S(1)} %bitcast.11, bf16[3,256,512]{2,1,0:T(8,128)(2,1)S(1)} %bitcast.14, f32[16,16,128]{2,1,0:T(8,128)} %get-tuple-element.15.after), custom_call_target="tpu_custom_call" | custom-call | flops 1409286144 | bytes 3932160 | tf_op jit(solution)/shard_map/details/pallas_call | solution.py:381
  46.5 0.0 copy-start.2
  46.5 0.0 copy-start
  46.5 0.0 collective-permute-done.3.other
  46.5 0.0 all-to-all-done.1.gathered
  46.5 1.7 %corner.1 = (f32[448,128]{1,0:T(8,128)}, f32[96,128]{1,0:T(8,128)S(1)}) custom-call(s32[2]{0:T(128)S(1)} %pad_add_fusion.place, f32[16,16,128]{2,1,0:T(8,128)S(1)} %all-to-all-done.1.gathered, f32[448,128]{1,0:T(8,128)S(1)} %get-tuple-element.16.back_in, f32[96,128]{1,0:T(8,128)S(1)} %add_multiply_fusion.after.mine.half, ...), custom_call_target="tpu_custom_call" | custom-call | tf_op jit(solution)/shard_map/corner/pallas_call | solution.py:388
  48.2 7.7 %all-to-all-start.2 = ((f32[32,14,1,128]{3,2,1,0:T(1,128)}), f32[32,14,1,128]{3,2,1,0:T(1,128)S(1)}, u32[]{:S(2)}, u32[]{:S(2)}) async-start(f32[32,14,1,128]{3,2,1,0:T(1,128)} %bitcast.5), calls=%async_computation.2 | async-start | bytes 458752 | tf_op jit(solution)/shard_map/all_to_all | solution.py:306
  55.8 6.5 %collective-permute-start.4 = (f32[96,128]{1,0:T(8,128)S(1)}, f32[96,128]{1,0:T(8,128)S(1)}, u32[]{:S(2)}, u32[]{:S(2)}) collective-permute-start(f32[96,128]{1,0:T(8,128)S(1)} %get-tuple-element.18.after.mine), channel_id=1, source_target_pairs={{0,256},{32,288},{64,320},{96,352},{128,384},{160,416},{192,448},{... | collective-permute-start | bytes 147464 | tf_op jit(solution)/shard_map/ppermute | solution.py:318
  62.4 0.0 copy-done.2
  62.4 0.7 line.1
  63.1 2.7 %collective-permute-done.4.other = f32[96,128]{1,0:T(8,128)S(1)} collective-permute-done((f32[96,128]{1,0:T(8,128)S(1)}, f32[96,128]{1,0:T(8,128)S(1)}, u32[]{:S(2)}, u32[]{:S(2)}) %collective-permute-start.4) | collective-permute-done | bytes 49184 | tf_op jit(solution)/shard_map/ppermute | solution.py:318
  65.7 2.7 %all-to-all-done.2 = f32[32,14,1,128]{3,2,1,0:T(1,128)S(1)} async-done(((f32[32,14,1,128]{3,2,1,0:T(1,128)}), f32[32,14,1,128]{3,2,1,0:T(1,128)S(1)}, u32[]{:S(2)}, u32[]{:S(2)}) %all-to-all-start.2) | async-done | bytes 229408 | tf_op jit(solution)/shard_map/all_to_all | solution.py:306
  68.4 0.0 copy-done
  68.4 2.1 %finish.1 = bf16[3,256,512]{2,1,0:T(8,128)(2,1)} custom-call(f32[448,128]{1,0:T(8,128)S(1)} %bitcast.9, f32[96,128]{1,0:T(8,128)S(1)} %get-tuple-element.18.after.mine, f32[96,128]{1,0:T(8,128)S(1)} %collective-permute-done.4.other, f32[96,128]{1,0:T(8,128)S(1)} %get-tuple-element.19.partial, f32[8,512]{1,0:T(8,128)S(1)} %get-tuple-element.20.mask, ...), custom_call_target="tpu_custom_call" | custom-call | tf_op jit(solution)/shard_map/finish/pallas_call | solution.py:402
Async XLA Ops:
  0.0 42.4 %copy-start.1 = (bf16[3,32,8,512]{3,2,1,0:T(8,128)(2,1)S(1)}, bf16[3,32,8,512]{3,2,1,0:T(8,128)(2,1)}, u32[]{:S(2)}) copy-start(bf16[3,32,8,512]{3,2,1,0:T(8,128)(2,1)} %param.4) | copy-start | bytes 2359300
  3.9 21.8 %all-to-all-start = ((f32[32,14,1,128]{3,2,1,0:T(1,128)}), f32[32,14,1,128]{3,2,1,0:T(1,128)S(1)}, u32[]{:S(2)}, u32[]{:S(2)}) async-start(f32[32,14,1,128]{3,2,1,0:T(1,128)} %bitcast.15), calls=%async_computation | async-start | bytes 458752 | tf_op jit(solution)/shard_map/all_to_all | solution.py:306
  14.1 8.3 %collective-permute-start.2 = (f32[96,128]{1,0:T(8,128)}, f32[96,128]{1,0:T(8,128)S(1)}, u32[]{:S(2)}, u32[]{:S(2)}) collective-permute-start(f32[96,128]{1,0:T(8,128)} %get-tuple-element.14.mine), channel_id=1, source_target_pairs={{0,96},{32,64},{64,32},{96,0},{128,224},{160,192},{192,160},{224,1... | collective-permute-start | bytes 147464 | tf_op jit(solution)/shard_map/ppermute | solution.py:318
  17.2 6.5 %collective-permute-start.1 = (f32[96,128]{1,0:T(8,128)}, f32[96,128]{1,0:T(8,128)S(1)}, u32[]{:S(2)}, u32[]{:S(2)}) collective-permute-start(f32[96,128]{1,0:T(8,128)} %get-tuple-element.14.mine), channel_id=1, source_target_pairs={{0,64},{32,96},{64,0},{96,32},{128,192},{160,224},{192,128},{224,1... | collective-permute-start | bytes 147464 | tf_op jit(solution)/shard_map/ppermute | solution.py:318
  20.3 3.4 %collective-permute-start = (f32[96,128]{1,0:T(8,128)}, f32[96,128]{1,0:T(8,128)S(1)}, u32[]{:S(2)}, u32[]{:S(2)}) collective-permute-start(f32[96,128]{1,0:T(8,128)} %get-tuple-element.14.mine), channel_id=1, source_target_pairs={{0,32},{32,0},{64,96},{96,64},{128,160},{160,128},{192,224},{224,1... | collective-permute-start | bytes 147464 | tf_op jit(solution)/shard_map/ppermute | solution.py:318
  27.2 19.3 %all-to-all-start.1 = ((f32[16,16,128]{2,1,0:T(8,128)}), f32[16,16,128]{2,1,0:T(8,128)S(1)}, u32[]{:S(2)}, u32[]{:S(2)}) async-start(f32[16,16,128]{2,1,0:T(8,128)} %get-tuple-element.15.after), calls=%async_computation.1 | async-start | bytes 262144 | tf_op jit(solution)/shard_map/all_to_all | solution.py:306
  37.6 8.8 %collective-permute-start.3 = (f32[96,128]{1,0:T(8,128)S(1)}, f32[96,128]{1,0:T(8,128)S(1)}, u32[]{:S(2)}, u32[]{:S(2)}) collective-permute-start(f32[96,128]{1,0:T(8,128)S(1)} %add_multiply_fusion.after.mine.half), channel_id=1, source_target_pairs={{0,128},{32,160},{64,192},{96,224},{128,0},{160,32},{192,64},{224,... | collective-permute-start | bytes 147464 | tf_op jit(solution)/shard_map/ppermute | solution.py:318
  46.5 15.9 %copy-start.2 = (f32[96,128]{1,0:T(8,128)S(1)}, f32[96,128]{1,0:T(8,128)}, u32[]{:S(2)}) copy-start(f32[96,128]{1,0:T(8,128)} %get-tuple-element.14.mine) | copy-start | bytes 147460
  46.5 22.0 %copy-start = (bf16[3,32,8,512]{3,2,1,0:T(8,128)(2,1)S(1)}, bf16[3,32,8,512]{3,2,1,0:T(8,128)(2,1)}, u32[]{:S(2)}) copy-start(bf16[3,32,8,512]{3,2,1,0:T(8,128)(2,1)} %param.5) | copy-start | bytes 2359300
  48.2 20.3 %all-to-all-start.2 = ((f32[32,14,1,128]{3,2,1,0:T(1,128)}), f32[32,14,1,128]{3,2,1,0:T(1,128)S(1)}, u32[]{:S(2)}, u32[]{:S(2)}) async-start(f32[32,14,1,128]{3,2,1,0:T(1,128)} %bitcast.5), calls=%async_computation.2 | async-start | bytes 458752 | tf_op jit(solution)/shard_map/all_to_all | solution.py:306
  55.8 9.9 %collective-permute-start.4 = (f32[96,128]{1,0:T(8,128)S(1)}, f32[96,128]{1,0:T(8,128)S(1)}, u32[]{:S(2)}, u32[]{:S(2)}) collective-permute-start(f32[96,128]{1,0:T(8,128)S(1)} %get-tuple-element.18.after.mine), channel_id=1, source_target_pairs={{0,256},{32,288},{64,320},{96,352},{128,384},{160,416},{192,448},{... | collective-permute-start | bytes 147464 | tf_op jit(solution)/shard_map/ppermute | solution.py:318

commit v5 on v4

--- a/solution.py
+++ b/solution.py
@@ -11,6 +11,7 @@
 ZB = 4
 CHUNKS = 12
 ROWS = 14
+BACK = 13
 EXTRA = 12
 KEPT = 13
 CORNER = 48
@@ -158,8 +159,13 @@
             line[chunk * BY : (chunk + 1) * BY, :] = part[planes : planes + BY]
             turned = jnp.broadcast_to(part[0:1], (8, BZ))
             turned = pltpu.roll(turned, c * SLICE, 1) if c else turned
-            extra[zb] = jnp.where(lane >> 4 == (turn + c) & 7, turned, extra[zb])
-    send[pl.ds(EXTRA, planes, stride=ROWS), :] = jnp.concatenate(extra, axis=0)
+            extra[zb] = jnp.where(lane >> 4 == (7 - turn + c) & 7, turned, extra[zb])
+    for zb in range(ZB):
+        turned = pltpu.roll(extra[zb], 0, 1, stride=SLICE, stride_axis=0)
+        turned = pltpu.roll(turned, SLICE, 1)
+        for row in range(8):
+            at = (zb * 8 + 7 - row) * ROWS + EXTRA
+            send[at : at + 1, :] = turned[row : row + 1]
 
 
 def level_tables(length):
@@ -174,19 +180,20 @@
     planes = recv.shape[0] // ROWS
     forward, inverse = level_tables(planes)
     extra = recv[pl.ds(EXTRA, planes, stride=ROWS), :]
-    extra = pltpu.roll(extra, (BZ - SLICE * (place[1] & 7)) & (BZ - 1), 1)
     lane = iota((PACKED, BZ), 1)
     row = iota((PACKED, BZ), 0)
     heads = recv[KEPT : KEPT + 1, :]
     first = 4 * row + (place[1] >> 3)
     low = jnp.sum(jnp.where(lane == first, heads, 0.0), axis=1, keepdims=True)
     high = jnp.sum(jnp.where(lane == first + HALF, heads, 0.0), axis=1, keepdims=True)
-    levels = left_product(forward, jnp.where(iota((planes, BZ), 1) < CORNER, extra, 0.0))
+    levels = left_product(forward, extra)
     packed = levels[0:PACKED] + pltpu.roll(levels[PACKED:planes], HALF, 1)
     packed = jnp.where(lane == CORNER, low, packed)
     packed = jnp.where(lane == HALF + CORNER, high, packed)
-    shifted = pltpu.roll(jnp.broadcast_to(heads, (PACKED, BZ)), (LINE_KEPT - ZB * place[1]) & (BZ - 1), 1)
-    packed = jnp.where((lane >= LINE_KEPT) & (lane < LINE_KEPT + ZB), shifted, packed)
+    own = jnp.where(lane >> 2 == place[1], heads, 0.0).astype(BF16)
+    source, target = iota((BZ, BZ), 0), iota((BZ, BZ), 1)
+    slot = jnp.where(target == LINE_KEPT + (source & 3), 1.0, 0.0).astype(BF16)
+    packed = packed + jnp.dot(own, slot, preferred_element_type=F32)
     for g in range(corner.shape[0]):
         corner[g] = packed
     pick = jnp.where(iota((BZ, ZB * BZ), 0) & 3 == iota((BZ, ZB * BZ), 1) >> 7, 1.0, 0.0)
@@ -199,7 +206,7 @@
         )
         data = left_product(inverse, left_product(forward, data) * mask)
         for zb in range(ZB):
-            back[pl.ds(c * ZB + zb, planes, stride=ROWS), :] = data[:, zb * BZ : (zb + 1) * BZ]
+            back[pl.ds(c * ZB + zb, planes, stride=BACK), :] = data[:, zb * BZ : (zb + 1) * BZ]
 
 
 def details_kernel(place, recv, vort, after, detail):
@@ -228,7 +235,7 @@
     del after
     means[...] = (mine[...] + other[...]) * 0.5
     slabs = gathered.shape[0]
-    planes = back.shape[0] // ROWS
+    planes = back.shape[0] // BACK
     lane = iota((PACKED, BZ), 1)
     back[...] = back_in[...]
     values = forward_levels([gathered[g] for g in range(slabs)])
@@ -240,8 +247,7 @@
         total = total + values[p] * jnp.where(lane < HALF, low, high) * sign
     total = jnp.concatenate([total, pltpu.roll(total, HALF, 1)], axis=0)
     total = jnp.where(iota((planes, BZ), 1) < CORNER, total, 0.0)
-    total = pltpu.roll(left_product(level_tables(planes)[1], total), SLICE * (place[1] & 7), 1)
-    back[pl.ds(EXTRA, planes, stride=ROWS), :] = total
+    back[pl.ds(EXTRA, planes, stride=BACK), :] = left_product(level_tables(planes)[1], total)
 
 
 def line_kernel(place, gathered, after, mine, one, two, three, half, other, total, mask):
@@ -263,12 +269,16 @@
         total[span, :] = result
 
 
-def finish_kernel(got, mine, other, partial, mask, detail, velocity, out, rows):
-    planes = got.shape[0] // ROWS
+def finish_kernel(got, mine, other, partial, mask, detail, velocity, out_hbm, rows, out, sems):
+    planes = got.shape[0] // BACK
     parts, cells, wide = velocity.shape
     inverse = level_tables(planes)[1]
-    extra = got[pl.ds(EXTRA, planes, stride=ROWS), :]
+    extra = got[pl.ds(EXTRA, planes, stride=BACK), :]
     slot, lane = iota((8, BZ), 0), iota((8, BZ), 1)
+    turned = [
+        pltpu.roll(extra[zb * 8 : (zb + 1) * 8], 0, 1, stride=SLICE, stride_axis=0)
+        for zb in range(ZB)
+    ]
     for c in range(parts):
         columns = []
         for zb in range(ZB):
@@ -278,16 +288,16 @@
             mean = (mine[span, :] + other[span, :]) * 0.5
             total = partial[span, :] + last * mask[4:5, lanes] + mean * mask[0:1, lanes]
             rows[parts * planes + c * BY : parts * planes + (c + 1) * BY, lanes] = total
-            corner = extra[zb * 8 : (zb + 1) * 8]
-            corner = jnp.where(lane >> 4 == (slot + c) & 7, corner, 0.0)
+            corner = jnp.where(lane >> 4 == (slot + c) & 7, turned[zb], 0.0)
             corner = jnp.sum(corner, axis=0, keepdims=True)
             corner = pltpu.roll(corner, BZ - c * SLICE, 1) if c else corner
-            data = got[pl.ds(c * ZB + zb, planes, stride=ROWS), :]
+            data = got[pl.ds(c * ZB + zb, planes, stride=BACK), :]
             columns.append(jnp.where(iota((planes, BZ), 0) == 0, corner, data))
         rows[c * planes : (c + 1) * planes, :] = left_product(
             inverse, jnp.concatenate(columns, axis=1)
         )
     rows[...] = remix(rows[...], unmix_table(wide))
+    copies = []
     for x in range(planes):
         span = slice(x * BY, (x + 1) * BY)
         smooth = [
@@ -300,6 +310,17 @@
         for c in range(parts):
             a, b = (c + 1) % parts, (c + 2) % parts
             out[c, span, :] = (smooth[a] * speed[b] - smooth[b] * speed[a]).astype(BF16)
+        if (x + 1) % 8 == 0:
+            done = pl.ds((x - 7) * BY, 8 * BY)
+            for c in range(parts):
+                copies.append(
+                    pltpu.make_async_copy(
+                        out.at[c, done, :], out_hbm.at[c, done, :], sems.at[len(copies)]
+                    )
+                )
+                copies[-1].start()
+    for copy in copies:
+        copy.wait()
 
 
 def exchange(value, axis):
@@ -307,8 +328,8 @@
 
 
 def over_yz(rows, planes):
-    moved = exchange(rows.reshape(planes, ROWS, 1, BZ), "yz")
-    return moved.reshape(planes * ROWS, BZ)
+    moved = exchange(rows.reshape(planes, -1, 1, BZ), "yz")
+    return moved.reshape(rows.shape)
 
 
 def from_partner(value, distance):
@@ -333,13 +354,13 @@
     def array(*shape):
         return jax.ShapeDtypeStruct(shape, F32)
 
-    def call(kernel, name, out_shape, in_specs, scratch=(), cost=None, params=params):
+    def call(kernel, name, out_shape, in_specs, scratch=(), cost=None, params=params, out=vmem):
         many = isinstance(out_shape, tuple)
         return pl.pallas_call(
             kernel,
             out_shape=out_shape,
             in_specs=in_specs,
-            out_specs=tuple(vmem for _ in out_shape) if many else vmem,
+            out_specs=tuple(out for _ in out_shape) if many else out,
             scratch_shapes=list(scratch),
             compiler_params=params,
             cost_estimate=cost,
@@ -373,7 +394,7 @@
     back, corner = call(
         plane_kernel,
         "plane",
-        (array(planes * ROWS, BZ), array(slabs, PACKED, BZ)),
+        (array(planes * BACK, BZ), array(slabs, PACKED, BZ)),
         [smem, vmem, loose],
     )(place, recv, half)
     gathered = exchange(corner, "gx")
@@ -388,7 +409,7 @@
     back, means = call(
         corner_kernel,
         "corner",
-        (array(planes * ROWS, BZ), array(*line_shape)),
+        (array(planes * BACK, BZ), array(*line_shape)),
         [smem] + [vmem] * 4 + [loose],
     )(place, gathered, back, half, opposite, detail)
     got = over_yz(back, planes)
@@ -404,7 +425,12 @@
         "finish",
         jax.ShapeDtypeStruct((parts, cells, wide), BF16),
         [vmem] * 7,
-        [pltpu.VMEM((parts * (planes + tall), wide), F32)],
+        [
+            pltpu.VMEM((parts * (planes + tall), wide), F32),
+            pltpu.VMEM((parts, cells, wide), BF16),
+            pltpu.SemaphoreType.DMA((parts * planes // 8,)),
+        ],
+        out=loose,
     )(got, means, other, partial, mask, detail, velocity.reshape(parts, cells, wide))
     return out.reshape(parts, planes, tall, wide)
 

time: 71.1 us -> 70.9 us (level)
  no operation moved by 1% of the time
where the time goes in v5:
time: 70.9 us; the launch traced here: 70.4 us
  starting transfers between devices  47.7 us (67%)
  Pallas kernels  13.2 us (19%)
  waiting for transfers between devices  7.61 us (11%)
  other arithmetic  0.89 us (1%)
  between operations  0.86 us (1%)
    all_to_all x3, starting transfers between devices, exchange(): return lax.all_to_all(value, axis, split_axis=0, concat_axis=0, tiled=True)  28.3 us
    ppermute x5, starting transfers between devices, from_partner(): return lax.ppermute(value, 'gx', pairs)  19.5 us
    pallas_call x1, Pallas kernels, body(): call(details_kernel, 'details', array(parts, cells, wide), [smem, vmem, v...  4.07 us
    ppermute x5, waiting for transfers between devices, from_partner(): return lax.ppermute(value, 'gx', pairs)  3.95 us
    all_to_all x3, waiting for transfers between devices, exchange(): return lax.all_to_all(value, axis, split_axis=0, concat_axis=0, tiled=True)  3.66 us
    pallas_call x1, Pallas kernels, body(): call(head_kernel, 'head', (array(planes * ROWS, BZ), array(*line_shape)),...  3.29 us
    pallas_call x1, Pallas kernels, body(): call(finish_kernel, 'finish', jax.ShapeDtypeStruct((parts, cells, wide),...  2.16 us
    pallas_call x1, Pallas kernels, body(): call(corner_kernel, 'corner', (array(planes * BACK, BZ), array(*line_shap...  1.58 us
  transfers between devices with their start and end apart: 8, of which 4 were waited for; matrix products, arithmetic and copies ran while one was open for 1% of the time, Pallas kernels for 7%

profile of v5, /device:TPU:8, one launch (start us, length us, event | category | flops | bytes accessed | tf_op | source)
XLA Modules:
  0.0 70.4 jit_solution(16397375680964197168)
XLA Ops:
  0.0 0.0 copy-start.1
  0.7 3.3 %head.1 = (f32[448,128]{1,0:T(8,128)}, f32[96,128]{1,0:T(8,128)}) custom-call(s32[1]{0:T(128)S(6)} %copy.7.counts_hbm, s32[1,128]{1,0:T(1,128)} %blocks_hbm.1, bf16[3,256,512]{2,1,0:T(8,128)(2,1)} %bitcast.13), custom_call_target="tpu_custom_call" | custom-call | tf_op jit(solution)/shard_map/head/pallas_call | solution.py:378
  4.0 10.2 %all-to-all-start = ((f32[32,14,1,128]{3,2,1,0:T(1,128)}), f32[32,14,1,128]{3,2,1,0:T(1,128)S(1)}, u32[]{:S(2)}, u32[]{:S(2)}) async-start(f32[32,14,1,128]{3,2,1,0:T(1,128)} %bitcast.15), calls=%async_computation | async-start | bytes 458752 | tf_op jit(solution)/shard_map/all_to_all | solution.py:327
  14.2 3.2 %collective-permute-start.2 = (f32[96,128]{1,0:T(8,128)}, f32[96,128]{1,0:T(8,128)S(1)}, u32[]{:S(2)}, u32[]{:S(2)}) collective-permute-start(f32[96,128]{1,0:T(8,128)} %get-tuple-element.14.mine), channel_id=1, source_target_pairs={{0,96},{32,64},{64,32},{96,0},{128,224},{160,192},{192,160},{224,1... | collective-permute-start | bytes 147464 | tf_op jit(solution)/shard_map/ppermute | solution.py:339
  17.4 3.0 %collective-permute-start.1 = (f32[96,128]{1,0:T(8,128)}, f32[96,128]{1,0:T(8,128)S(1)}, u32[]{:S(2)}, u32[]{:S(2)}) collective-permute-start(f32[96,128]{1,0:T(8,128)} %get-tuple-element.14.mine), channel_id=1, source_target_pairs={{0,64},{32,96},{64,0},{96,32},{128,192},{160,224},{192,128},{224,1... | collective-permute-start | bytes 147464 | tf_op jit(solution)/shard_map/ppermute | solution.py:339
  20.4 2.0 %collective-permute-start = (f32[96,128]{1,0:T(8,128)}, f32[96,128]{1,0:T(8,128)S(1)}, u32[]{:S(2)}, u32[]{:S(2)}) collective-permute-start(f32[96,128]{1,0:T(8,128)} %get-tuple-element.14.mine), channel_id=1, source_target_pairs={{0,32},{32,0},{64,96},{96,64},{128,160},{160,128},{192,224},{224,1... | collective-permute-start | bytes 147464 | tf_op jit(solution)/shard_map/ppermute | solution.py:339
  22.5 0.1 pad_add_fusion.place
  22.5 0.0 collective-permute-done.2.three
  22.5 1.3 %collective-permute-done.1.two = f32[96,128]{1,0:T(8,128)S(1)} collective-permute-done((f32[96,128]{1,0:T(8,128)}, f32[96,128]{1,0:T(8,128)S(1)}, u32[]{:S(2)}, u32[]{:S(2)}) %collective-permute-start.1) | collective-permute-done | bytes 49184 | tf_op jit(solution)/shard_map/ppermute | solution.py:339
  23.8 0.0 collective-permute-done.one
  23.8 0.8 %add_multiply_fusion.after.mine.half = f32[96,128]{1,0:T(8,128)S(1)} fusion(f32[96,128]{1,0:T(8,128)S(1)} %collective-permute-done.1.two, f32[96,128]{1,0:T(8,128)S(1)} %collective-permute-done.2.three, f32[96,128]{1,0:T(8,128)} %get-tuple-element.14.mine, f32[96,128]{1,0:T(8,128)S(1)} %collective-permute-done.one), kind=kLoop, calls=%fused_computation | loop fusion | flops 49152 | bytes 245760 | tf_op jit(solution)/shard_map/mul | solution.py:393
  24.7 1.2 %all-to-all-done = f32[32,14,1,128]{3,2,1,0:T(1,128)S(1)} async-done(((f32[32,14,1,128]{3,2,1,0:T(1,128)}), f32[32,14,1,128]{3,2,1,0:T(1,128)S(1)}, u32[]{:S(2)}, u32[]{:S(2)}) %all-to-all-start) | async-done | bytes 229408 | tf_op jit(solution)/shard_map/all_to_all | solution.py:327
  25.9 1.4 %plane.1 = (f32[416,128]{1,0:T(8,128)S(1)}, f32[16,16,128]{2,1,0:T(8,128)}) custom-call(s32[2]{0:T(128)S(1)} %pad_add_fusion.place, f32[448,128]{1,0:T(8,128)S(1)} %bitcast.9, f32[96,128]{1,0:T(8,128)S(1)} %add_multiply_fusion.after.mine.half), custom_call_target="tpu_custom_call" | custom-call | tf_op jit(solution)/shard_map/plane/pallas_call | solution.py:394
  27.3 10.4 %all-to-all-start.1 = ((f32[16,16,128]{2,1,0:T(8,128)}), f32[16,16,128]{2,1,0:T(8,128)S(1)}, u32[]{:S(2)}, u32[]{:S(2)}) async-start(f32[16,16,128]{2,1,0:T(8,128)} %get-tuple-element.15.after), calls=%async_computation.1 | async-start | bytes 262144 | tf_op jit(solution)/shard_map/all_to_all | solution.py:327
  37.7 4.7 %collective-permute-start.3 = (f32[96,128]{1,0:T(8,128)S(1)}, f32[96,128]{1,0:T(8,128)S(1)}, u32[]{:S(2)}, u32[]{:S(2)}) collective-permute-start(f32[96,128]{1,0:T(8,128)S(1)} %add_multiply_fusion.after.mine.half), channel_id=1, source_target_pairs={{0,128},{32,160},{64,192},{96,224},{128,0},{160,32},{192,64},{224,... | collective-permute-start | bytes 147464 | tf_op jit(solution)/shard_map/ppermute | solution.py:339
  42.4 0.0 copy-done.1
  42.4 4.1 %details.1.after.detail = f32[3,256,512]{2,1,0:T(8,128)S(1)} custom-call(s32[2]{0:T(128)S(1)} %pad_add_fusion.place, f32[448,128]{1,0:T(8,128)S(1)} %bitcast.10, bf16[3,256,512]{2,1,0:T(8,128)(2,1)S(1)} %bitcast.14, f32[16,16,128]{2,1,0:T(8,128)} %get-tuple-element.15.after), custom_call_target="tpu_custom_call" | custom-call | flops 1409286144 | bytes 3932160 | tf_op jit(solution)/shard_map/details/pallas_call | solution.py:402
  46.5 0.0 copy-start.2
  46.5 0.0 copy-start
  46.5 0.0 collective-permute-done.3.other
  46.5 0.0 all-to-all-done.1.gathered
  46.6 1.6 %corner.1 = (f32[416,128]{1,0:T(8,128)}, f32[96,128]{1,0:T(8,128)S(1)}) custom-call(s32[2]{0:T(128)S(1)} %pad_add_fusion.place, f32[16,16,128]{2,1,0:T(8,128)S(1)} %all-to-all-done.1.gathered, f32[416,128]{1,0:T(8,128)S(1)} %get-tuple-element.16.back_in, f32[96,128]{1,0:T(8,128)S(1)} %add_multiply_fusion.after.mine.half, ...), custom_call_target="tpu_custom_call" | custom-call | tf_op jit(solution)/shard_map/corner/pallas_call | solution.py:409
  48.1 7.7 %all-to-all-start.2 = ((f32[32,13,1,128]{3,2,1,0:T(1,128)}), f32[32,13,1,128]{3,2,1,0:T(1,128)S(1)}, u32[]{:S(2)}, u32[]{:S(2)}) async-start(f32[32,13,1,128]{3,2,1,0:T(1,128)} %bitcast.5), calls=%async_computation.2 | async-start | bytes 425984 | tf_op jit(solution)/shard_map/all_to_all | solution.py:327
  55.8 6.5 %collective-permute-start.4 = (f32[96,128]{1,0:T(8,128)S(1)}, f32[96,128]{1,0:T(8,128)S(1)}, u32[]{:S(2)}, u32[]{:S(2)}) collective-permute-start(f32[96,128]{1,0:T(8,128)S(1)} %get-tuple-element.18.after.mine), channel_id=1, source_target_pairs={{0,256},{32,288},{64,320},{96,352},{128,384},{160,416},{192,448},{... | collective-permute-start | bytes 147464 | tf_op jit(solution)/shard_map/ppermute | solution.py:339
  62.4 0.0 copy-done.2
  62.4 0.7 line.1
  63.1 2.7 %collective-permute-done.4.other = f32[96,128]{1,0:T(8,128)S(1)} collective-permute-done((f32[96,128]{1,0:T(8,128)S(1)}, f32[96,128]{1,0:T(8,128)S(1)}, u32[]{:S(2)}, u32[]{:S(2)}) %collective-permute-start.4) | collective-permute-done | bytes 49184 | tf_op jit(solution)/shard_map/ppermute | solution.py:339
  65.7 2.5 %all-to-all-done.2 = f32[32,13,1,128]{3,2,1,0:T(1,128)S(1)} async-done(((f32[32,13,1,128]{3,2,1,0:T(1,128)}), f32[32,13,1,128]{3,2,1,0:T(1,128)S(1)}, u32[]{:S(2)}, u32[]{:S(2)}) %all-to-all-start.2) | async-done | bytes 213024 | tf_op jit(solution)/shard_map/all_to_all | solution.py:327
  68.2 0.0 copy-done
  68.2 2.2 %finish.1 = bf16[3,256,512]{2,1,0:T(8,128)(2,1)} custom-call(f32[416,128]{1,0:T(8,128)S(1)} %bitcast.11, f32[96,128]{1,0:T(8,128)S(1)} %get-tuple-element.18.after.mine, f32[96,128]{1,0:T(8,128)S(1)} %collective-permute-done.4.other, f32[96,128]{1,0:T(8,128)S(1)} %get-tuple-element.19.partial, f32[8,512]{1,0:T(8,128)S(1)} %get-tuple-element.20.mask, ...), custom_call_target="tpu_custom_call" | custom-call | tf_op jit(solution)/shard_map/finish/pallas_call | solution.py:423
Async XLA Ops:
  0.0 42.4 %copy-start.1 = (bf16[3,32,8,512]{3,2,1,0:T(8,128)(2,1)S(1)}, bf16[3,32,8,512]{3,2,1,0:T(8,128)(2,1)}, u32[]{:S(2)}) copy-start(bf16[3,32,8,512]{3,2,1,0:T(8,128)(2,1)} %param.4) | copy-start | bytes 2359300
  4.0 21.8 %all-to-all-start = ((f32[32,14,1,128]{3,2,1,0:T(1,128)}), f32[32,14,1,128]{3,2,1,0:T(1,128)S(1)}, u32[]{:S(2)}, u32[]{:S(2)}) async-start(f32[32,14,1,128]{3,2,1,0:T(1,128)} %bitcast.15), calls=%async_computation | async-start | bytes 458752 | tf_op jit(solution)/shard_map/all_to_all | solution.py:327
  14.2 8.3 %collective-permute-start.2 = (f32[96,128]{1,0:T(8,128)}, f32[96,128]{1,0:T(8,128)S(1)}, u32[]{:S(2)}, u32[]{:S(2)}) collective-permute-start(f32[96,128]{1,0:T(8,128)} %get-tuple-element.14.mine), channel_id=1, source_target_pairs={{0,96},{32,64},{64,32},{96,0},{128,224},{160,192},{192,160},{224,1... | collective-permute-start | bytes 147464 | tf_op jit(solution)/shard_map/ppermute | solution.py:339
  17.4 6.5 %collective-permute-start.1 = (f32[96,128]{1,0:T(8,128)}, f32[96,128]{1,0:T(8,128)S(1)}, u32[]{:S(2)}, u32[]{:S(2)}) collective-permute-start(f32[96,128]{1,0:T(8,128)} %get-tuple-element.14.mine), channel_id=1, source_target_pairs={{0,64},{32,96},{64,0},{96,32},{128,192},{160,224},{192,128},{224,1... | collective-permute-start | bytes 147464 | tf_op jit(solution)/shard_map/ppermute | solution.py:339
  20.4 3.4 %collective-permute-start = (f32[96,128]{1,0:T(8,128)}, f32[96,128]{1,0:T(8,128)S(1)}, u32[]{:S(2)}, u32[]{:S(2)}) collective-permute-start(f32[96,128]{1,0:T(8,128)} %get-tuple-element.14.mine), channel_id=1, source_target_pairs={{0,32},{32,0},{64,96},{96,64},{128,160},{160,128},{192,224},{224,1... | collective-permute-start | bytes 147464 | tf_op jit(solution)/shard_map/ppermute | solution.py:339
  27.3 19.3 %all-to-all-start.1 = ((f32[16,16,128]{2,1,0:T(8,128)}), f32[16,16,128]{2,1,0:T(8,128)S(1)}, u32[]{:S(2)}, u32[]{:S(2)}) async-start(f32[16,16,128]{2,1,0:T(8,128)} %get-tuple-element.15.after), calls=%async_computation.1 | async-start | bytes 262144 | tf_op jit(solution)/shard_map/all_to_all | solution.py:327
  37.7 8.8 %collective-permute-start.3 = (f32[96,128]{1,0:T(8,128)S(1)}, f32[96,128]{1,0:T(8,128)S(1)}, u32[]{:S(2)}, u32[]{:S(2)}) collective-permute-start(f32[96,128]{1,0:T(8,128)S(1)} %add_multiply_fusion.after.mine.half), channel_id=1, source_target_pairs={{0,128},{32,160},{64,192},{96,224},{128,0},{160,32},{192,64},{224,... | collective-permute-start | bytes 147464 | tf_op jit(solution)/shard_map/ppermute | solution.py:339
  46.5 15.9 %copy-start.2 = (f32[96,128]{1,0:T(8,128)S(1)}, f32[96,128]{1,0:T(8,128)}, u32[]{:S(2)}) copy-start(f32[96,128]{1,0:T(8,128)} %get-tuple-element.14.mine) | copy-start | bytes 147460
  46.5 21.7 %copy-start = (bf16[3,32,8,512]{3,2,1,0:T(8,128)(2,1)S(1)}, bf16[3,32,8,512]{3,2,1,0:T(8,128)(2,1)}, u32[]{:S(2)}) copy-start(bf16[3,32,8,512]{3,2,1,0:T(8,128)(2,1)} %param.5) | copy-start | bytes 2359300
  48.1 20.0 %all-to-all-start.2 = ((f32[32,13,1,128]{3,2,1,0:T(1,128)}), f32[32,13,1,128]{3,2,1,0:T(1,128)S(1)}, u32[]{:S(2)}, u32[]{:S(2)}) async-start(f32[32,13,1,128]{3,2,1,0:T(1,128)} %bitcast.5), calls=%async_computation.2 | async-start | bytes 425984 | tf_op jit(solution)/shard_map/all_to_all | solution.py:327
  55.8 9.9 %collective-permute-start.4 = (f32[96,128]{1,0:T(8,128)S(1)}, f32[96,128]{1,0:T(8,128)S(1)}, u32[]{:S(2)}, u32[]{:S(2)}) collective-permute-start(f32[96,128]{1,0:T(8,128)S(1)} %get-tuple-element.18.after.mine), channel_id=1, source_target_pairs={{0,256},{32,288},{64,320},{96,352},{128,384},{160,416},{192,448},{... | collective-permute-start | bytes 147464 | tf_op jit(solution)/shard_map/ppermute | solution.py:339

commit v6 on v5

--- a/solution.py
+++ b/solution.py
@@ -19,6 +19,7 @@
 HALF = 64
 LINE_KEPT = 52
 PACKED = 16
+PIECES = 4
 F32 = jnp.float32
 BF16 = jnp.bfloat16
 
@@ -120,13 +121,23 @@
 def head_kernel(counts_hbm, blocks_hbm, vort_hbm, send, line, counts, blocks, vort, sems):
     parts, cells, wide = vort.shape
     planes = cells // BY
-    copies = [
-        pltpu.make_async_copy(vort_hbm.at[c], vort.at[c], sems.at[c]) for c in range(parts)
+    lists = [
+        pltpu.make_async_copy(blocks_hbm, blocks, sems.at[parts * PIECES]),
+        pltpu.make_async_copy(counts_hbm, counts, sems.at[parts * PIECES + 1]),
     ]
-    copies.append(pltpu.make_async_copy(blocks_hbm, blocks, sems.at[parts]))
-    copies.append(pltpu.make_async_copy(counts_hbm, counts, sems.at[parts + 1]))
-    for copy in reversed(copies):
+    for copy in lists:
         copy.start()
+    copies = []
+    size = cells // PIECES
+    for c in range(parts):
+        for piece in range(PIECES):
+            part = pl.ds(piece * size, size)
+            copies.append(
+                pltpu.make_async_copy(
+                    vort_hbm.at[c, part, :], vort.at[c, part, :], sems.at[len(copies)]
+                )
+            )
+            copies[-1].start()
     row, column = iota((planes + BY, cells), 0), iota((planes + BY, cells), 1)
     fine = jnp.where(row - planes == column & (BY - 1), 1.0, 0.0) - 1.0 / BY
     table = jnp.where(
@@ -135,8 +146,8 @@
         fine * (1.0 / planes),
     ).astype(BF16)
     mix = mix_table(wide)
-    copies[parts].wait()
-    copies[parts + 1].wait()
+    for copy in lists:
+        copy.wait()
     nblocks = blocks.shape[1]
     square = (nblocks, nblocks)
     listed = (blocks[...] == iota(square, 0)) & (iota(square, 1) < counts[0])
@@ -150,7 +161,8 @@
     lane, turn = iota((8, BZ), 1), iota((8, BZ), 0)
     extra = [jnp.zeros((8, BZ), F32) for zb in range(ZB)]
     for c in range(parts):
-        copies[c].wait()
+        for piece in range(PIECES):
+            copies[c * PIECES + piece].wait()
         rows = remix(jnp.dot(table, vort[c], preferred_element_type=F32), mix)
         for zb in range(ZB):
             chunk = c * ZB + zb
@@ -269,7 +281,7 @@
         total[span, :] = result
 
 
-def finish_kernel(got, mine, other, partial, mask, detail, velocity, out_hbm, rows, out, sems):
+def finish_kernel(got, mine, other, partial, mask, detail, velocity, out_hbm, rows, line, out, sems):
     planes = got.shape[0] // BACK
     parts, cells, wide = velocity.shape
     inverse = level_tables(planes)[1]
@@ -287,7 +299,7 @@
             last = (mine[span, :] - other[span, :]) * 0.5
             mean = (mine[span, :] + other[span, :]) * 0.5
             total = partial[span, :] + last * mask[4:5, lanes] + mean * mask[0:1, lanes]
-            rows[parts * planes + c * BY : parts * planes + (c + 1) * BY, lanes] = total
+            line[c * BY : (c + 1) * BY, lanes] = total
             corner = jnp.where(lane >> 4 == (slot + c) & 7, turned[zb], 0.0)
             corner = jnp.sum(corner, axis=0, keepdims=True)
             corner = pltpu.roll(corner, BZ - c * SLICE, 1) if c else corner
@@ -296,14 +308,16 @@
         rows[c * planes : (c + 1) * planes, :] = left_product(
             inverse, jnp.concatenate(columns, axis=1)
         )
-    rows[...] = remix(rows[...], unmix_table(wide))
+    unmix = unmix_table(wide)
+    line[...] = remix(line[...], unmix)
+    rows[...] = remix(rows[...], unmix)
     copies = []
     for x in range(planes):
         span = slice(x * BY, (x + 1) * BY)
         smooth = [
             detail[c, span, :]
             + rows[c * planes + x : c * planes + x + 1, :]
-            + rows[parts * planes + c * BY : parts * planes + (c + 1) * BY, :]
+            + line[c * BY : (c + 1) * BY, :]
             for c in range(parts)
         ]
         speed = [velocity[c, span, :].astype(F32) for c in range(parts)]
@@ -384,7 +398,7 @@
             pltpu.SMEM(counts.shape, jnp.int32),
             pltpu.VMEM(blocks.shape, jnp.int32),
             vort_scratch,
-            pltpu.SemaphoreType.DMA((parts + 2,)),
+            pltpu.SemaphoreType.DMA((parts * PIECES + 2,)),
         ],
         params=pltpu.CompilerParams(vmem_limit_bytes=60 * 1024 * 1024),
     )(counts, blocks, vort)
@@ -426,7 +440,8 @@
         jax.ShapeDtypeStruct((parts, cells, wide), BF16),
         [vmem] * 7,
         [
-            pltpu.VMEM((parts * (planes + tall), wide), F32),
+            pltpu.VMEM((parts * planes, wide), F32),
+            pltpu.VMEM((parts * tall, wide), F32),
             pltpu.VMEM((parts, cells, wide), BF16),
             pltpu.SemaphoreType.DMA((parts * planes // 8,)),
         ],

time: 70.9 us -> 70.5 us (level)
  no operation moved by 1% of the time
where the time goes in v6:
time: 70.5 us; the launch traced here: 69.9 us
  starting transfers between devices  47.7 us (68%)
  Pallas kernels  12.8 us (18%)
  waiting for transfers between devices  7.6 us (11%)
  other arithmetic  0.89 us (1%)
  between operations  0.86 us (1%)
    all_to_all x3, starting transfers between devices, exchange(): return lax.all_to_all(value, axis, split_axis=0, concat_axis=0, tiled=True)  28.3 us
    ppermute x5, starting transfers between devices, from_partner(): return lax.ppermute(value, 'gx', pairs)  19.5 us
    pallas_call x1, Pallas kernels, body(): call(details_kernel, 'details', array(parts, cells, wide), [smem, vmem, v...  4.08 us
    ppermute x5, waiting for transfers between devices, from_partner(): return lax.ppermute(value, 'gx', pairs)  3.95 us
    all_to_all x3, waiting for transfers between devices, exchange(): return lax.all_to_all(value, axis, split_axis=0, concat_axis=0, tiled=True)  3.65 us
    pallas_call x1, Pallas kernels, body(): call(head_kernel, 'head', (array(planes * ROWS, BZ), array(*line_shape)),...  3.21 us
    pallas_call x1, Pallas kernels, body(): call(finish_kernel, 'finish', jax.ShapeDtypeStruct((parts, cells, wide),...  1.81 us
    pallas_call x1, Pallas kernels, body(): call(corner_kernel, 'corner', (array(planes * BACK, BZ), array(*line_shap...  1.58 us
  transfers between devices with their start and end apart: 8, of which 4 were waited for; matrix products, arithmetic and copies ran while one was open for 1% of the time, Pallas kernels for 7%

profile of v6, /device:TPU:8, one launch (start us, length us, event | category | flops | bytes accessed | tf_op | source)
XLA Modules:
  0.0 69.9 jit_solution(13263357671810052353)
XLA Ops:
  0.0 0.0 copy-start.1
  0.7 3.2 %head.1 = (f32[448,128]{1,0:T(8,128)}, f32[96,128]{1,0:T(8,128)}) custom-call(s32[1]{0:T(128)S(6)} %copy.7.counts_hbm, s32[1,128]{1,0:T(1,128)} %blocks_hbm.1, bf16[3,256,512]{2,1,0:T(8,128)(2,1)} %bitcast.13), custom_call_target="tpu_custom_call" | custom-call | tf_op jit(solution)/shard_map/head/pallas_call | solution.py:392
  3.9 10.2 %all-to-all-start = ((f32[32,14,1,128]{3,2,1,0:T(1,128)}), f32[32,14,1,128]{3,2,1,0:T(1,128)S(1)}, u32[]{:S(2)}, u32[]{:S(2)}) async-start(f32[32,14,1,128]{3,2,1,0:T(1,128)} %bitcast.15), calls=%async_computation | async-start | bytes 458752 | tf_op jit(solution)/shard_map/all_to_all | solution.py:341
  14.1 3.2 %collective-permute-start.2 = (f32[96,128]{1,0:T(8,128)}, f32[96,128]{1,0:T(8,128)S(1)}, u32[]{:S(2)}, u32[]{:S(2)}) collective-permute-start(f32[96,128]{1,0:T(8,128)} %get-tuple-element.14.mine), channel_id=1, source_target_pairs={{0,96},{32,64},{64,32},{96,0},{128,224},{160,192},{192,160},{224,1... | collective-permute-start | bytes 147464 | tf_op jit(solution)/shard_map/ppermute | solution.py:353
  17.3 3.0 %collective-permute-start.1 = (f32[96,128]{1,0:T(8,128)}, f32[96,128]{1,0:T(8,128)S(1)}, u32[]{:S(2)}, u32[]{:S(2)}) collective-permute-start(f32[96,128]{1,0:T(8,128)} %get-tuple-element.14.mine), channel_id=1, source_target_pairs={{0,64},{32,96},{64,0},{96,32},{128,192},{160,224},{192,128},{224,1... | collective-permute-start | bytes 147464 | tf_op jit(solution)/shard_map/ppermute | solution.py:353
  20.3 2.0 %collective-permute-start = (f32[96,128]{1,0:T(8,128)}, f32[96,128]{1,0:T(8,128)S(1)}, u32[]{:S(2)}, u32[]{:S(2)}) collective-permute-start(f32[96,128]{1,0:T(8,128)} %get-tuple-element.14.mine), channel_id=1, source_target_pairs={{0,32},{32,0},{64,96},{96,64},{128,160},{160,128},{192,224},{224,1... | collective-permute-start | bytes 147464 | tf_op jit(solution)/shard_map/ppermute | solution.py:353
  22.4 0.1 pad_add_fusion.place
  22.5 0.0 collective-permute-done.2.three
  22.5 1.3 %collective-permute-done.1.two = f32[96,128]{1,0:T(8,128)S(1)} collective-permute-done((f32[96,128]{1,0:T(8,128)}, f32[96,128]{1,0:T(8,128)S(1)}, u32[]{:S(2)}, u32[]{:S(2)}) %collective-permute-start.1) | collective-permute-done | bytes 49184 | tf_op jit(solution)/shard_map/ppermute | solution.py:353
  23.7 0.0 collective-permute-done.one
  23.8 0.8 %add_multiply_fusion.after.mine.half = f32[96,128]{1,0:T(8,128)S(1)} fusion(f32[96,128]{1,0:T(8,128)S(1)} %collective-permute-done.1.two, f32[96,128]{1,0:T(8,128)S(1)} %collective-permute-done.2.three, f32[96,128]{1,0:T(8,128)} %get-tuple-element.14.mine, f32[96,128]{1,0:T(8,128)S(1)} %collective-permute-done.one), kind=kLoop, calls=%fused_computation | loop fusion | flops 49152 | bytes 245760 | tf_op jit(solution)/shard_map/mul | solution.py:407
  24.6 1.2 %all-to-all-done = f32[32,14,1,128]{3,2,1,0:T(1,128)S(1)} async-done(((f32[32,14,1,128]{3,2,1,0:T(1,128)}), f32[32,14,1,128]{3,2,1,0:T(1,128)S(1)}, u32[]{:S(2)}, u32[]{:S(2)}) %all-to-all-start) | async-done | bytes 229408 | tf_op jit(solution)/shard_map/all_to_all | solution.py:341
  25.8 1.4 %plane.1 = (f32[416,128]{1,0:T(8,128)S(1)}, f32[16,16,128]{2,1,0:T(8,128)}) custom-call(s32[2]{0:T(128)S(1)} %pad_add_fusion.place, f32[448,128]{1,0:T(8,128)S(1)} %bitcast.9, f32[96,128]{1,0:T(8,128)S(1)} %add_multiply_fusion.after.mine.half), custom_call_target="tpu_custom_call" | custom-call | tf_op jit(solution)/shard_map/plane/pallas_call | solution.py:408
  27.2 10.4 %all-to-all-start.1 = ((f32[16,16,128]{2,1,0:T(8,128)}), f32[16,16,128]{2,1,0:T(8,128)S(1)}, u32[]{:S(2)}, u32[]{:S(2)}) async-start(f32[16,16,128]{2,1,0:T(8,128)} %get-tuple-element.15.after), calls=%async_computation.1 | async-start | bytes 262144 | tf_op jit(solution)/shard_map/all_to_all | solution.py:341
  37.6 4.7 %collective-permute-start.3 = (f32[96,128]{1,0:T(8,128)S(1)}, f32[96,128]{1,0:T(8,128)S(1)}, u32[]{:S(2)}, u32[]{:S(2)}) collective-permute-start(f32[96,128]{1,0:T(8,128)S(1)} %add_multiply_fusion.after.mine.half), channel_id=1, source_target_pairs={{0,128},{32,160},{64,192},{96,224},{128,0},{160,32},{192,64},{224,... | collective-permute-start | bytes 147464 | tf_op jit(solution)/shard_map/ppermute | solution.py:353
  42.4 0.0 copy-done.1
  42.4 4.1 %details.1.after.detail = f32[3,256,512]{2,1,0:T(8,128)S(1)} custom-call(s32[2]{0:T(128)S(1)} %pad_add_fusion.place, f32[448,128]{1,0:T(8,128)S(1)} %bitcast.10, bf16[3,256,512]{2,1,0:T(8,128)(2,1)S(1)} %bitcast.14, f32[16,16,128]{2,1,0:T(8,128)} %get-tuple-element.15.after), custom_call_target="tpu_custom_call" | custom-call | flops 1409286144 | bytes 3932160 | tf_op jit(solution)/shard_map/details/pallas_call | solution.py:416
  46.4 0.0 copy-start.2
  46.4 0.0 copy-start
  46.5 0.0 collective-permute-done.3.other
  46.5 0.0 all-to-all-done.1.gathered
  46.5 1.6 %corner.1 = (f32[416,128]{1,0:T(8,128)}, f32[96,128]{1,0:T(8,128)S(1)}) custom-call(s32[2]{0:T(128)S(1)} %pad_add_fusion.place, f32[16,16,128]{2,1,0:T(8,128)S(1)} %all-to-all-done.1.gathered, f32[416,128]{1,0:T(8,128)S(1)} %get-tuple-element.16.back_in, f32[96,128]{1,0:T(8,128)S(1)} %add_multiply_fusion.after.mine.half, ...), custom_call_target="tpu_custom_call" | custom-call | tf_op jit(solution)/shard_map/corner/pallas_call | solution.py:423
  48.1 7.7 %all-to-all-start.2 = ((f32[32,13,1,128]{3,2,1,0:T(1,128)}), f32[32,13,1,128]{3,2,1,0:T(1,128)S(1)}, u32[]{:S(2)}, u32[]{:S(2)}) async-start(f32[32,13,1,128]{3,2,1,0:T(1,128)} %bitcast.5), calls=%async_computation.2 | async-start | bytes 425984 | tf_op jit(solution)/shard_map/all_to_all | solution.py:341
  55.8 6.5 %collective-permute-start.4 = (f32[96,128]{1,0:T(8,128)S(1)}, f32[96,128]{1,0:T(8,128)S(1)}, u32[]{:S(2)}, u32[]{:S(2)}) collective-permute-start(f32[96,128]{1,0:T(8,128)S(1)} %get-tuple-element.18.after.mine), channel_id=1, source_target_pairs={{0,256},{32,288},{64,320},{96,352},{128,384},{160,416},{192,448},{... | collective-permute-start | bytes 147464 | tf_op jit(solution)/shard_map/ppermute | solution.py:353
  62.3 0.0 copy-done.2
  62.3 0.7 %line.1 = (f32[96,128]{1,0:T(8,128)S(1)}, f32[8,512]{1,0:T(8,128)S(1)}) custom-call(s32[2]{0:T(128)S(1)} %pad_add_fusion.place, f32[16,16,128]{2,1,0:T(8,128)S(1)} %all-to-all-done.1.gathered, f32[96,128]{1,0:T(8,128)S(1)} %get-tuple-element.18.after.mine, f32[96,128]{1,0:T(8,128)S(1)} %copy-done.2, f32[96,128]{1,0:T(8,128)S(1)} %collective-permute-done.one, ...), custom_call_target="tpu_custom_call" | custom-call | tf_op jit(solution)/shard_map/line/pallas_call | solution.py:431
  63.0 2.7 %collective-permute-done.4.other = f32[96,128]{1,0:T(8,128)S(1)} collective-permute-done((f32[96,128]{1,0:T(8,128)S(1)}, f32[96,128]{1,0:T(8,128)S(1)}, u32[]{:S(2)}, u32[]{:S(2)}) %collective-permute-start.4) | collective-permute-done | bytes 49184 | tf_op jit(solution)/shard_map/ppermute | solution.py:353
  65.6 2.4 %all-to-all-done.2 = f32[32,13,1,128]{3,2,1,0:T(1,128)S(1)} async-done(((f32[32,13,1,128]{3,2,1,0:T(1,128)}), f32[32,13,1,128]{3,2,1,0:T(1,128)S(1)}, u32[]{:S(2)}, u32[]{:S(2)}) %all-to-all-start.2) | async-done | bytes 213024 | tf_op jit(solution)/shard_map/all_to_all | solution.py:341
  68.1 0.0 copy-done
  68.1 1.8 %finish.1 = bf16[3,256,512]{2,1,0:T(8,128)(2,1)} custom-call(f32[416,128]{1,0:T(8,128)S(1)} %bitcast.11, f32[96,128]{1,0:T(8,128)S(1)} %get-tuple-element.18.after.mine, f32[96,128]{1,0:T(8,128)S(1)} %collective-permute-done.4.other, f32[96,128]{1,0:T(8,128)S(1)} %get-tuple-element.19.partial, f32[8,512]{1,0:T(8,128)S(1)} %get-tuple-element.20.mask, ...), custom_call_target="tpu_custom_call" | custom-call | tf_op jit(solution)/shard_map/finish/pallas_call | solution.py:437
Async XLA Ops:
  0.0 42.4 %copy-start.1 = (bf16[3,32,8,512]{3,2,1,0:T(8,128)(2,1)S(1)}, bf16[3,32,8,512]{3,2,1,0:T(8,128)(2,1)}, u32[]{:S(2)}) copy-start(bf16[3,32,8,512]{3,2,1,0:T(8,128)(2,1)} %param.4) | copy-start | bytes 2359300
  3.9 21.8 %all-to-all-start = ((f32[32,14,1,128]{3,2,1,0:T(1,128)}), f32[32,14,1,128]{3,2,1,0:T(1,128)S(1)}, u32[]{:S(2)}, u32[]{:S(2)}) async-start(f32[32,14,1,128]{3,2,1,0:T(1,128)} %bitcast.15), calls=%async_computation | async-start | bytes 458752 | tf_op jit(solution)/shard_map/all_to_all | solution.py:341
  14.1 8.3 %collective-permute-start.2 = (f32[96,128]{1,0:T(8,128)}, f32[96,128]{1,0:T(8,128)S(1)}, u32[]{:S(2)}, u32[]{:S(2)}) collective-permute-start(f32[96,128]{1,0:T(8,128)} %get-tuple-element.14.mine), channel_id=1, source_target_pairs={{0,96},{32,64},{64,32},{96,0},{128,224},{160,192},{192,160},{224,1... | collective-permute-start | bytes 147464 | tf_op jit(solution)/shard_map/ppermute | solution.py:353
  17.3 6.5 %collective-permute-start.1 = (f32[96,128]{1,0:T(8,128)}, f32[96,128]{1,0:T(8,128)S(1)}, u32[]{:S(2)}, u32[]{:S(2)}) collective-permute-start(f32[96,128]{1,0:T(8,128)} %get-tuple-element.14.mine), channel_id=1, source_target_pairs={{0,64},{32,96},{64,0},{96,32},{128,192},{160,224},{192,128},{224,1... | collective-permute-start | bytes 147464 | tf_op jit(solution)/shard_map/ppermute | solution.py:353
  20.3 3.4 %collective-permute-start = (f32[96,128]{1,0:T(8,128)}, f32[96,128]{1,0:T(8,128)S(1)}, u32[]{:S(2)}, u32[]{:S(2)}) collective-permute-start(f32[96,128]{1,0:T(8,128)} %get-tuple-element.14.mine), channel_id=1, source_target_pairs={{0,32},{32,0},{64,96},{96,64},{128,160},{160,128},{192,224},{224,1... | collective-permute-start | bytes 147464 | tf_op jit(solution)/shard_map/ppermute | solution.py:353
  27.2 19.3 %all-to-all-start.1 = ((f32[16,16,128]{2,1,0:T(8,128)}), f32[16,16,128]{2,1,0:T(8,128)S(1)}, u32[]{:S(2)}, u32[]{:S(2)}) async-start(f32[16,16,128]{2,1,0:T(8,128)} %get-tuple-element.15.after), calls=%async_computation.1 | async-start | bytes 262144 | tf_op jit(solution)/shard_map/all_to_all | solution.py:341
  37.6 8.8 %collective-permute-start.3 = (f32[96,128]{1,0:T(8,128)S(1)}, f32[96,128]{1,0:T(8,128)S(1)}, u32[]{:S(2)}, u32[]{:S(2)}) collective-permute-start(f32[96,128]{1,0:T(8,128)S(1)} %add_multiply_fusion.after.mine.half), channel_id=1, source_target_pairs={{0,128},{32,160},{64,192},{96,224},{128,0},{160,32},{192,64},{224,... | collective-permute-start | bytes 147464 | tf_op jit(solution)/shard_map/ppermute | solution.py:353
  46.4 15.8 %copy-start.2 = (f32[96,128]{1,0:T(8,128)S(1)}, f32[96,128]{1,0:T(8,128)}, u32[]{:S(2)}) copy-start(f32[96,128]{1,0:T(8,128)} %get-tuple-element.14.mine) | copy-start | bytes 147460
  46.4 21.6 %copy-start = (bf16[3,32,8,512]{3,2,1,0:T(8,128)(2,1)S(1)}, bf16[3,32,8,512]{3,2,1,0:T(8,128)(2,1)}, u32[]{:S(2)}) copy-start(bf16[3,32,8,512]{3,2,1,0:T(8,128)(2,1)} %param.5) | copy-start | bytes 2359300
  48.1 20.0 %all-to-all-start.2 = ((f32[32,13,1,128]{3,2,1,0:T(1,128)}), f32[32,13,1,128]{3,2,1,0:T(1,128)S(1)}, u32[]{:S(2)}, u32[]{:S(2)}) async-start(f32[32,13,1,128]{3,2,1,0:T(1,128)} %bitcast.5), calls=%async_computation.2 | async-start | bytes 425984 | tf_op jit(solution)/shard_map/all_to_all | solution.py:341
  55.8 9.9 %collective-permute-start.4 = (f32[96,128]{1,0:T(8,128)S(1)}, f32[96,128]{1,0:T(8,128)S(1)}, u32[]{:S(2)}, u32[]{:S(2)}) collective-permute-start(f32[96,128]{1,0:T(8,128)S(1)} %get-tuple-element.18.after.mine), channel_id=1, source_target_pairs={{0,256},{32,288},{64,320},{96,352},{128,384},{160,416},{192,448},{... | collective-permute-start | bytes 147464 | tf_op jit(solution)/shard_map/ppermute | solution.py:353

commit v7 on v6

--- a/solution.py
+++ b/solution.py
@@ -187,10 +187,10 @@
     return forward, inverse
 
 
-def plane_kernel(place, recv, after, back, corner):
+def pack_kernel(place, recv, after, corner):
     del after
     planes = recv.shape[0] // ROWS
-    forward, inverse = level_tables(planes)
+    forward = level_tables(planes)[0]
     extra = recv[pl.ds(EXTRA, planes, stride=ROWS), :]
     lane = iota((PACKED, BZ), 1)
     row = iota((PACKED, BZ), 0)
@@ -208,6 +208,12 @@
     packed = packed + jnp.dot(own, slot, preferred_element_type=F32)
     for g in range(corner.shape[0]):
         corner[g] = packed
+
+
+def plane_kernel(place, recv, after, back):
+    del after
+    planes = recv.shape[0] // ROWS
+    forward, inverse = level_tables(planes)
     pick = jnp.where(iota((BZ, ZB * BZ), 0) & 3 == iota((BZ, ZB * BZ), 1) >> 7, 1.0, 0.0)
     own = recv[pl.ds(place[1] * ROWS + KEPT, 1), :]
     spread = jnp.where(iota((planes, BZ), 1) >> 2 == iota((planes, BZ), 0), own, 0.0)
@@ -243,8 +249,7 @@
         detail[c] = remix(left_product(inverse, rows * mask), unmix)
 
 
-def corner_kernel(place, gathered, back_in, mine, other, after, back, means):
-    del after
+def corner_kernel(place, gathered, back_in, mine, other, back, means):
     means[...] = (mine[...] + other[...]) * 0.5
     slabs = gathered.shape[0]
     planes = back.shape[0] // BACK
@@ -405,27 +410,20 @@
     recv = over_yz(send, planes)
     near = [from_partner(line, distance) for distance in (1, 2, 3)]
     half = (line + near[0] + (near[1] + near[2])) * 0.25
-    back, corner = call(
-        plane_kernel,
-        "plane",
-        (array(planes * BACK, BZ), array(slabs, PACKED, BZ)),
-        [smem, vmem, loose],
+    corner = call(
+        pack_kernel, "pack", array(slabs, PACKED, BZ), [smem, vmem, loose]
     )(place, recv, half)
     gathered = exchange(corner, "gx")
     opposite = from_partner(half, 4)
-    detail = call(
-        details_kernel,
-        "details",
-        array(parts, cells, wide),
-        [smem, vmem, vmem, loose],
-        cost=cost(7),
-    )(place, recv, vort, corner)
+    back = call(
+        plane_kernel, "plane", array(planes * BACK, BZ), [smem, vmem, loose]
+    )(place, recv, corner)
     back, means = call(
         corner_kernel,
         "corner",
         (array(planes * BACK, BZ), array(*line_shape)),
-        [smem] + [vmem] * 4 + [loose],
-    )(place, gathered, back, half, opposite, detail)
+        [smem] + [vmem] * 4,
+    )(place, gathered, back, half, opposite)
     got = over_yz(back, planes)
     other = from_partner(means, 8)
     partial, mask = call(
@@ -434,6 +432,13 @@
         (array(*line_shape), array(8, wide)),
         [smem, vmem, loose] + [vmem] * 6,
     )(place, gathered, means, line, *near, half, opposite)
+    detail = call(
+        details_kernel,
+        "details",
+        array(parts, cells, wide),
+        [smem, vmem, vmem, loose],
+        cost=cost(7),
+    )(place, recv, vort, partial)
     out = call(
         finish_kernel,
         "finish",

time: 70.5 us -> 70.9 us (level)
  the two profiles are of different devices: /device:TPU:8 before, /device:TPU:2 now
where the time goes in v7:
time: 70.9 us; the launch traced here: 70.2 us
  starting transfers between devices  49.1 us (69%)
  Pallas kernels  14 us (20%)
  waiting for transfers between devices  4.35 us (6%)
  local copies, waits for them, and re-layouts  1.14 us (2%)
  other arithmetic  0.89 us (1%)
  between operations  0.79 us (1%)
    all_to_all x3, starting transfers between devices, exchange(): return lax.all_to_all(value, axis, split_axis=0, concat_axis=0, tiled=True)  29.5 us
    ppermute x5, starting transfers between devices, from_partner(): return lax.ppermute(value, 'gx', pairs)  19.6 us
    pallas_call x1, Pallas kernels, body(): call(details_kernel, 'details', array(parts, cells, wide), [smem, vmem, v...  4.08 us
    ppermute x5, waiting for transfers between devices, from_partner(): return lax.ppermute(value, 'gx', pairs)  3.95 us
    pallas_call x1, Pallas kernels, body(): call(head_kernel, 'head', (array(planes * ROWS, BZ), array(*line_shape)),...  3.21 us
    pallas_call x1, Pallas kernels, body(): call(finish_kernel, 'finish', jax.ShapeDtypeStruct((parts, cells, wide),...  1.81 us
    pallas_call x1, Pallas kernels, body(): call(corner_kernel, 'corner', (array(planes * BACK, BZ), array(*line_shap...  1.58 us
  transfers between devices with their start and end apart: 8, of which 4 were waited for; matrix products, arithmetic and copies ran while one was open for 1% of the time, Pallas kernels for 8%

profile of v7, /device:TPU:2, one launch (start us, length us, event | category | flops | bytes accessed | tf_op | source)
XLA Modules:
  0.0 70.2 jit_solution(10053207903859970751)
XLA Ops:
  0.7 3.2 %head.1 = (f32[448,128]{1,0:T(8,128)}, f32[96,128]{1,0:T(8,128)}) custom-call(s32[1]{0:T(128)S(6)} %copy.7.counts_hbm, s32[1,128]{1,0:T(1,128)} %blocks_hbm.1, bf16[3,256,512]{2,1,0:T(8,128)(2,1)} %bitcast.14), custom_call_target="tpu_custom_call" | custom-call | tf_op jit(solution)/shard_map/head/pallas_call | solution.py:397
  3.9 0.0 copy-start.2
  3.9 10.4 %all-to-all-start = ((f32[32,14,1,128]{3,2,1,0:T(1,128)}), f32[32,14,1,128]{3,2,1,0:T(1,128)S(1)}, u32[]{:S(2)}, u32[]{:S(2)}) async-start(f32[32,14,1,128]{3,2,1,0:T(1,128)} %bitcast.16), calls=%async_computation | async-start | bytes 458752 | tf_op jit(solution)/shard_map/all_to_all | solution.py:346
  14.3 3.2 %collective-permute-start.2 = (f32[96,128]{1,0:T(8,128)}, f32[96,128]{1,0:T(8,128)S(1)}, u32[]{:S(2)}, u32[]{:S(2)}) collective-permute-start(f32[96,128]{1,0:T(8,128)} %get-tuple-element.12.mine), channel_id=1, source_target_pairs={{0,96},{32,64},{64,32},{96,0},{128,224},{160,192},{192,160},{224,1... | collective-permute-start | bytes 147464 | tf_op jit(solution)/shard_map/ppermute | solution.py:358
  17.4 3.0 %collective-permute-start.1 = (f32[96,128]{1,0:T(8,128)}, f32[96,128]{1,0:T(8,128)S(1)}, u32[]{:S(2)}, u32[]{:S(2)}) collective-permute-start(f32[96,128]{1,0:T(8,128)} %get-tuple-element.12.mine), channel_id=1, source_target_pairs={{0,64},{32,96},{64,0},{96,32},{128,192},{160,224},{192,128},{224,1... | collective-permute-start | bytes 147464 | tf_op jit(solution)/shard_map/ppermute | solution.py:358
  20.5 2.0 %collective-permute-start = (f32[96,128]{1,0:T(8,128)}, f32[96,128]{1,0:T(8,128)S(1)}, u32[]{:S(2)}, u32[]{:S(2)}) collective-permute-start(f32[96,128]{1,0:T(8,128)} %get-tuple-element.12.mine), channel_id=1, source_target_pairs={{0,32},{32,0},{64,96},{96,64},{128,160},{160,128},{192,224},{224,1... | collective-permute-start | bytes 147464 | tf_op jit(solution)/shard_map/ppermute | solution.py:358
  22.5 0.1 pad_add_fusion.place
  22.6 0.0 collective-permute-done.2.three
  22.6 1.3 %collective-permute-done.1.two = f32[96,128]{1,0:T(8,128)S(1)} collective-permute-done((f32[96,128]{1,0:T(8,128)}, f32[96,128]{1,0:T(8,128)S(1)}, u32[]{:S(2)}, u32[]{:S(2)}) %collective-permute-start.1) | collective-permute-done | bytes 49184 | tf_op jit(solution)/shard_map/ppermute | solution.py:358
  23.9 0.0 collective-permute-done.one
  23.9 0.8 %add_multiply_fusion.after.mine.half = f32[96,128]{1,0:T(8,128)S(1)} fusion(f32[96,128]{1,0:T(8,128)S(1)} %collective-permute-done.1.two, f32[96,128]{1,0:T(8,128)S(1)} %collective-permute-done.2.three, f32[96,128]{1,0:T(8,128)} %get-tuple-element.12.mine, f32[96,128]{1,0:T(8,128)S(1)} %collective-permute-done.one), kind=kLoop, calls=%fused_computation | loop fusion | flops 49152 | bytes 245760 | tf_op jit(solution)/shard_map/mul | solution.py:412
  24.7 0.2 all-to-all-done
  24.9 1.4 %pack.1.after = f32[16,16,128]{2,1,0:T(8,128)} custom-call(s32[2]{0:T(128)S(1)} %pad_add_fusion.place, f32[448,128]{1,0:T(8,128)S(1)} %bitcast.9, f32[96,128]{1,0:T(8,128)S(1)} %add_multiply_fusion.after.mine.half), custom_call_target="tpu_custom_call" | custom-call | tf_op jit(solution)/shard_map/pack/pallas_call | solution.py:413
  26.4 10.4 %all-to-all-start.1 = ((f32[16,16,128]{2,1,0:T(8,128)}), f32[16,16,128]{2,1,0:T(8,128)S(1)}, u32[]{:S(2)}, u32[]{:S(2)}) async-start(f32[16,16,128]{2,1,0:T(8,128)} %pack.1.after), calls=%async_computation.1 | async-start | bytes 262144 | tf_op jit(solution)/shard_map/all_to_all | solution.py:346
  36.8 4.7 %collective-permute-start.3 = (f32[96,128]{1,0:T(8,128)S(1)}, f32[96,128]{1,0:T(8,128)S(1)}, u32[]{:S(2)}, u32[]{:S(2)}) collective-permute-start(f32[96,128]{1,0:T(8,128)S(1)} %add_multiply_fusion.after.mine.half), channel_id=1, source_target_pairs={{0,128},{32,160},{64,192},{96,224},{128,0},{160,32},{192,64},{224,... | collective-permute-start | bytes 147464 | tf_op jit(solution)/shard_map/ppermute | solution.py:358
  41.5 1.2 %plane.1.back_in = f32[416,128]{1,0:T(8,128)S(1)} custom-call(s32[2]{0:T(128)S(1)} %pad_add_fusion.place, f32[448,128]{1,0:T(8,128)S(1)} %bitcast.10, f32[16,16,128]{2,1,0:T(8,128)} %pack.1.after), custom_call_target="tpu_custom_call" | custom-call | tf_op jit(solution)/shard_map/plane/pallas_call | solution.py:418
  42.7 2.7 %collective-permute-done.3.other = f32[96,128]{1,0:T(8,128)S(1)} collective-permute-done((f32[96,128]{1,0:T(8,128)S(1)}, f32[96,128]{1,0:T(8,128)S(1)}, u32[]{:S(2)}, u32[]{:S(2)}) %collective-permute-start.3) | collective-permute-done | bytes 49184 | tf_op jit(solution)/shard_map/ppermute | solution.py:358
  45.3 0.2 all-to-all-done.1.gathered
  45.5 1.6 %corner.1 = (f32[416,128]{1,0:T(8,128)}, f32[96,128]{1,0:T(8,128)S(1)}) custom-call(s32[2]{0:T(128)S(1)} %pad_add_fusion.place, f32[16,16,128]{2,1,0:T(8,128)S(1)} %all-to-all-done.1.gathered, f32[416,128]{1,0:T(8,128)S(1)} %plane.1.back_in, f32[96,128]{1,0:T(8,128)S(1)} %add_multiply_fusion.after.mine.half, f32[96,128]{1,0:T(8,128)S(1)} %collective-permute-done.3.other), custom_call_target="tpu_custom_call" | custom-call | tf_op jit(solution)/shard_map/corner/pallas_call | solution.py:421
  47.1 8.7 %all-to-all-start.2 = ((f32[32,13,1,128]{3,2,1,0:T(1,128)}), f32[32,13,1,128]{3,2,1,0:T(1,128)S(1)}, u32[]{:S(2)}, u32[]{:S(2)}) async-start(f32[32,13,1,128]{3,2,1,0:T(1,128)} %bitcast.5), calls=%async_computation.2 | async-start | bytes 425984 | tf_op jit(solution)/shard_map/all_to_all | solution.py:346
  55.8 6.6 %collective-permute-start.4 = (f32[96,128]{1,0:T(8,128)S(1)}, f32[96,128]{1,0:T(8,128)S(1)}, u32[]{:S(2)}, u32[]{:S(2)}) collective-permute-start(f32[96,128]{1,0:T(8,128)S(1)} %get-tuple-element.14.after.mine), channel_id=1, source_target_pairs={{0,256},{32,288},{64,320},{96,352},{128,384},{160,416},{192,448},{... | collective-permute-start | bytes 147464 | tf_op jit(solution)/shard_map/ppermute | solution.py:358
  62.4 0.0 copy-done.2
  62.4 0.7 line.1
  63.1 0.0 copy-start.1
  63.1 1.1 %copy-done.1 = bf16[3,32,8,512]{3,2,1,0:T(8,128)(2,1)S(1)} copy-done((bf16[3,32,8,512]{3,2,1,0:T(8,128)(2,1)S(1)}, bf16[3,32,8,512]{3,2,1,0:T(8,128)(2,1)}, u32[]{:S(2)}) %copy-start.1) | copy-done | bytes 786456
  64.3 0.0 copy-start
  64.3 4.1 %details.1.detail = f32[3,256,512]{2,1,0:T(8,128)S(1)} custom-call(s32[2]{0:T(128)S(1)} %pad_add_fusion.place, f32[448,128]{1,0:T(8,128)S(1)} %bitcast.11, bf16[3,256,512]{2,1,0:T(8,128)(2,1)S(1)} %bitcast.15, f32[96,128]{1,0:T(8,128)S(1)} %get-tuple-element.15.after.partial), custom_call_target="tpu_custom_call" | custom-call | flops 1409286144 | bytes 3932160 | tf_op jit(solution)/shard_map/details/pallas_call | solution.py:435
  68.4 0.0 collective-permute-done.4.other
  68.4 0.0 all-to-all-done.2
  68.4 0.0 copy-done
  68.4 1.8 %finish.1 = bf16[3,256,512]{2,1,0:T(8,128)(2,1)} custom-call(f32[416,128]{1,0:T(8,128)S(1)} %bitcast.12, f32[96,128]{1,0:T(8,128)S(1)} %get-tuple-element.14.after.mine, f32[96,128]{1,0:T(8,128)S(1)} %collective-permute-done.4.other, f32[96,128]{1,0:T(8,128)S(1)} %get-tuple-element.15.after.partial, f32[8,512]{1,0:T(8,128)S(1)} %get-tuple-element.16.mask, ...), custom_call_target="tpu_custom_call" | custom-call | tf_op jit(solution)/shard_map/finish/pallas_call | solution.py:442
Async XLA Ops:
  3.9 58.6 %copy-start.2 = (f32[96,128]{1,0:T(8,128)S(1)}, f32[96,128]{1,0:T(8,128)}, u32[]{:S(2)}) copy-start(f32[96,128]{1,0:T(8,128)} %get-tuple-element.12.mine) | copy-start | bytes 147460
  3.9 21.1 %all-to-all-start = ((f32[32,14,1,128]{3,2,1,0:T(1,128)}), f32[32,14,1,128]{3,2,1,0:T(1,128)S(1)}, u32[]{:S(2)}, u32[]{:S(2)}) async-start(f32[32,14,1,128]{3,2,1,0:T(1,128)} %bitcast.16), calls=%async_computation | async-start | bytes 458752 | tf_op jit(solution)/shard_map/all_to_all | solution.py:346
  14.3 8.3 %collective-permute-start.2 = (f32[96,128]{1,0:T(8,128)}, f32[96,128]{1,0:T(8,128)S(1)}, u32[]{:S(2)}, u32[]{:S(2)}) collective-permute-start(f32[96,128]{1,0:T(8,128)} %get-tuple-element.12.mine), channel_id=1, source_target_pairs={{0,96},{32,64},{64,32},{96,0},{128,224},{160,192},{192,160},{224,1... | collective-permute-start | bytes 147464 | tf_op jit(solution)/shard_map/ppermute | solution.py:358
  17.4 6.5 %collective-permute-start.1 = (f32[96,128]{1,0:T(8,128)}, f32[96,128]{1,0:T(8,128)S(1)}, u32[]{:S(2)}, u32[]{:S(2)}) collective-permute-start(f32[96,128]{1,0:T(8,128)} %get-tuple-element.12.mine), channel_id=1, source_target_pairs={{0,64},{32,96},{64,0},{96,32},{128,192},{160,224},{192,128},{224,1... | collective-permute-start | bytes 147464 | tf_op jit(solution)/shard_map/ppermute | solution.py:358
  20.5 3.4 %collective-permute-start = (f32[96,128]{1,0:T(8,128)}, f32[96,128]{1,0:T(8,128)S(1)}, u32[]{:S(2)}, u32[]{:S(2)}) collective-permute-start(f32[96,128]{1,0:T(8,128)} %get-tuple-element.12.mine), channel_id=1, source_target_pairs={{0,32},{32,0},{64,96},{96,64},{128,160},{160,128},{192,224},{224,1... | collective-permute-start | bytes 147464 | tf_op jit(solution)/shard_map/ppermute | solution.py:358
  26.4 19.2 %all-to-all-start.1 = ((f32[16,16,128]{2,1,0:T(8,128)}), f32[16,16,128]{2,1,0:T(8,128)S(1)}, u32[]{:S(2)}, u32[]{:S(2)}) async-start(f32[16,16,128]{2,1,0:T(8,128)} %pack.1.after), calls=%async_computation.1 | async-start | bytes 262144 | tf_op jit(solution)/shard_map/all_to_all | solution.py:346
  36.8 8.6 %collective-permute-start.3 = (f32[96,128]{1,0:T(8,128)S(1)}, f32[96,128]{1,0:T(8,128)S(1)}, u32[]{:S(2)}, u32[]{:S(2)}) collective-permute-start(f32[96,128]{1,0:T(8,128)S(1)} %add_multiply_fusion.after.mine.half), channel_id=1, source_target_pairs={{0,128},{32,160},{64,192},{96,224},{128,0},{160,32},{192,64},{224,... | collective-permute-start | bytes 147464 | tf_op jit(solution)/shard_map/ppermute | solution.py:358
  47.1 21.3 %all-to-all-start.2 = ((f32[32,13,1,128]{3,2,1,0:T(1,128)}), f32[32,13,1,128]{3,2,1,0:T(1,128)S(1)}, u32[]{:S(2)}, u32[]{:S(2)}) async-start(f32[32,13,1,128]{3,2,1,0:T(1,128)} %bitcast.5), calls=%async_computation.2 | async-start | bytes 425984 | tf_op jit(solution)/shard_map/all_to_all | solution.py:346
  55.8 12.6 %collective-permute-start.4 = (f32[96,128]{1,0:T(8,128)S(1)}, f32[96,128]{1,0:T(8,128)S(1)}, u32[]{:S(2)}, u32[]{:S(2)}) collective-permute-start(f32[96,128]{1,0:T(8,128)S(1)} %get-tuple-element.14.after.mine), channel_id=1, source_target_pairs={{0,256},{32,288},{64,320},{96,352},{128,384},{160,416},{192,448},{... | collective-permute-start | bytes 147464 | tf_op jit(solution)/shard_map/ppermute | solution.py:358
  63.1 1.1 %copy-start.1 = (bf16[3,32,8,512]{3,2,1,0:T(8,128)(2,1)S(1)}, bf16[3,32,8,512]{3,2,1,0:T(8,128)(2,1)}, u32[]{:S(2)}) copy-start(bf16[3,32,8,512]{3,2,1,0:T(8,128)(2,1)} %param.4) | copy-start | bytes 2359300
  64.3 4.1 %copy-start = (bf16[3,32,8,512]{3,2,1,0:T(8,128)(2,1)S(1)}, bf16[3,32,8,512]{3,2,1,0:T(8,128)(2,1)}, u32[]{:S(2)}) copy-start(bf16[3,32,8,512]{3,2,1,0:T(8,128)(2,1)} %param.5) | copy-start | bytes 2359300

commit v8 on v6

--- a/solution.py
+++ b/solution.py
@@ -180,6 +180,10 @@
             send[at : at + 1, :] = turned[row : row + 1]
 
 
+def own_place():
+    return lax.axis_index("gx"), lax.axis_index("yz")
+
+
 def level_tables(length):
     square = (length, length)
     forward = weight_of(iota(square, 0), iota(square, 1), length).astype(BF16)
@@ -187,7 +191,8 @@
     return forward, inverse
 
 
-def plane_kernel(place, recv, after, back, corner):
+def plane_kernel(recv, after, back, corner):
+    place = own_place()
     del after
     planes = recv.shape[0] // ROWS
     forward, inverse = level_tables(planes)
@@ -221,7 +226,8 @@
             back[pl.ds(c * ZB + zb, planes, stride=BACK), :] = data[:, zb * BZ : (zb + 1) * BZ]
 
 
-def details_kernel(place, recv, vort, after, detail):
+def details_kernel(recv, vort, after, detail):
+    place = own_place()
     del after
     parts, cells, wide = vort.shape
     planes = cells // BY
@@ -243,7 +249,8 @@
         detail[c] = remix(left_product(inverse, rows * mask), unmix)
 
 
-def corner_kernel(place, gathered, back_in, mine, other, after, back, means):
+def corner_kernel(gathered, back_in, mine, other, after, back, means):
+    place = own_place()
     del after
     means[...] = (mine[...] + other[...]) * 0.5
     slabs = gathered.shape[0]
@@ -262,7 +269,8 @@
     back[pl.ds(EXTRA, planes, stride=BACK), :] = left_product(level_tables(planes)[1], total)
 
 
-def line_kernel(place, gathered, after, mine, one, two, three, half, other, total, mask):
+def line_kernel(gathered, after, mine, one, two, three, half, other, total, mask):
+    place = own_place()
     del after
     wanted = [gathered[0, 0:1, :]]
     for level in range(4):
@@ -357,11 +365,9 @@
     parts, planes, tall, wide = vorticity.shape
     cells = planes * tall
     slabs = lax.axis_size("gx")
-    smem = pl.BlockSpec(memory_space=pltpu.SMEM)
     vmem = pl.BlockSpec(memory_space=pltpu.VMEM)
     loose = pl.BlockSpec(memory_space=pl.ANY)
     params = pltpu.CompilerParams(vmem_limit_bytes=32 * 1024 * 1024)
-    place = jnp.stack([lax.axis_index("gx"), lax.axis_index("yz")]).astype(jnp.int32)
     vort = vorticity.reshape(parts, cells, wide)
     line_shape = (CHUNKS * BY, BZ)
 
@@ -409,31 +415,31 @@
         plane_kernel,
         "plane",
         (array(planes * BACK, BZ), array(slabs, PACKED, BZ)),
-        [smem, vmem, loose],
-    )(place, recv, half)
+        [vmem, loose],
+    )(recv, half)
     gathered = exchange(corner, "gx")
     opposite = from_partner(half, 4)
     detail = call(
         details_kernel,
         "details",
         array(parts, cells, wide),
-        [smem, vmem, vmem, loose],
+        [vmem, vmem, loose],
         cost=cost(7),
-    )(place, recv, vort, corner)
+    )(recv, vort, corner)
     back, means = call(
         corner_kernel,
         "corner",
         (array(planes * BACK, BZ), array(*line_shape)),
-        [smem] + [vmem] * 4 + [loose],
-    )(place, gathered, back, half, opposite, detail)
+        [vmem] * 4 + [loose],
+    )(gathered, back, half, opposite, detail)
     got = over_yz(back, planes)
     other = from_partner(means, 8)
     partial, mask = call(
         line_kernel,
         "line",
         (array(*line_shape), array(8, wide)),
-        [smem, vmem, loose] + [vmem] * 6,
-    )(place, gathered, means, line, *near, half, opposite)
+        [vmem, loose] + [vmem] * 6,
+    )(gathered, means, line, *near, half, opposite)
     out = call(
         finish_kernel,
         "finish",

time: 70.5 us -> 69.3 us (0.983)
  Pallas kernels: 12.8 us -> 10.6 us
  waiting for transfers between devices: 7.6 us -> 8.65 us
    pallas_call x2, Pallas kernels: 4.78 us -> 3.7 us  [the longest x1 3.54 us: body(): call(details_kernel, 'details', array(parts, cells, wide), [vmem, vmem, l...]
    ppermute x5, waiting for transfers between devices: 3.95 us -> 4.72 us  [from_partner(): return lax.ppermute(value, 'gx', pairs)]
  transfers between devices with their start and end apart: 8 -> 8, of which waited for: 4 -> 6; matrix products, arithmetic and copies ran while one was open for 1% -> 1% of each run, Pallas kernels for 7% -> 5%
where the time goes in v8:
time: 69.3 us; the launch traced here: 68.8 us
  starting transfers between devices  47.9 us (69%)
  Pallas kernels  10.6 us (15%)
  waiting for transfers between devices  8.65 us (12%)
  between operations  0.85 us (1%)
  other arithmetic  0.81 us (1%)
    all_to_all x3, starting transfers between devices, exchange(): return lax.all_to_all(value, axis, split_axis=0, concat_axis=0, tiled=True)  28.3 us
    ppermute x5, starting transfers between devices, from_partner(): return lax.ppermute(value, 'gx', pairs)  19.6 us
    ppermute x5, waiting for transfers between devices, from_partner(): return lax.ppermute(value, 'gx', pairs)  4.72 us
    all_to_all x3, waiting for transfers between devices, exchange(): return lax.all_to_all(value, axis, split_axis=0, concat_axis=0, tiled=True)  3.93 us
    pallas_call x1, Pallas kernels, body(): call(details_kernel, 'details', array(parts, cells, wide), [vmem, vmem, l...  3.54 us
    pallas_call x1, Pallas kernels, body(): call(head_kernel, 'head', (array(planes * ROWS, BZ), array(*line_shape)),...  3.21 us
    pallas_call x1, Pallas kernels, body(): call(finish_kernel, 'finish', jax.ShapeDtypeStruct((parts, cells, wide),...  1.75 us
  transfers between devices with their start and end apart: 8, of which 6 were waited for; matrix products, arithmetic and copies ran while one was open for 1% of the time, Pallas kernels for 5%

profile of v8, /device:TPU:8, one launch (start us, length us, event | category | flops | bytes accessed | tf_op | source)
XLA Modules:
  0.0 68.8 jit_solution(16240614355504677678)
XLA Ops:
  0.0 0.0 copy-start.1
  0.7 3.2 %head.1 = (f32[448,128]{1,0:T(8,128)}, f32[96,128]{1,0:T(8,128)}) custom-call(s32[1]{0:T(128)S(6)} %copy.7.counts_hbm, s32[1,128]{1,0:T(1,128)} %blocks_hbm.1, bf16[3,256,512]{2,1,0:T(8,128)(2,1)} %bitcast.11), custom_call_target="tpu_custom_call" | custom-call | tf_op jit(solution)/shard_map/head/pallas_call | solution.py:398
  3.9 10.2 %all-to-all-start = ((f32[32,14,1,128]{3,2,1,0:T(1,128)}), f32[32,14,1,128]{3,2,1,0:T(1,128)S(1)}, u32[]{:S(2)}, u32[]{:S(2)}) async-start(f32[32,14,1,128]{3,2,1,0:T(1,128)} %bitcast.13), calls=%async_computation | async-start | bytes 458752 | tf_op jit(solution)/shard_map/all_to_all | solution.py:349
  14.1 3.2 %collective-permute-start.2 = (f32[96,128]{1,0:T(8,128)}, f32[96,128]{1,0:T(8,128)S(1)}, u32[]{:S(2)}, u32[]{:S(2)}) collective-permute-start(f32[96,128]{1,0:T(8,128)} %get-tuple-element.14.mine), channel_id=1, source_target_pairs={{0,96},{32,64},{64,32},{96,0},{128,224},{160,192},{192,160},{224,1... | collective-permute-start | bytes 147464 | tf_op jit(solution)/shard_map/ppermute | solution.py:361
  17.3 3.0 %collective-permute-start.1 = (f32[96,128]{1,0:T(8,128)}, f32[96,128]{1,0:T(8,128)S(1)}, u32[]{:S(2)}, u32[]{:S(2)}) collective-permute-start(f32[96,128]{1,0:T(8,128)} %get-tuple-element.14.mine), channel_id=1, source_target_pairs={{0,64},{32,96},{64,0},{96,32},{128,192},{160,224},{192,128},{224,1... | collective-permute-start | bytes 147464 | tf_op jit(solution)/shard_map/ppermute | solution.py:361
  20.3 2.0 %collective-permute-start = (f32[96,128]{1,0:T(8,128)}, f32[96,128]{1,0:T(8,128)S(1)}, u32[]{:S(2)}, u32[]{:S(2)}) collective-permute-start(f32[96,128]{1,0:T(8,128)} %get-tuple-element.14.mine), channel_id=1, source_target_pairs={{0,32},{32,0},{64,96},{96,64},{128,160},{160,128},{192,224},{224,1... | collective-permute-start | bytes 147464 | tf_op jit(solution)/shard_map/ppermute | solution.py:361
  22.4 0.0 collective-permute-done.2.three
  22.4 1.4 %collective-permute-done.1.two = f32[96,128]{1,0:T(8,128)S(1)} collective-permute-done((f32[96,128]{1,0:T(8,128)}, f32[96,128]{1,0:T(8,128)S(1)}, u32[]{:S(2)}, u32[]{:S(2)}) %collective-permute-start.1) | collective-permute-done | bytes 49184 | tf_op jit(solution)/shard_map/ppermute | solution.py:361
  23.7 0.0 collective-permute-done.one
  23.8 0.8 %add_multiply_fusion.after.mine.half = f32[96,128]{1,0:T(8,128)S(1)} fusion(f32[96,128]{1,0:T(8,128)S(1)} %collective-permute-done.1.two, f32[96,128]{1,0:T(8,128)S(1)} %collective-permute-done.2.three, f32[96,128]{1,0:T(8,128)} %get-tuple-element.14.mine, f32[96,128]{1,0:T(8,128)S(1)} %collective-permute-done.one), kind=kLoop, calls=%fused_computation | loop fusion | flops 49152 | bytes 245760 | tf_op jit(solution)/shard_map/mul | solution.py:413
  24.6 1.2 %all-to-all-done = f32[32,14,1,128]{3,2,1,0:T(1,128)S(1)} async-done(((f32[32,14,1,128]{3,2,1,0:T(1,128)}), f32[32,14,1,128]{3,2,1,0:T(1,128)S(1)}, u32[]{:S(2)}, u32[]{:S(2)}) %all-to-all-start) | async-done | bytes 229408 | tf_op jit(solution)/shard_map/all_to_all | solution.py:349
  25.8 0.9 %plane.1 = (f32[416,128]{1,0:T(8,128)S(1)}, f32[16,16,128]{2,1,0:T(8,128)}) custom-call(f32[448,128]{1,0:T(8,128)S(1)} %bitcast.7, f32[96,128]{1,0:T(8,128)S(1)} %add_multiply_fusion.after.mine.half), custom_call_target="tpu_custom_call" | custom-call | tf_op jit(solution)/shard_map/plane/pallas_call | solution.py:414
  26.7 10.4 %all-to-all-start.1 = ((f32[16,16,128]{2,1,0:T(8,128)}), f32[16,16,128]{2,1,0:T(8,128)S(1)}, u32[]{:S(2)}, u32[]{:S(2)}) async-start(f32[16,16,128]{2,1,0:T(8,128)} %get-tuple-element.15.after), calls=%async_computation.1 | async-start | bytes 262144 | tf_op jit(solution)/shard_map/all_to_all | solution.py:349
  37.1 4.7 %collective-permute-start.3 = (f32[96,128]{1,0:T(8,128)S(1)}, f32[96,128]{1,0:T(8,128)S(1)}, u32[]{:S(2)}, u32[]{:S(2)}) collective-permute-start(f32[96,128]{1,0:T(8,128)S(1)} %add_multiply_fusion.after.mine.half), channel_id=1, source_target_pairs={{0,128},{32,160},{64,192},{96,224},{128,0},{160,32},{192,64},{224,... | collective-permute-start | bytes 147464 | tf_op jit(solution)/shard_map/ppermute | solution.py:361
  41.8 0.0 copy-done.1
  41.8 3.5 %details.1.after.detail = f32[3,256,512]{2,1,0:T(8,128)S(1)} custom-call(f32[448,128]{1,0:T(8,128)S(1)} %bitcast.8, bf16[3,256,512]{2,1,0:T(8,128)(2,1)S(1)} %bitcast.12, f32[16,16,128]{2,1,0:T(8,128)} %get-tuple-element.15.after), custom_call_target="tpu_custom_call" | custom-call | flops 1409286144 | bytes 3932160 | tf_op jit(solution)/shard_map/details/pallas_call | solution.py:422
  45.4 0.0 copy-start.2
  45.4 0.0 copy-start
  45.4 0.3 collective-permute-done.3.other
  45.6 0.2 all-to-all-done.1.gathered
  45.8 1.0 %corner.1 = (f32[416,128]{1,0:T(8,128)}, f32[96,128]{1,0:T(8,128)S(1)}) custom-call(f32[16,16,128]{2,1,0:T(8,128)S(1)} %all-to-all-done.1.gathered, f32[416,128]{1,0:T(8,128)S(1)} %get-tuple-element.16.back_in, f32[96,128]{1,0:T(8,128)S(1)} %add_multiply_fusion.after.mine.half, f32[96,128]{1,0:T(8,128)S(1)} %collective-permute-done.3.other, ...), custom_call_target="tpu_custom_call" | custom-call | tf_op jit(solution)/shard_map/corner/pallas_call | solution.py:429
  46.9 7.7 %all-to-all-start.2 = ((f32[32,13,1,128]{3,2,1,0:T(1,128)}), f32[32,13,1,128]{3,2,1,0:T(1,128)S(1)}, u32[]{:S(2)}, u32[]{:S(2)}) async-start(f32[32,13,1,128]{3,2,1,0:T(1,128)} %bitcast.3), calls=%async_computation.2 | async-start | bytes 425984 | tf_op jit(solution)/shard_map/all_to_all | solution.py:349
  54.6 6.6 %collective-permute-start.4 = (f32[96,128]{1,0:T(8,128)S(1)}, f32[96,128]{1,0:T(8,128)S(1)}, u32[]{:S(2)}, u32[]{:S(2)}) collective-permute-start(f32[96,128]{1,0:T(8,128)S(1)} %get-tuple-element.18.after.mine), channel_id=1, source_target_pairs={{0,256},{32,288},{64,320},{96,352},{128,384},{160,416},{192,448},{... | collective-permute-start | bytes 147464 | tf_op jit(solution)/shard_map/ppermute | solution.py:361
  61.2 0.0 copy-done.2
  61.2 0.2 line.1
  61.4 3.1 %collective-permute-done.4.other = f32[96,128]{1,0:T(8,128)S(1)} collective-permute-done((f32[96,128]{1,0:T(8,128)S(1)}, f32[96,128]{1,0:T(8,128)S(1)}, u32[]{:S(2)}, u32[]{:S(2)}) %collective-permute-start.4) | collective-permute-done | bytes 49184 | tf_op jit(solution)/shard_map/ppermute | solution.py:361
  64.5 2.6 %all-to-all-done.2 = f32[32,13,1,128]{3,2,1,0:T(1,128)S(1)} async-done(((f32[32,13,1,128]{3,2,1,0:T(1,128)}), f32[32,13,1,128]{3,2,1,0:T(1,128)S(1)}, u32[]{:S(2)}, u32[]{:S(2)}) %all-to-all-start.2) | async-done | bytes 213024 | tf_op jit(solution)/shard_map/all_to_all | solution.py:349
  67.0 0.0 copy-done
  67.0 1.8 %finish.1 = bf16[3,256,512]{2,1,0:T(8,128)(2,1)} custom-call(f32[416,128]{1,0:T(8,128)S(1)} %bitcast.9, f32[96,128]{1,0:T(8,128)S(1)} %get-tuple-element.18.after.mine, f32[96,128]{1,0:T(8,128)S(1)} %collective-permute-done.4.other, f32[96,128]{1,0:T(8,128)S(1)} %get-tuple-element.19.partial, f32[8,512]{1,0:T(8,128)S(1)} %get-tuple-element.20.mask, ...), custom_call_target="tpu_custom_call" | custom-call | tf_op jit(solution)/shard_map/finish/pallas_call | solution.py:443
Async XLA Ops:
  0.0 41.8 %copy-start.1 = (bf16[3,32,8,512]{3,2,1,0:T(8,128)(2,1)S(1)}, bf16[3,32,8,512]{3,2,1,0:T(8,128)(2,1)}, u32[]{:S(2)}) copy-start(bf16[3,32,8,512]{3,2,1,0:T(8,128)(2,1)} %param.4) | copy-start | bytes 2359300
  3.9 21.8 %all-to-all-start = ((f32[32,14,1,128]{3,2,1,0:T(1,128)}), f32[32,14,1,128]{3,2,1,0:T(1,128)S(1)}, u32[]{:S(2)}, u32[]{:S(2)}) async-start(f32[32,14,1,128]{3,2,1,0:T(1,128)} %bitcast.13), calls=%async_computation | async-start | bytes 458752 | tf_op jit(solution)/shard_map/all_to_all | solution.py:349
  14.1 8.2 %collective-permute-start.2 = (f32[96,128]{1,0:T(8,128)}, f32[96,128]{1,0:T(8,128)S(1)}, u32[]{:S(2)}, u32[]{:S(2)}) collective-permute-start(f32[96,128]{1,0:T(8,128)} %get-tuple-element.14.mine), channel_id=1, source_target_pairs={{0,96},{32,64},{64,32},{96,0},{128,224},{160,192},{192,160},{224,1... | collective-permute-start | bytes 147464 | tf_op jit(solution)/shard_map/ppermute | solution.py:361
  17.3 6.5 %collective-permute-start.1 = (f32[96,128]{1,0:T(8,128)}, f32[96,128]{1,0:T(8,128)S(1)}, u32[]{:S(2)}, u32[]{:S(2)}) collective-permute-start(f32[96,128]{1,0:T(8,128)} %get-tuple-element.14.mine), channel_id=1, source_target_pairs={{0,64},{32,96},{64,0},{96,32},{128,192},{160,224},{192,128},{224,1... | collective-permute-start | bytes 147464 | tf_op jit(solution)/shard_map/ppermute | solution.py:361
  20.3 3.4 %collective-permute-start = (f32[96,128]{1,0:T(8,128)}, f32[96,128]{1,0:T(8,128)S(1)}, u32[]{:S(2)}, u32[]{:S(2)}) collective-permute-start(f32[96,128]{1,0:T(8,128)} %get-tuple-element.14.mine), channel_id=1, source_target_pairs={{0,32},{32,0},{64,96},{96,64},{128,160},{160,128},{192,224},{224,1... | collective-permute-start | bytes 147464 | tf_op jit(solution)/shard_map/ppermute | solution.py:361
  26.7 19.2 %all-to-all-start.1 = ((f32[16,16,128]{2,1,0:T(8,128)}), f32[16,16,128]{2,1,0:T(8,128)S(1)}, u32[]{:S(2)}, u32[]{:S(2)}) async-start(f32[16,16,128]{2,1,0:T(8,128)} %get-tuple-element.15.after), calls=%async_computation.1 | async-start | bytes 262144 | tf_op jit(solution)/shard_map/all_to_all | solution.py:349
  37.1 8.6 %collective-permute-start.3 = (f32[96,128]{1,0:T(8,128)S(1)}, f32[96,128]{1,0:T(8,128)S(1)}, u32[]{:S(2)}, u32[]{:S(2)}) collective-permute-start(f32[96,128]{1,0:T(8,128)S(1)} %add_multiply_fusion.after.mine.half), channel_id=1, source_target_pairs={{0,128},{32,160},{64,192},{96,224},{128,0},{160,32},{192,64},{224,... | collective-permute-start | bytes 147464 | tf_op jit(solution)/shard_map/ppermute | solution.py:361
  45.4 15.8 %copy-start.2 = (f32[96,128]{1,0:T(8,128)S(1)}, f32[96,128]{1,0:T(8,128)}, u32[]{:S(2)}) copy-start(f32[96,128]{1,0:T(8,128)} %get-tuple-element.14.mine) | copy-start | bytes 147460
  45.4 21.6 %copy-start = (bf16[3,32,8,512]{3,2,1,0:T(8,128)(2,1)S(1)}, bf16[3,32,8,512]{3,2,1,0:T(8,128)(2,1)}, u32[]{:S(2)}) copy-start(bf16[3,32,8,512]{3,2,1,0:T(8,128)(2,1)} %param.5) | copy-start | bytes 2359300
  46.9 20.2 %all-to-all-start.2 = ((f32[32,13,1,128]{3,2,1,0:T(1,128)}), f32[32,13,1,128]{3,2,1,0:T(1,128)S(1)}, u32[]{:S(2)}, u32[]{:S(2)}) async-start(f32[32,13,1,128]{3,2,1,0:T(1,128)} %bitcast.3), calls=%async_computation.2 | async-start | bytes 425984 | tf_op jit(solution)/shard_map/all_to_all | solution.py:349
  54.6 9.9 %collective-permute-start.4 = (f32[96,128]{1,0:T(8,128)S(1)}, f32[96,128]{1,0:T(8,128)S(1)}, u32[]{:S(2)}, u32[]{:S(2)}) collective-permute-start(f32[96,128]{1,0:T(8,128)S(1)} %get-tuple-element.18.after.mine), channel_id=1, source_target_pairs={{0,256},{32,288},{64,320},{96,352},{128,384},{160,416},{192,448},{... | collective-permute-start | bytes 147464 | tf_op jit(solution)/shard_map/ppermute | solution.py:361

commit v9 on v8

--- a/solution.py
+++ b/solution.py
@@ -191,11 +191,11 @@
     return forward, inverse
 
 
-def plane_kernel(recv, after, back, corner):
+def pack_kernel(recv, after, corner):
     place = own_place()
     del after
     planes = recv.shape[0] // ROWS
-    forward, inverse = level_tables(planes)
+    forward = level_tables(planes)[0]
     extra = recv[pl.ds(EXTRA, planes, stride=ROWS), :]
     lane = iota((PACKED, BZ), 1)
     row = iota((PACKED, BZ), 0)
@@ -213,6 +213,14 @@
     packed = packed + jnp.dot(own, slot, preferred_element_type=F32)
     for g in range(corner.shape[0]):
         corner[g] = packed
+
+
+def plane_kernel(recv, after, back):
+    place = own_place()
+    del after
+    planes = recv.shape[0] // ROWS
+    forward, inverse = level_tables(planes)
+    unmix = unmix_table(ZB * BZ)
     pick = jnp.where(iota((BZ, ZB * BZ), 0) & 3 == iota((BZ, ZB * BZ), 1) >> 7, 1.0, 0.0)
     own = recv[pl.ds(place[1] * ROWS + KEPT, 1), :]
     spread = jnp.where(iota((planes, BZ), 1) >> 2 == iota((planes, BZ), 0), own, 0.0)
@@ -221,7 +229,7 @@
         data = jnp.concatenate(
             [recv[pl.ds(c * ZB + zb, planes, stride=ROWS), :] for zb in range(ZB)], axis=1
         )
-        data = left_product(inverse, left_product(forward, data) * mask)
+        data = remix(left_product(inverse, left_product(forward, data) * mask), unmix)
         for zb in range(ZB):
             back[pl.ds(c * ZB + zb, planes, stride=BACK), :] = data[:, zb * BZ : (zb + 1) * BZ]
 
@@ -307,18 +315,16 @@
             last = (mine[span, :] - other[span, :]) * 0.5
             mean = (mine[span, :] + other[span, :]) * 0.5
             total = partial[span, :] + last * mask[4:5, lanes] + mean * mask[0:1, lanes]
-            line[c * BY : (c + 1) * BY, lanes] = total
             corner = jnp.where(lane >> 4 == (slot + c) & 7, turned[zb], 0.0)
             corner = jnp.sum(corner, axis=0, keepdims=True)
             corner = pltpu.roll(corner, BZ - c * SLICE, 1) if c else corner
+            line[c * BY : (c + 1) * BY, lanes] = total + corner
             data = got[pl.ds(c * ZB + zb, planes, stride=BACK), :]
-            columns.append(jnp.where(iota((planes, BZ), 0) == 0, corner, data))
+            columns.append(jnp.where(iota((planes, BZ), 0) == 0, 0.0, data))
         rows[c * planes : (c + 1) * planes, :] = left_product(
             inverse, jnp.concatenate(columns, axis=1)
         )
-    unmix = unmix_table(wide)
-    line[...] = remix(line[...], unmix)
-    rows[...] = remix(rows[...], unmix)
+    line[...] = remix(line[...], unmix_table(wide))
     copies = []
     for x in range(planes):
         span = slice(x * BY, (x + 1) * BY)
@@ -411,14 +417,10 @@
     recv = over_yz(send, planes)
     near = [from_partner(line, distance) for distance in (1, 2, 3)]
     half = (line + near[0] + (near[1] + near[2])) * 0.25
-    back, corner = call(
-        plane_kernel,
-        "plane",
-        (array(planes * BACK, BZ), array(slabs, PACKED, BZ)),
-        [vmem, loose],
-    )(recv, half)
+    corner = call(pack_kernel, "pack", array(slabs, PACKED, BZ), [vmem, loose])(recv, half)
     gathered = exchange(corner, "gx")
     opposite = from_partner(half, 4)
+    back = call(plane_kernel, "plane", array(planes * BACK, BZ), [vmem, loose])(recv, corner)
     detail = call(
         details_kernel,
         "details",

time: 69.3 us -> 69.5 us (level)
  Pallas kernels: 10.6 us -> 11.9 us
  starting transfers between devices: 47.9 us -> 47.1 us
    pallas_call x1 -> x2, Pallas kernels: 0.88 us -> 2.07 us  [the longest x1 1.2 us: body(): call(plane_kernel, 'plane', array(planes * BACK, BZ), [vmem, loose])]
    all_to_all x3, waiting for transfers between devices: 3.93 us -> 3.03 us  [exchange(): return lax.all_to_all(value, axis, split_axis=0, concat_axis=0, tiled=True)]
    ppermute x5, starting transfers between devices: 19.6 us -> 18.8 us  [from_partner(): return lax.ppermute(value, 'gx', pairs)]
  transfers between devices with their start and end apart: 8 -> 8, of which waited for: 6 -> 4; matrix products, arithmetic and copies ran while one was open for 1% -> 1% of each run, Pallas kernels for 5% -> 7%
where the time goes in v9:
time: 69.5 us; the launch traced here: 69 us
  starting transfers between devices  47.1 us (68%)
  Pallas kernels  11.9 us (17%)
  waiting for transfers between devices  8.27 us (12%)
  between operations  0.87 us (1%)
  other arithmetic  0.81 us (1%)
    all_to_all x3, starting transfers between devices, exchange(): return lax.all_to_all(value, axis, split_axis=0, concat_axis=0, tiled=True)  28.3 us
    ppermute x5, starting transfers between devices, from_partner(): return lax.ppermute(value, 'gx', pairs)  18.8 us
    ppermute x5, waiting for transfers between devices, from_partner(): return lax.ppermute(value, 'gx', pairs)  5.24 us
    pallas_call x1, Pallas kernels, body(): call(details_kernel, 'details', array(parts, cells, wide), [vmem, vmem, l...  3.54 us
    pallas_call x1, Pallas kernels, body(): call(head_kernel, 'head', (array(planes * ROWS, BZ), array(*line_shape)),...  3.21 us
    all_to_all x3, waiting for transfers between devices, exchange(): return lax.all_to_all(value, axis, split_axis=0, concat_axis=0, tiled=True)  3.03 us
    pallas_call x1, Pallas kernels, body(): call(finish_kernel, 'finish', jax.ShapeDtypeStruct((parts, cells, wide),...  1.92 us
  transfers between devices with their start and end apart: 8, of which 4 were waited for; matrix products, arithmetic and copies ran while one was open for 1% of the time, Pallas kernels for 7%

profile of v9, /device:TPU:8, one launch (start us, length us, event | category | flops | bytes accessed | tf_op | source)
XLA Modules:
  0.0 69.0 jit_solution(5185042405023079243)
XLA Ops:
  0.0 0.0 copy-start.1
  0.7 3.2 %head.1 = (f32[448,128]{1,0:T(8,128)}, f32[96,128]{1,0:T(8,128)}) custom-call(s32[1]{0:T(128)S(6)} %copy.7.counts_hbm, s32[1,128]{1,0:T(1,128)} %blocks_hbm.1, bf16[3,256,512]{2,1,0:T(8,128)(2,1)} %bitcast.12), custom_call_target="tpu_custom_call" | custom-call | tf_op jit(solution)/shard_map/head/pallas_call | solution.py:404
  3.9 10.2 %all-to-all-start = ((f32[32,14,1,128]{3,2,1,0:T(1,128)}), f32[32,14,1,128]{3,2,1,0:T(1,128)S(1)}, u32[]{:S(2)}, u32[]{:S(2)}) async-start(f32[32,14,1,128]{3,2,1,0:T(1,128)} %bitcast.14), calls=%async_computation | async-start | bytes 458752 | tf_op jit(solution)/shard_map/all_to_all | solution.py:355
  14.1 3.2 %collective-permute-start.2 = (f32[96,128]{1,0:T(8,128)}, f32[96,128]{1,0:T(8,128)S(1)}, u32[]{:S(2)}, u32[]{:S(2)}) collective-permute-start(f32[96,128]{1,0:T(8,128)} %get-tuple-element.12.mine), channel_id=1, source_target_pairs={{0,96},{32,64},{64,32},{96,0},{128,224},{160,192},{192,160},{224,1... | collective-permute-start | bytes 147464 | tf_op jit(solution)/shard_map/ppermute | solution.py:367
  17.3 3.0 %collective-permute-start.1 = (f32[96,128]{1,0:T(8,128)}, f32[96,128]{1,0:T(8,128)S(1)}, u32[]{:S(2)}, u32[]{:S(2)}) collective-permute-start(f32[96,128]{1,0:T(8,128)} %get-tuple-element.12.mine), channel_id=1, source_target_pairs={{0,64},{32,96},{64,0},{96,32},{128,192},{160,224},{192,128},{224,1... | collective-permute-start | bytes 147464 | tf_op jit(solution)/shard_map/ppermute | solution.py:367
  20.3 2.0 %collective-permute-start = (f32[96,128]{1,0:T(8,128)}, f32[96,128]{1,0:T(8,128)S(1)}, u32[]{:S(2)}, u32[]{:S(2)}) collective-permute-start(f32[96,128]{1,0:T(8,128)} %get-tuple-element.12.mine), channel_id=1, source_target_pairs={{0,32},{32,0},{64,96},{96,64},{128,160},{160,128},{192,224},{224,1... | collective-permute-start | bytes 147464 | tf_op jit(solution)/shard_map/ppermute | solution.py:367
  22.4 0.0 collective-permute-done.2.three
  22.4 1.4 %collective-permute-done.1.two = f32[96,128]{1,0:T(8,128)S(1)} collective-permute-done((f32[96,128]{1,0:T(8,128)}, f32[96,128]{1,0:T(8,128)S(1)}, u32[]{:S(2)}, u32[]{:S(2)}) %collective-permute-start.1) | collective-permute-done | bytes 49184 | tf_op jit(solution)/shard_map/ppermute | solution.py:367
  23.7 0.0 collective-permute-done.one
  23.8 0.8 %add_multiply_fusion.after.mine.half = f32[96,128]{1,0:T(8,128)S(1)} fusion(f32[96,128]{1,0:T(8,128)S(1)} %collective-permute-done.1.two, f32[96,128]{1,0:T(8,128)S(1)} %collective-permute-done.2.three, f32[96,128]{1,0:T(8,128)} %get-tuple-element.12.mine, f32[96,128]{1,0:T(8,128)S(1)} %collective-permute-done.one), kind=kLoop, calls=%fused_computation | loop fusion | flops 49152 | bytes 245760 | tf_op jit(solution)/shard_map/mul | solution.py:419
  24.6 1.2 %all-to-all-done = f32[32,14,1,128]{3,2,1,0:T(1,128)S(1)} async-done(((f32[32,14,1,128]{3,2,1,0:T(1,128)}), f32[32,14,1,128]{3,2,1,0:T(1,128)S(1)}, u32[]{:S(2)}, u32[]{:S(2)}) %all-to-all-start) | async-done | bytes 229408 | tf_op jit(solution)/shard_map/all_to_all | solution.py:355
  25.8 0.9 %pack.1.after = f32[16,16,128]{2,1,0:T(8,128)} custom-call(f32[448,128]{1,0:T(8,128)S(1)} %bitcast.7, f32[96,128]{1,0:T(8,128)S(1)} %add_multiply_fusion.after.mine.half), custom_call_target="tpu_custom_call" | custom-call | tf_op jit(solution)/shard_map/pack/pallas_call | solution.py:420
  26.6 10.4 %all-to-all-start.1 = ((f32[16,16,128]{2,1,0:T(8,128)}), f32[16,16,128]{2,1,0:T(8,128)S(1)}, u32[]{:S(2)}, u32[]{:S(2)}) async-start(f32[16,16,128]{2,1,0:T(8,128)} %pack.1.after), calls=%async_computation.1 | async-start | bytes 262144 | tf_op jit(solution)/shard_map/all_to_all | solution.py:355
  37.1 4.7 %collective-permute-start.3 = (f32[96,128]{1,0:T(8,128)S(1)}, f32[96,128]{1,0:T(8,128)S(1)}, u32[]{:S(2)}, u32[]{:S(2)}) collective-permute-start(f32[96,128]{1,0:T(8,128)S(1)} %add_multiply_fusion.after.mine.half), channel_id=1, source_target_pairs={{0,128},{32,160},{64,192},{96,224},{128,0},{160,32},{192,64},{224,... | collective-permute-start | bytes 147464 | tf_op jit(solution)/shard_map/ppermute | solution.py:367
  41.8 0.0 copy-done.1
  41.8 3.5 %details.1.after.detail = f32[3,256,512]{2,1,0:T(8,128)S(1)} custom-call(f32[448,128]{1,0:T(8,128)S(1)} %bitcast.8, bf16[3,256,512]{2,1,0:T(8,128)(2,1)S(1)} %bitcast.13, f32[16,16,128]{2,1,0:T(8,128)} %pack.1.after), custom_call_target="tpu_custom_call" | custom-call | flops 1409286144 | bytes 3932160 | tf_op jit(solution)/shard_map/details/pallas_call | solution.py:424
  45.4 0.0 copy-start.2
  45.4 1.2 %plane.1.back_in = f32[416,128]{1,0:T(8,128)S(1)} custom-call(f32[448,128]{1,0:T(8,128)S(1)} %bitcast.9, f32[16,16,128]{2,1,0:T(8,128)} %pack.1.after), custom_call_target="tpu_custom_call" | custom-call | tf_op jit(solution)/shard_map/plane/pallas_call | solution.py:423
  46.6 0.0 copy-start
  46.6 0.0 collective-permute-done.3.other
  46.6 0.0 all-to-all-done.1.gathered
  46.6 1.0 %corner.1 = (f32[416,128]{1,0:T(8,128)}, f32[96,128]{1,0:T(8,128)S(1)}) custom-call(f32[16,16,128]{2,1,0:T(8,128)S(1)} %all-to-all-done.1.gathered, f32[416,128]{1,0:T(8,128)S(1)} %plane.1.back_in, f32[96,128]{1,0:T(8,128)S(1)} %add_multiply_fusion.after.mine.half, f32[96,128]{1,0:T(8,128)S(1)} %collective-permute-done.3.other, ...), custom_call_target="tpu_custom_call" | custom-call | tf_op jit(solution)/shard_map/corner/pallas_call | solution.py:431
  47.6 7.7 %all-to-all-start.2 = ((f32[32,13,1,128]{3,2,1,0:T(1,128)}), f32[32,13,1,128]{3,2,1,0:T(1,128)S(1)}, u32[]{:S(2)}, u32[]{:S(2)}) async-start(f32[32,13,1,128]{3,2,1,0:T(1,128)} %bitcast.3), calls=%async_computation.2 | async-start | bytes 425984 | tf_op jit(solution)/shard_map/all_to_all | solution.py:355
  55.3 5.8 %collective-permute-start.4 = (f32[96,128]{1,0:T(8,128)S(1)}, f32[96,128]{1,0:T(8,128)S(1)}, u32[]{:S(2)}, u32[]{:S(2)}) collective-permute-start(f32[96,128]{1,0:T(8,128)S(1)} %get-tuple-element.14.after.mine), channel_id=1, source_target_pairs={{0,256},{32,288},{64,320},{96,352},{128,384},{160,416},{192,448},{... | collective-permute-start | bytes 147464 | tf_op jit(solution)/shard_map/ppermute | solution.py:367
  61.2 0.0 copy-done.2
  61.2 0.2 line.1
  61.4 3.9 %collective-permute-done.4.other = f32[96,128]{1,0:T(8,128)S(1)} collective-permute-done((f32[96,128]{1,0:T(8,128)S(1)}, f32[96,128]{1,0:T(8,128)S(1)}, u32[]{:S(2)}, u32[]{:S(2)}) %collective-permute-start.4) | collective-permute-done | bytes 49184 | tf_op jit(solution)/shard_map/ppermute | solution.py:367
  65.2 1.8 %all-to-all-done.2 = f32[32,13,1,128]{3,2,1,0:T(1,128)S(1)} async-done(((f32[32,13,1,128]{3,2,1,0:T(1,128)}), f32[32,13,1,128]{3,2,1,0:T(1,128)S(1)}, u32[]{:S(2)}, u32[]{:S(2)}) %all-to-all-start.2) | async-done | bytes 213024 | tf_op jit(solution)/shard_map/all_to_all | solution.py:355
  67.1 0.0 copy-done
  67.1 1.9 %finish.1 = bf16[3,256,512]{2,1,0:T(8,128)(2,1)} custom-call(f32[416,128]{1,0:T(8,128)S(1)} %bitcast.10, f32[96,128]{1,0:T(8,128)S(1)} %get-tuple-element.14.after.mine, f32[96,128]{1,0:T(8,128)S(1)} %collective-permute-done.4.other, f32[96,128]{1,0:T(8,128)S(1)} %get-tuple-element.15.partial, f32[8,512]{1,0:T(8,128)S(1)} %get-tuple-element.16.mask, ...), custom_call_target="tpu_custom_call" | custom-call | tf_op jit(solution)/shard_map/finish/pallas_call | solution.py:445
Async XLA Ops:
  0.0 41.8 %copy-start.1 = (bf16[3,32,8,512]{3,2,1,0:T(8,128)(2,1)S(1)}, bf16[3,32,8,512]{3,2,1,0:T(8,128)(2,1)}, u32[]{:S(2)}) copy-start(bf16[3,32,8,512]{3,2,1,0:T(8,128)(2,1)} %param.4) | copy-start | bytes 2359300
  3.9 21.8 %all-to-all-start = ((f32[32,14,1,128]{3,2,1,0:T(1,128)}), f32[32,14,1,128]{3,2,1,0:T(1,128)S(1)}, u32[]{:S(2)}, u32[]{:S(2)}) async-start(f32[32,14,1,128]{3,2,1,0:T(1,128)} %bitcast.14), calls=%async_computation | async-start | bytes 458752 | tf_op jit(solution)/shard_map/all_to_all | solution.py:355
  14.1 8.2 %collective-permute-start.2 = (f32[96,128]{1,0:T(8,128)}, f32[96,128]{1,0:T(8,128)S(1)}, u32[]{:S(2)}, u32[]{:S(2)}) collective-permute-start(f32[96,128]{1,0:T(8,128)} %get-tuple-element.12.mine), channel_id=1, source_target_pairs={{0,96},{32,64},{64,32},{96,0},{128,224},{160,192},{192,160},{224,1... | collective-permute-start | bytes 147464 | tf_op jit(solution)/shard_map/ppermute | solution.py:367
  17.3 6.5 %collective-permute-start.1 = (f32[96,128]{1,0:T(8,128)}, f32[96,128]{1,0:T(8,128)S(1)}, u32[]{:S(2)}, u32[]{:S(2)}) collective-permute-start(f32[96,128]{1,0:T(8,128)} %get-tuple-element.12.mine), channel_id=1, source_target_pairs={{0,64},{32,96},{64,0},{96,32},{128,192},{160,224},{192,128},{224,1... | collective-permute-start | bytes 147464 | tf_op jit(solution)/shard_map/ppermute | solution.py:367
  20.3 3.4 %collective-permute-start = (f32[96,128]{1,0:T(8,128)}, f32[96,128]{1,0:T(8,128)S(1)}, u32[]{:S(2)}, u32[]{:S(2)}) collective-permute-start(f32[96,128]{1,0:T(8,128)} %get-tuple-element.12.mine), channel_id=1, source_target_pairs={{0,32},{32,0},{64,96},{96,64},{128,160},{160,128},{192,224},{224,1... | collective-permute-start | bytes 147464 | tf_op jit(solution)/shard_map/ppermute | solution.py:367
  26.6 20.0 %all-to-all-start.1 = ((f32[16,16,128]{2,1,0:T(8,128)}), f32[16,16,128]{2,1,0:T(8,128)S(1)}, u32[]{:S(2)}, u32[]{:S(2)}) async-start(f32[16,16,128]{2,1,0:T(8,128)} %pack.1.after), calls=%async_computation.1 | async-start | bytes 262144 | tf_op jit(solution)/shard_map/all_to_all | solution.py:355
  37.1 9.5 %collective-permute-start.3 = (f32[96,128]{1,0:T(8,128)S(1)}, f32[96,128]{1,0:T(8,128)S(1)}, u32[]{:S(2)}, u32[]{:S(2)}) collective-permute-start(f32[96,128]{1,0:T(8,128)S(1)} %add_multiply_fusion.after.mine.half), channel_id=1, source_target_pairs={{0,128},{32,160},{64,192},{96,224},{128,0},{160,32},{192,64},{224,... | collective-permute-start | bytes 147464 | tf_op jit(solution)/shard_map/ppermute | solution.py:367
  45.4 15.8 %copy-start.2 = (f32[96,128]{1,0:T(8,128)S(1)}, f32[96,128]{1,0:T(8,128)}, u32[]{:S(2)}) copy-start(f32[96,128]{1,0:T(8,128)} %get-tuple-element.12.mine) | copy-start | bytes 147460
  46.6 20.5 %copy-start = (bf16[3,32,8,512]{3,2,1,0:T(8,128)(2,1)S(1)}, bf16[3,32,8,512]{3,2,1,0:T(8,128)(2,1)}, u32[]{:S(2)}) copy-start(bf16[3,32,8,512]{3,2,1,0:T(8,128)(2,1)} %param.5) | copy-start | bytes 2359300
  47.6 19.4 %all-to-all-start.2 = ((f32[32,13,1,128]{3,2,1,0:T(1,128)}), f32[32,13,1,128]{3,2,1,0:T(1,128)S(1)}, u32[]{:S(2)}, u32[]{:S(2)}) async-start(f32[32,13,1,128]{3,2,1,0:T(1,128)} %bitcast.3), calls=%async_computation.2 | async-start | bytes 425984 | tf_op jit(solution)/shard_map/all_to_all | solution.py:355
  55.3 9.9 %collective-permute-start.4 = (f32[96,128]{1,0:T(8,128)S(1)}, f32[96,128]{1,0:T(8,128)S(1)}, u32[]{:S(2)}, u32[]{:S(2)}) collective-permute-start(f32[96,128]{1,0:T(8,128)S(1)} %get-tuple-element.14.after.mine), channel_id=1, source_target_pairs={{0,256},{32,288},{64,320},{96,352},{128,384},{160,416},{192,448},{... | collective-permute-start | bytes 147464 | tf_op jit(solution)/shard_map/ppermute | solution.py:367

commit v10 on v8

--- a/solution.py
+++ b/solution.py
@@ -191,9 +191,8 @@
     return forward, inverse
 
 
-def plane_kernel(recv, after, back, corner):
+def plane_kernel(recv, mine, one, two, three, back, corner, half):
     place = own_place()
-    del after
     planes = recv.shape[0] // ROWS
     forward, inverse = level_tables(planes)
     extra = recv[pl.ds(EXTRA, planes, stride=ROWS), :]
@@ -213,6 +212,7 @@
     packed = packed + jnp.dot(own, slot, preferred_element_type=F32)
     for g in range(corner.shape[0]):
         corner[g] = packed
+    half[...] = (mine[...] + one[...] + (two[...] + three[...])) * 0.25
     pick = jnp.where(iota((BZ, ZB * BZ), 0) & 3 == iota((BZ, ZB * BZ), 1) >> 7, 1.0, 0.0)
     own = recv[pl.ds(place[1] * ROWS + KEPT, 1), :]
     spread = jnp.where(iota((planes, BZ), 1) >> 2 == iota((planes, BZ), 0), own, 0.0)
@@ -410,13 +410,12 @@
     )(counts, blocks, vort)
     recv = over_yz(send, planes)
     near = [from_partner(line, distance) for distance in (1, 2, 3)]
-    half = (line + near[0] + (near[1] + near[2])) * 0.25
-    back, corner = call(
+    back, corner, half = call(
         plane_kernel,
         "plane",
-        (array(planes * BACK, BZ), array(slabs, PACKED, BZ)),
-        [vmem, loose],
-    )(recv, half)
+        (array(planes * BACK, BZ), array(slabs, PACKED, BZ), array(*line_shape)),
+        [vmem] * 5,
+    )(recv, line, *near)
     gathered = exchange(corner, "gx")
     opposite = from_partner(half, 4)
     detail = call(

time: 69.3 us -> 69.3 us (level)
  starting transfers between devices: 47.9 us -> 47 us
  waiting for transfers between devices: 8.65 us -> 9.48 us
  other arithmetic: 0.81 us -> 0 us
  local copies, waits for them, and re-layouts: 0.01 us -> 0.81 us
    all_to_all x3, starting transfers between devices: 28.3 us -> 27.5 us  [exchange(): return lax.all_to_all(value, axis, split_axis=0, concat_axis=0, tiled=True)]
    all_to_all x3, waiting for transfers between devices: 3.93 us -> 4.75 us  [exchange(): return lax.all_to_all(value, axis, split_axis=0, concat_axis=0, tiled=True)]
    mul x1 -> x0, other arithmetic: 0.81 us -> none  [body(): half = (line + near[0] + (near[1] + near[2])) * 0.25]
    unnamed x6 -> x8, local copies, waits for them, and re-layouts: 0.01 us -> 0.81 us
  transfers between devices with their start and end apart: 8 -> 8, of which waited for: 6 -> 6; matrix products, arithmetic and copies ran while one was open for 1% -> 0% of each run, Pallas kernels for 5% -> 5%
where the time goes in v10:
time: 69.3 us; the launch traced here: 68.8 us
  starting transfers between devices  47 us (68%)
  Pallas kernels  10.6 us (15%)
  waiting for transfers between devices  9.48 us (14%)
  between operations  0.85 us (1%)
  local copies, waits for them, and re-layouts  0.81 us (1%)
    all_to_all x3, starting transfers between devices, exchange(): return lax.all_to_all(value, axis, split_axis=0, concat_axis=0, tiled=True)  27.5 us
    ppermute x5, starting transfers between devices, from_partner(): return lax.ppermute(value, 'gx', pairs)  19.6 us
    all_to_all x3, waiting for transfers between devices, exchange(): return lax.all_to_all(value, axis, split_axis=0, concat_axis=0, tiled=True)  4.75 us
    ppermute x5, waiting for transfers between devices, from_partner(): return lax.ppermute(value, 'gx', pairs)  4.73 us
    pallas_call x1, Pallas kernels, body(): call(details_kernel, 'details', array(parts, cells, wide), [vmem, vmem, l...  3.54 us
    pallas_call x1, Pallas kernels, body(): call(head_kernel, 'head', (array(planes * ROWS, BZ), array(*line_shape)),...  3.21 us
    pallas_call x1, Pallas kernels, body(): call(finish_kernel, 'finish', jax.ShapeDtypeStruct((parts, cells, wide),...  1.75 us
  transfers between devices with their start and end apart: 8, of which 6 were waited for; matrix products, arithmetic and copies ran while one was open for 0% of the time, Pallas kernels for 5%

profile of v10, /device:TPU:8, one launch (start us, length us, event | category | flops | bytes accessed | tf_op | source)
XLA Modules:
  0.0 68.8 jit_solution(9758452748203908177)
XLA Ops:
  0.0 0.0 copy-start.1
  0.7 3.2 %head.1 = (f32[448,128]{1,0:T(8,128)}, f32[96,128]{1,0:T(8,128)}) custom-call(s32[1]{0:T(128)S(6)} %copy.7.counts_hbm, s32[1,128]{1,0:T(1,128)} %blocks_hbm.1, bf16[3,256,512]{2,1,0:T(8,128)(2,1)} %bitcast.11), custom_call_target="tpu_custom_call" | custom-call | tf_op jit(solution)/shard_map/head/pallas_call | solution.py:398
  3.9 10.2 %all-to-all-start = ((f32[32,14,1,128]{3,2,1,0:T(1,128)}), f32[32,14,1,128]{3,2,1,0:T(1,128)S(1)}, u32[]{:S(2)}, u32[]{:S(2)}) async-start(f32[32,14,1,128]{3,2,1,0:T(1,128)} %bitcast.13), calls=%async_computation | async-start | bytes 458752 | tf_op jit(solution)/shard_map/all_to_all | solution.py:349
  14.1 3.2 %collective-permute-start.2 = (f32[96,128]{1,0:T(8,128)}, f32[96,128]{1,0:T(8,128)S(1)}, u32[]{:S(2)}, u32[]{:S(2)}) collective-permute-start(f32[96,128]{1,0:T(8,128)} %get-tuple-element.15.mine), channel_id=1, source_target_pairs={{0,96},{32,64},{64,32},{96,0},{128,224},{160,192},{192,160},{224,1... | collective-permute-start | bytes 147464 | tf_op jit(solution)/shard_map/ppermute | solution.py:361
  17.3 3.0 %collective-permute-start.1 = (f32[96,128]{1,0:T(8,128)}, f32[96,128]{1,0:T(8,128)S(1)}, u32[]{:S(2)}, u32[]{:S(2)}) collective-permute-start(f32[96,128]{1,0:T(8,128)} %get-tuple-element.15.mine), channel_id=1, source_target_pairs={{0,64},{32,96},{64,0},{96,32},{128,192},{160,224},{192,128},{224,1... | collective-permute-start | bytes 147464 | tf_op jit(solution)/shard_map/ppermute | solution.py:361
  20.3 2.0 %collective-permute-start = (f32[96,128]{1,0:T(8,128)}, f32[96,128]{1,0:T(8,128)S(1)}, u32[]{:S(2)}, u32[]{:S(2)}) collective-permute-start(f32[96,128]{1,0:T(8,128)} %get-tuple-element.15.mine), channel_id=1, source_target_pairs={{0,32},{32,0},{64,96},{96,64},{128,160},{160,128},{192,224},{224,1... | collective-permute-start | bytes 147464 | tf_op jit(solution)/shard_map/ppermute | solution.py:361
  22.4 0.0 collective-permute-done.2.three
  22.4 1.4 %collective-permute-done.1.two = f32[96,128]{1,0:T(8,128)S(1)} collective-permute-done((f32[96,128]{1,0:T(8,128)}, f32[96,128]{1,0:T(8,128)S(1)}, u32[]{:S(2)}, u32[]{:S(2)}) %collective-permute-start.1) | collective-permute-done | bytes 49184 | tf_op jit(solution)/shard_map/ppermute | solution.py:361
  23.7 0.0 collective-permute-done.one
  23.8 2.0 %all-to-all-done = f32[32,14,1,128]{3,2,1,0:T(1,128)S(1)} async-done(((f32[32,14,1,128]{3,2,1,0:T(1,128)}), f32[32,14,1,128]{3,2,1,0:T(1,128)S(1)}, u32[]{:S(2)}, u32[]{:S(2)}) %all-to-all-start) | async-done | bytes 229408 | tf_op jit(solution)/shard_map/all_to_all | solution.py:349
  25.8 0.0 copy-start.2
  25.8 0.8 %copy-done.2 = f32[96,128]{1,0:T(8,128)S(1)} copy-done((f32[96,128]{1,0:T(8,128)S(1)}, f32[96,128]{1,0:T(8,128)}, u32[]{:S(2)}) %copy-start.2) | copy-done | bytes 49176
  26.6 0.9 %plane.1 = (f32[416,128]{1,0:T(8,128)S(1)}, f32[16,16,128]{2,1,0:T(8,128)}, f32[96,128]{1,0:T(8,128)S(1)}) custom-call(f32[448,128]{1,0:T(8,128)S(1)} %bitcast.7, f32[96,128]{1,0:T(8,128)S(1)} %copy-done.2, f32[96,128]{1,0:T(8,128)S(1)} %collective-permute-done.one, f32[96,128]{1,0:T(8,128)S(1)} %collective-permute-done.1.two, ...), custom_call_target="tpu_custom_call" | custom-call | tf_op jit(solution)/shard_map/plane/pallas_call | solution.py:413
  27.5 10.4 %all-to-all-start.1 = ((f32[16,16,128]{2,1,0:T(8,128)}), f32[16,16,128]{2,1,0:T(8,128)S(1)}, u32[]{:S(2)}, u32[]{:S(2)}) async-start(f32[16,16,128]{2,1,0:T(8,128)} %get-tuple-element.16.after), calls=%async_computation.1 | async-start | bytes 262144 | tf_op jit(solution)/shard_map/all_to_all | solution.py:349
  37.9 4.7 %collective-permute-start.3 = (f32[96,128]{1,0:T(8,128)S(1)}, f32[96,128]{1,0:T(8,128)S(1)}, u32[]{:S(2)}, u32[]{:S(2)}) collective-permute-start(f32[96,128]{1,0:T(8,128)S(1)} %get-tuple-element.18.mine.half), channel_id=1, source_target_pairs={{0,128},{32,160},{64,192},{96,224},{128,0},{160,32},{192,64},{224,... | collective-permute-start | bytes 147464 | tf_op jit(solution)/shard_map/ppermute | solution.py:361
  42.6 0.0 copy-done.1
  42.6 3.5 %details.1.after.detail = f32[3,256,512]{2,1,0:T(8,128)S(1)} custom-call(f32[448,128]{1,0:T(8,128)S(1)} %bitcast.8, bf16[3,256,512]{2,1,0:T(8,128)(2,1)S(1)} %bitcast.12, f32[16,16,128]{2,1,0:T(8,128)} %get-tuple-element.16.after), custom_call_target="tpu_custom_call" | custom-call | flops 1409286144 | bytes 3932160 | tf_op jit(solution)/shard_map/details/pallas_call | solution.py:421
  46.2 0.0 copy-start.3
  46.2 0.0 copy-start
  46.2 0.3 collective-permute-done.3.other
  46.4 0.2 all-to-all-done.1.gathered
  46.6 1.0 %corner.1 = (f32[416,128]{1,0:T(8,128)}, f32[96,128]{1,0:T(8,128)S(1)}) custom-call(f32[16,16,128]{2,1,0:T(8,128)S(1)} %all-to-all-done.1.gathered, f32[416,128]{1,0:T(8,128)S(1)} %get-tuple-element.17.back_in, f32[96,128]{1,0:T(8,128)S(1)} %get-tuple-element.18.mine.half, f32[96,128]{1,0:T(8,128)S(1)} %collective-permute-done.3.other, ...), custom_call_target="tpu_custom_call" | custom-call | tf_op jit(solution)/shard_map/corner/pallas_call | solution.py:428
  47.7 6.9 %all-to-all-start.2 = ((f32[32,13,1,128]{3,2,1,0:T(1,128)}), f32[32,13,1,128]{3,2,1,0:T(1,128)S(1)}, u32[]{:S(2)}, u32[]{:S(2)}) async-start(f32[32,13,1,128]{3,2,1,0:T(1,128)} %bitcast.3), calls=%async_computation.2 | async-start | bytes 425984 | tf_op jit(solution)/shard_map/all_to_all | solution.py:349
  54.5 6.6 %collective-permute-start.4 = (f32[96,128]{1,0:T(8,128)S(1)}, f32[96,128]{1,0:T(8,128)S(1)}, u32[]{:S(2)}, u32[]{:S(2)}) collective-permute-start(f32[96,128]{1,0:T(8,128)S(1)} %get-tuple-element.20.after.mine), channel_id=1, source_target_pairs={{0,256},{32,288},{64,320},{96,352},{128,384},{160,416},{192,448},{... | collective-permute-start | bytes 147464 | tf_op jit(solution)/shard_map/ppermute | solution.py:361
  61.2 0.0 copy-done.3
  61.2 0.2 line.1
  61.3 3.1 %collective-permute-done.4.other = f32[96,128]{1,0:T(8,128)S(1)} collective-permute-done((f32[96,128]{1,0:T(8,128)S(1)}, f32[96,128]{1,0:T(8,128)S(1)}, u32[]{:S(2)}, u32[]{:S(2)}) %collective-permute-start.4) | collective-permute-done | bytes 49184 | tf_op jit(solution)/shard_map/ppermute | solution.py:361
  64.5 2.6 %all-to-all-done.2 = f32[32,13,1,128]{3,2,1,0:T(1,128)S(1)} async-done(((f32[32,13,1,128]{3,2,1,0:T(1,128)}), f32[32,13,1,128]{3,2,1,0:T(1,128)S(1)}, u32[]{:S(2)}, u32[]{:S(2)}) %all-to-all-start.2) | async-done | bytes 213024 | tf_op jit(solution)/shard_map/all_to_all | solution.py:349
  67.0 0.0 copy-done
  67.0 1.8 %finish.1 = bf16[3,256,512]{2,1,0:T(8,128)(2,1)} custom-call(f32[416,128]{1,0:T(8,128)S(1)} %bitcast.9, f32[96,128]{1,0:T(8,128)S(1)} %get-tuple-element.20.after.mine, f32[96,128]{1,0:T(8,128)S(1)} %collective-permute-done.4.other, f32[96,128]{1,0:T(8,128)S(1)} %get-tuple-element.21.partial, f32[8,512]{1,0:T(8,128)S(1)} %get-tuple-element.22.mask, ...), custom_call_target="tpu_custom_call" | custom-call | tf_op jit(solution)/shard_map/finish/pallas_call | solution.py:442
Async XLA Ops:
  0.0 42.6 %copy-start.1 = (bf16[3,32,8,512]{3,2,1,0:T(8,128)(2,1)S(1)}, bf16[3,32,8,512]{3,2,1,0:T(8,128)(2,1)}, u32[]{:S(2)}) copy-start(bf16[3,32,8,512]{3,2,1,0:T(8,128)(2,1)} %param.4) | copy-start | bytes 2359300
  3.9 21.8 %all-to-all-start = ((f32[32,14,1,128]{3,2,1,0:T(1,128)}), f32[32,14,1,128]{3,2,1,0:T(1,128)S(1)}, u32[]{:S(2)}, u32[]{:S(2)}) async-start(f32[32,14,1,128]{3,2,1,0:T(1,128)} %bitcast.13), calls=%async_computation | async-start | bytes 458752 | tf_op jit(solution)/shard_map/all_to_all | solution.py:349
  14.1 8.2 %collective-permute-start.2 = (f32[96,128]{1,0:T(8,128)}, f32[96,128]{1,0:T(8,128)S(1)}, u32[]{:S(2)}, u32[]{:S(2)}) collective-permute-start(f32[96,128]{1,0:T(8,128)} %get-tuple-element.15.mine), channel_id=1, source_target_pairs={{0,96},{32,64},{64,32},{96,0},{128,224},{160,192},{192,160},{224,1... | collective-permute-start | bytes 147464 | tf_op jit(solution)/shard_map/ppermute | solution.py:361
  17.3 6.5 %collective-permute-start.1 = (f32[96,128]{1,0:T(8,128)}, f32[96,128]{1,0:T(8,128)S(1)}, u32[]{:S(2)}, u32[]{:S(2)}) collective-permute-start(f32[96,128]{1,0:T(8,128)} %get-tuple-element.15.mine), channel_id=1, source_target_pairs={{0,64},{32,96},{64,0},{96,32},{128,192},{160,224},{192,128},{224,1... | collective-permute-start | bytes 147464 | tf_op jit(solution)/shard_map/ppermute | solution.py:361
  20.3 3.4 %collective-permute-start = (f32[96,128]{1,0:T(8,128)}, f32[96,128]{1,0:T(8,128)S(1)}, u32[]{:S(2)}, u32[]{:S(2)}) collective-permute-start(f32[96,128]{1,0:T(8,128)} %get-tuple-element.15.mine), channel_id=1, source_target_pairs={{0,32},{32,0},{64,96},{96,64},{128,160},{160,128},{192,224},{224,1... | collective-permute-start | bytes 147464 | tf_op jit(solution)/shard_map/ppermute | solution.py:361
  25.8 0.8 %copy-start.2 = (f32[96,128]{1,0:T(8,128)S(1)}, f32[96,128]{1,0:T(8,128)}, u32[]{:S(2)}) copy-start(f32[96,128]{1,0:T(8,128)} %get-tuple-element.15.mine) | copy-start | bytes 147460
  27.5 19.2 %all-to-all-start.1 = ((f32[16,16,128]{2,1,0:T(8,128)}), f32[16,16,128]{2,1,0:T(8,128)S(1)}, u32[]{:S(2)}, u32[]{:S(2)}) async-start(f32[16,16,128]{2,1,0:T(8,128)} %get-tuple-element.16.after), calls=%async_computation.1 | async-start | bytes 262144 | tf_op jit(solution)/shard_map/all_to_all | solution.py:349
  37.9 8.6 %collective-permute-start.3 = (f32[96,128]{1,0:T(8,128)S(1)}, f32[96,128]{1,0:T(8,128)S(1)}, u32[]{:S(2)}, u32[]{:S(2)}) collective-permute-start(f32[96,128]{1,0:T(8,128)S(1)} %get-tuple-element.18.mine.half), channel_id=1, source_target_pairs={{0,128},{32,160},{64,192},{96,224},{128,0},{160,32},{192,64},{224,... | collective-permute-start | bytes 147464 | tf_op jit(solution)/shard_map/ppermute | solution.py:361
  46.2 15.0 %copy-start.3 = (f32[96,128]{1,0:T(8,128)S(1)}, f32[96,128]{1,0:T(8,128)}, u32[]{:S(2)}) copy-start(f32[96,128]{1,0:T(8,128)} %get-tuple-element.15.mine) | copy-start | bytes 147460
  46.2 20.8 %copy-start = (bf16[3,32,8,512]{3,2,1,0:T(8,128)(2,1)S(1)}, bf16[3,32,8,512]{3,2,1,0:T(8,128)(2,1)}, u32[]{:S(2)}) copy-start(bf16[3,32,8,512]{3,2,1,0:T(8,128)(2,1)} %param.5) | copy-start | bytes 2359300
  47.7 19.3 %all-to-all-start.2 = ((f32[32,13,1,128]{3,2,1,0:T(1,128)}), f32[32,13,1,128]{3,2,1,0:T(1,128)S(1)}, u32[]{:S(2)}, u32[]{:S(2)}) async-start(f32[32,13,1,128]{3,2,1,0:T(1,128)} %bitcast.3), calls=%async_computation.2 | async-start | bytes 425984 | tf_op jit(solution)/shard_map/all_to_all | solution.py:349
  54.5 9.9 %collective-permute-start.4 = (f32[96,128]{1,0:T(8,128)S(1)}, f32[96,128]{1,0:T(8,128)S(1)}, u32[]{:S(2)}, u32[]{:S(2)}) collective-permute-start(f32[96,128]{1,0:T(8,128)S(1)} %get-tuple-element.20.after.mine), channel_id=1, source_target_pairs={{0,256},{32,288},{64,320},{96,352},{128,384},{160,416},{192,448},{... | collective-permute-start | bytes 147464 | tf_op jit(solution)/shard_map/ppermute | solution.py:361

commit v11 on v8

--- a/solution.py
+++ b/solution.py
@@ -73,10 +73,11 @@
 
 
 def right_product(value, table):
-    high, low = halves(value)
-    return jnp.dot(high, table, preferred_element_type=F32) + jnp.dot(
-        low, table, preferred_element_type=F32
-    )
+    rows = value.shape[0]
+    low = value - value.astype(BF16).astype(F32)
+    stacked = jnp.concatenate([value, low], axis=0).astype(BF16)
+    result = jnp.dot(stacked, table, preferred_element_type=F32)
+    return result[0:rows] + result[rows:]
 
 
 def remix(value, table):

time: 69.3 us -> 69.3 us (level)
  no operation moved by 1% of the time
where the time goes in v11:
time: 69.3 us; the launch traced here: 68.7 us
  starting transfers between devices  47.9 us (69%)
  Pallas kernels  10.5 us (15%)
  waiting for transfers between devices  8.68 us (13%)
  between operations  0.85 us (1%)
  other arithmetic  0.81 us (1%)
    all_to_all x3, starting transfers between devices, exchange(): return lax.all_to_all(value, axis, split_axis=0, concat_axis=0, tiled=True)  28.3 us
    ppermute x5, starting transfers between devices, from_partner(): return lax.ppermute(value, 'gx', pairs)  19.6 us
    ppermute x5, waiting for transfers between devices, from_partner(): return lax.ppermute(value, 'gx', pairs)  4.75 us
    all_to_all x3, waiting for transfers between devices, exchange(): return lax.all_to_all(value, axis, split_axis=0, concat_axis=0, tiled=True)  3.93 us
    pallas_call x1, Pallas kernels, body(): call(details_kernel, 'details', array(parts, cells, wide), [vmem, vmem, l...  3.51 us
    pallas_call x1, Pallas kernels, body(): call(head_kernel, 'head', (array(planes * ROWS, BZ), array(*line_shape)),...  3.17 us
    pallas_call x1, Pallas kernels, body(): call(finish_kernel, 'finish', jax.ShapeDtypeStruct((parts, cells, wide),...  1.74 us
  transfers between devices with their start and end apart: 8, of which 6 were waited for; matrix products, arithmetic and copies ran while one was open for 1% of the time, Pallas kernels for 5%

profile of v11, /device:TPU:8, one launch (start us, length us, event | category | flops | bytes accessed | tf_op | source)
XLA Modules:
  0.0 68.7 jit_solution(4746715953089159913)
XLA Ops:
  0.0 0.0 copy-start.1
  0.7 3.2 %head.1 = (f32[448,128]{1,0:T(8,128)}, f32[96,128]{1,0:T(8,128)}) custom-call(s32[1]{0:T(128)S(6)} %copy.7.counts_hbm, s32[1,128]{1,0:T(1,128)} %blocks_hbm.1, bf16[3,256,512]{2,1,0:T(8,128)(2,1)} %bitcast.11), custom_call_target="tpu_custom_call" | custom-call | tf_op jit(solution)/shard_map/head/pallas_call | solution.py:399
  3.9 10.2 %all-to-all-start = ((f32[32,14,1,128]{3,2,1,0:T(1,128)}), f32[32,14,1,128]{3,2,1,0:T(1,128)S(1)}, u32[]{:S(2)}, u32[]{:S(2)}) async-start(f32[32,14,1,128]{3,2,1,0:T(1,128)} %bitcast.13), calls=%async_computation | async-start | bytes 458752 | tf_op jit(solution)/shard_map/all_to_all | solution.py:350
  14.1 3.2 %collective-permute-start.2 = (f32[96,128]{1,0:T(8,128)}, f32[96,128]{1,0:T(8,128)S(1)}, u32[]{:S(2)}, u32[]{:S(2)}) collective-permute-start(f32[96,128]{1,0:T(8,128)} %get-tuple-element.14.mine), channel_id=1, source_target_pairs={{0,96},{32,64},{64,32},{96,0},{128,224},{160,192},{192,160},{224,1... | collective-permute-start | bytes 147464 | tf_op jit(solution)/shard_map/ppermute | solution.py:362
  17.3 3.0 %collective-permute-start.1 = (f32[96,128]{1,0:T(8,128)}, f32[96,128]{1,0:T(8,128)S(1)}, u32[]{:S(2)}, u32[]{:S(2)}) collective-permute-start(f32[96,128]{1,0:T(8,128)} %get-tuple-element.14.mine), channel_id=1, source_target_pairs={{0,64},{32,96},{64,0},{96,32},{128,192},{160,224},{192,128},{224,1... | collective-permute-start | bytes 147464 | tf_op jit(solution)/shard_map/ppermute | solution.py:362
  20.3 2.0 %collective-permute-start = (f32[96,128]{1,0:T(8,128)}, f32[96,128]{1,0:T(8,128)S(1)}, u32[]{:S(2)}, u32[]{:S(2)}) collective-permute-start(f32[96,128]{1,0:T(8,128)} %get-tuple-element.14.mine), channel_id=1, source_target_pairs={{0,32},{32,0},{64,96},{96,64},{128,160},{160,128},{192,224},{224,1... | collective-permute-start | bytes 147464 | tf_op jit(solution)/shard_map/ppermute | solution.py:362
  22.3 0.0 collective-permute-done.2.three
  22.3 1.4 %collective-permute-done.1.two = f32[96,128]{1,0:T(8,128)S(1)} collective-permute-done((f32[96,128]{1,0:T(8,128)}, f32[96,128]{1,0:T(8,128)S(1)}, u32[]{:S(2)}, u32[]{:S(2)}) %collective-permute-start.1) | collective-permute-done | bytes 49184 | tf_op jit(solution)/shard_map/ppermute | solution.py:362
  23.7 0.0 collective-permute-done.one
  23.7 0.8 %add_multiply_fusion.after.mine.half = f32[96,128]{1,0:T(8,128)S(1)} fusion(f32[96,128]{1,0:T(8,128)S(1)} %collective-permute-done.1.two, f32[96,128]{1,0:T(8,128)S(1)} %collective-permute-done.2.three, f32[96,128]{1,0:T(8,128)} %get-tuple-element.14.mine, f32[96,128]{1,0:T(8,128)S(1)} %collective-permute-done.one), kind=kLoop, calls=%fused_computation | loop fusion | flops 49152 | bytes 245760 | tf_op jit(solution)/shard_map/mul | solution.py:414
  24.5 1.2 %all-to-all-done = f32[32,14,1,128]{3,2,1,0:T(1,128)S(1)} async-done(((f32[32,14,1,128]{3,2,1,0:T(1,128)}), f32[32,14,1,128]{3,2,1,0:T(1,128)S(1)}, u32[]{:S(2)}, u32[]{:S(2)}) %all-to-all-start) | async-done | bytes 229408 | tf_op jit(solution)/shard_map/all_to_all | solution.py:350
  25.7 0.9 %plane.1 = (f32[416,128]{1,0:T(8,128)S(1)}, f32[16,16,128]{2,1,0:T(8,128)}) custom-call(f32[448,128]{1,0:T(8,128)S(1)} %bitcast.7, f32[96,128]{1,0:T(8,128)S(1)} %add_multiply_fusion.after.mine.half), custom_call_target="tpu_custom_call" | custom-call | tf_op jit(solution)/shard_map/plane/pallas_call | solution.py:415
  26.6 10.4 %all-to-all-start.1 = ((f32[16,16,128]{2,1,0:T(8,128)}), f32[16,16,128]{2,1,0:T(8,128)S(1)}, u32[]{:S(2)}, u32[]{:S(2)}) async-start(f32[16,16,128]{2,1,0:T(8,128)} %get-tuple-element.15.after), calls=%async_computation.1 | async-start | bytes 262144 | tf_op jit(solution)/shard_map/all_to_all | solution.py:350
  37.0 4.7 %collective-permute-start.3 = (f32[96,128]{1,0:T(8,128)S(1)}, f32[96,128]{1,0:T(8,128)S(1)}, u32[]{:S(2)}, u32[]{:S(2)}) collective-permute-start(f32[96,128]{1,0:T(8,128)S(1)} %add_multiply_fusion.after.mine.half), channel_id=1, source_target_pairs={{0,128},{32,160},{64,192},{96,224},{128,0},{160,32},{192,64},{224,... | collective-permute-start | bytes 147464 | tf_op jit(solution)/shard_map/ppermute | solution.py:362
  41.8 0.0 copy-done.1
  41.8 3.5 %details.1.after.detail = f32[3,256,512]{2,1,0:T(8,128)S(1)} custom-call(f32[448,128]{1,0:T(8,128)S(1)} %bitcast.8, bf16[3,256,512]{2,1,0:T(8,128)(2,1)S(1)} %bitcast.12, f32[16,16,128]{2,1,0:T(8,128)} %get-tuple-element.15.after), custom_call_target="tpu_custom_call" | custom-call | flops 1409286144 | bytes 3932160 | tf_op jit(solution)/shard_map/details/pallas_call | solution.py:423
  45.3 0.0 copy-start.2
  45.3 0.0 copy-start
  45.3 0.3 collective-permute-done.3.other
  45.6 0.2 all-to-all-done.1.gathered
  45.8 1.0 %corner.1 = (f32[416,128]{1,0:T(8,128)}, f32[96,128]{1,0:T(8,128)S(1)}) custom-call(f32[16,16,128]{2,1,0:T(8,128)S(1)} %all-to-all-done.1.gathered, f32[416,128]{1,0:T(8,128)S(1)} %get-tuple-element.16.back_in, f32[96,128]{1,0:T(8,128)S(1)} %add_multiply_fusion.after.mine.half, f32[96,128]{1,0:T(8,128)S(1)} %collective-permute-done.3.other, ...), custom_call_target="tpu_custom_call" | custom-call | tf_op jit(solution)/shard_map/corner/pallas_call | solution.py:430
  46.8 7.7 %all-to-all-start.2 = ((f32[32,13,1,128]{3,2,1,0:T(1,128)}), f32[32,13,1,128]{3,2,1,0:T(1,128)S(1)}, u32[]{:S(2)}, u32[]{:S(2)}) async-start(f32[32,13,1,128]{3,2,1,0:T(1,128)} %bitcast.3), calls=%async_computation.2 | async-start | bytes 425984 | tf_op jit(solution)/shard_map/all_to_all | solution.py:350
  54.5 6.6 %collective-permute-start.4 = (f32[96,128]{1,0:T(8,128)S(1)}, f32[96,128]{1,0:T(8,128)S(1)}, u32[]{:S(2)}, u32[]{:S(2)}) collective-permute-start(f32[96,128]{1,0:T(8,128)S(1)} %get-tuple-element.18.after.mine), channel_id=1, source_target_pairs={{0,256},{32,288},{64,320},{96,352},{128,384},{160,416},{192,448},{... | collective-permute-start | bytes 147464 | tf_op jit(solution)/shard_map/ppermute | solution.py:362
  61.2 0.0 copy-done.2
  61.2 0.2 line.1
  61.3 3.1 %collective-permute-done.4.other = f32[96,128]{1,0:T(8,128)S(1)} collective-permute-done((f32[96,128]{1,0:T(8,128)S(1)}, f32[96,128]{1,0:T(8,128)S(1)}, u32[]{:S(2)}, u32[]{:S(2)}) %collective-permute-start.4) | collective-permute-done | bytes 49184 | tf_op jit(solution)/shard_map/ppermute | solution.py:362
  64.4 2.6 %all-to-all-done.2 = f32[32,13,1,128]{3,2,1,0:T(1,128)S(1)} async-done(((f32[32,13,1,128]{3,2,1,0:T(1,128)}), f32[32,13,1,128]{3,2,1,0:T(1,128)S(1)}, u32[]{:S(2)}, u32[]{:S(2)}) %all-to-all-start.2) | async-done | bytes 213024 | tf_op jit(solution)/shard_map/all_to_all | solution.py:350
  67.0 0.0 copy-done
  67.0 1.7 %finish.1 = bf16[3,256,512]{2,1,0:T(8,128)(2,1)} custom-call(f32[416,128]{1,0:T(8,128)S(1)} %bitcast.9, f32[96,128]{1,0:T(8,128)S(1)} %get-tuple-element.18.after.mine, f32[96,128]{1,0:T(8,128)S(1)} %collective-permute-done.4.other, f32[96,128]{1,0:T(8,128)S(1)} %get-tuple-element.19.partial, f32[8,512]{1,0:T(8,128)S(1)} %get-tuple-element.20.mask, ...), custom_call_target="tpu_custom_call" | custom-call | tf_op jit(solution)/shard_map/finish/pallas_call | solution.py:444
Async XLA Ops:
  0.0 41.8 %copy-start.1 = (bf16[3,32,8,512]{3,2,1,0:T(8,128)(2,1)S(1)}, bf16[3,32,8,512]{3,2,1,0:T(8,128)(2,1)}, u32[]{:S(2)}) copy-start(bf16[3,32,8,512]{3,2,1,0:T(8,128)(2,1)} %param.4) | copy-start | bytes 2359300
  3.9 21.8 %all-to-all-start = ((f32[32,14,1,128]{3,2,1,0:T(1,128)}), f32[32,14,1,128]{3,2,1,0:T(1,128)S(1)}, u32[]{:S(2)}, u32[]{:S(2)}) async-start(f32[32,14,1,128]{3,2,1,0:T(1,128)} %bitcast.13), calls=%async_computation | async-start | bytes 458752 | tf_op jit(solution)/shard_map/all_to_all | solution.py:350
  14.1 8.2 %collective-permute-start.2 = (f32[96,128]{1,0:T(8,128)}, f32[96,128]{1,0:T(8,128)S(1)}, u32[]{:S(2)}, u32[]{:S(2)}) collective-permute-start(f32[96,128]{1,0:T(8,128)} %get-tuple-element.14.mine), channel_id=1, source_target_pairs={{0,96},{32,64},{64,32},{96,0},{128,224},{160,192},{192,160},{224,1... | collective-permute-start | bytes 147464 | tf_op jit(solution)/shard_map/ppermute | solution.py:362
  17.3 6.5 %collective-permute-start.1 = (f32[96,128]{1,0:T(8,128)}, f32[96,128]{1,0:T(8,128)S(1)}, u32[]{:S(2)}, u32[]{:S(2)}) collective-permute-start(f32[96,128]{1,0:T(8,128)} %get-tuple-element.14.mine), channel_id=1, source_target_pairs={{0,64},{32,96},{64,0},{96,32},{128,192},{160,224},{192,128},{224,1... | collective-permute-start | bytes 147464 | tf_op jit(solution)/shard_map/ppermute | solution.py:362
  20.3 3.4 %collective-permute-start = (f32[96,128]{1,0:T(8,128)}, f32[96,128]{1,0:T(8,128)S(1)}, u32[]{:S(2)}, u32[]{:S(2)}) collective-permute-start(f32[96,128]{1,0:T(8,128)} %get-tuple-element.14.mine), channel_id=1, source_target_pairs={{0,32},{32,0},{64,96},{96,64},{128,160},{160,128},{192,224},{224,1... | collective-permute-start | bytes 147464 | tf_op jit(solution)/shard_map/ppermute | solution.py:362
  26.6 19.2 %all-to-all-start.1 = ((f32[16,16,128]{2,1,0:T(8,128)}), f32[16,16,128]{2,1,0:T(8,128)S(1)}, u32[]{:S(2)}, u32[]{:S(2)}) async-start(f32[16,16,128]{2,1,0:T(8,128)} %get-tuple-element.15.after), calls=%async_computation.1 | async-start | bytes 262144 | tf_op jit(solution)/shard_map/all_to_all | solution.py:350
  37.0 8.6 %collective-permute-start.3 = (f32[96,128]{1,0:T(8,128)S(1)}, f32[96,128]{1,0:T(8,128)S(1)}, u32[]{:S(2)}, u32[]{:S(2)}) collective-permute-start(f32[96,128]{1,0:T(8,128)S(1)} %add_multiply_fusion.after.mine.half), channel_id=1, source_target_pairs={{0,128},{32,160},{64,192},{96,224},{128,0},{160,32},{192,64},{224,... | collective-permute-start | bytes 147464 | tf_op jit(solution)/shard_map/ppermute | solution.py:362
  45.3 15.9 %copy-start.2 = (f32[96,128]{1,0:T(8,128)S(1)}, f32[96,128]{1,0:T(8,128)}, u32[]{:S(2)}) copy-start(f32[96,128]{1,0:T(8,128)} %get-tuple-element.14.mine) | copy-start | bytes 147460
  45.3 21.7 %copy-start = (bf16[3,32,8,512]{3,2,1,0:T(8,128)(2,1)S(1)}, bf16[3,32,8,512]{3,2,1,0:T(8,128)(2,1)}, u32[]{:S(2)}) copy-start(bf16[3,32,8,512]{3,2,1,0:T(8,128)(2,1)} %param.5) | copy-start | bytes 2359300
  46.8 20.2 %all-to-all-start.2 = ((f32[32,13,1,128]{3,2,1,0:T(1,128)}), f32[32,13,1,128]{3,2,1,0:T(1,128)S(1)}, u32[]{:S(2)}, u32[]{:S(2)}) async-start(f32[32,13,1,128]{3,2,1,0:T(1,128)} %bitcast.3), calls=%async_computation.2 | async-start | bytes 425984 | tf_op jit(solution)/shard_map/all_to_all | solution.py:350
  54.5 9.9 %collective-permute-start.4 = (f32[96,128]{1,0:T(8,128)S(1)}, f32[96,128]{1,0:T(8,128)S(1)}, u32[]{:S(2)}, u32[]{:S(2)}) collective-permute-start(f32[96,128]{1,0:T(8,128)S(1)} %get-tuple-element.18.after.mine), channel_id=1, source_target_pairs={{0,256},{32,288},{64,320},{96,352},{128,384},{160,416},{192,448},{... | collective-permute-start | bytes 147464 | tf_op jit(solution)/shard_map/ppermute | solution.py:362
